TPU v7x, 128 devices: a whole 4x4x4 slice. The times are simulated.
128 devices in a mesh: dom: 128 (over y, x, z, core).
Axes of the slice: x: 4, y: 4, z: 4, core: 2. Of those that a mesh axis runs over, the one named last changes fastest.
Arguments:
- vectors: bfloat16 [64, 524288], P(None, 'dom')
- diag_tiles: bfloat16 [4096, 128, 128], P('dom'), as said below
- pair_tiles: bfloat16 [12288, 2, 128, 128], P('dom'), as said below
- halo_tiles: bfloat16 [16384, 128, 128], P('dom'), as said below
- halo_rows: int32 [128, 128], P('dom'), may hold values from 1 to 31, as said below
- pair_index: int32 [128, 96, 2], P('dom'), may hold values from 0 to 31, as said below
- pair_count: int32 [128], P('dom'), may hold values from 24 to 96, as said below
Outputs:
- basis: bfloat16 [64, 524288], P(None, 'dom')
- ritz: float32 [64, 64], replicated
Inputs may be any that keep to these rules, and one draw needn't show every extreme that they name: `diag_tiles`: each tile is symmetric. `pair_tiles`: entry [j, 1] is the transpose of entry [j, 0]. `halo_tiles`: entry d * 128 + p is the transpose of entry p * 128 + d. `halo_rows`: no entry is a multiple of 4. `pair_index`: the 96 entries of a partition are distinct pairs (r, c) with r < c. The first pair_count[d] entries of pair_index[d] are live; some partition has 96.
All inputs are finite; a program needn't handle non-finite values.
Results may differ from a plain program's by a relative error of at most 0.023.
Values may be sent and summed in bfloat16 or wider, within the bound.
No kernel may reach another device: no remote copies, remote signals or barrier semaphores. Data moves between devices by JAX's collectives and lax.ppermute only.
A program may use at most 128 MiB of HBM per device.

v0:
```python
import jax
import jax.numpy as jnp
from jax import lax
from jax.sharding import PartitionSpec as P

DEGREE = 4


first_centre = -0.5


def local(vectors, diag_tiles, pair_tiles, halo_tiles, halo_rows, pair_index, pair_count):
    vec_width = vectors.shape[0]
    tile_size = diag_tiles.shape[1]
    blocks = diag_tiles.shape[0]
    peers = lax.axis_size("dom")
    total_rows = tile_size * blocks * peers
    block_iota = jnp.arange(blocks)
    row_ids = pair_index[0, :, 0]
    col_ids = pair_index[0, :, 1]
    live_mask = (jnp.arange(pair_index.shape[1]) < pair_count[0]).astype(jnp.float32)
    onehot_first = (row_ids[:, None] == block_iota[None, :]).astype(jnp.float32) * live_mask[
        :, None
    ]
    onehot_second = (col_ids[:, None] == block_iota[None, :]).astype(jnp.float32) * live_mask[
        :, None
    ]
    send_rows = halo_rows[0]
    onehot_halo = (send_rows[:, None] == block_iota[None, :]).astype(jnp.float32)

    def halo_terms(arrived):
        products = jnp.einsum(
            "kpj,pij->kpi", arrived, halo_tiles, preferred_element_type=jnp.float32
        )
        return jnp.einsum("kpi,pr->kri", products, onehot_halo)

    def operator(current):
        blocked = current.reshape(vec_width, blocks, tile_size)
        outgoing = jnp.take(blocked, send_rows, axis=1)
        result = halo_terms(
            lax.all_to_all(outgoing, "dom", split_axis=1, concat_axis=1, tiled=True)
        )
        result = result + jnp.einsum(
            "krj,rij->kri", blocked, diag_tiles, preferred_element_type=jnp.float32
        )
        from_cols = jnp.take(blocked, col_ids, axis=1)
        from_rows = jnp.take(blocked, row_ids, axis=1)
        upper_terms = jnp.einsum(
            "kej,eij->kei", from_cols, pair_tiles[:, 0], preferred_element_type=jnp.float32
        )
        lower_terms = jnp.einsum(
            "kej,eij->kei", from_rows, pair_tiles[:, 1], preferred_element_type=jnp.float32
        )
        result = result + jnp.einsum("kei,er->kri", upper_terms, onehot_first)
        result = result + jnp.einsum("kei,er->kri", lower_terms, onehot_second)
        return result.reshape(vec_width, blocks * tile_size)

    def subspace_step(start, first, centre):
        previous = start
        current = (first - centre * start.astype(jnp.float32)).astype(jnp.bfloat16)
        for degree in range(DEGREE - 1):
            applied = operator(current)
            following = (
                2.0 * (applied - centre * current.astype(jnp.float32))
                - previous.astype(jnp.float32)
            ).astype(jnp.bfloat16)
            previous, current = (current, following)
        partial_value = jnp.dot(current, current.T, preferred_element_type=jnp.float32) / total_rows
        gram_matrix = lax.psum(partial_value, "dom")
        chol_lower = jnp.linalg.cholesky(gram_matrix)
        inverse = jax.scipy.linalg.solve_triangular(
            chol_lower, jnp.eye(vec_width, dtype=jnp.float32), lower=True
        )
        following = jnp.dot(
            inverse, current.astype(jnp.float32), precision=lax.Precision.HIGHEST
        ).astype(jnp.bfloat16)
        applied = operator(following)
        projected = (
            jnp.dot(following.astype(jnp.float32), applied.T, precision=lax.Precision.HIGHEST)
            / total_rows
        )
        return (following, applied, projected)

    first = operator(vectors)
    basis_one, image_one, partial_one = subspace_step(vectors, first, first_centre)
    mean_ritz = jnp.trace(lax.psum(partial_one, "dom")) / vec_width
    basis, image_two, partial_two = subspace_step(basis_one, image_one, mean_ritz - 1.0)
    ritz = lax.psum(partial_two, "dom")
    return (basis, ritz)


def solution(mesh):
    return jax.shard_map(
        local,
        mesh=mesh,
        in_specs=(
            P(None, "dom"),
            P("dom", None, None),
            P("dom", None, None, None),
            P("dom", None, None),
            P("dom", None),
            P("dom", None, None),
            P("dom"),
        ),
        out_specs=(P(None, "dom"), P()),
        check_vma=False,
    )
```

profile of v0, /device:TPU:0, one launch (start us, length us, event | category | flops | bytes accessed | tf_op | source)
XLA Modules:
  0.0 754.9 jit_solution(12341436978885757109)
XLA Ops:
  8.6 11.7 %all-to-all-start = ((bf16[64,128,128]{2,0,1:T(8,128)(2,1)}), bf16[64,128,128]{2,0,1:T(8,128)(2,1)}, u32[]{:S(2)}, u32[]{:S(2)}) async-start(bf16[64,128,128]{2,0,1:T(8,128)(2,1)} %select_bitcast_fusion.8), calls=%async_computation | async-start | bytes 4194304 | tf_op jit(solution)/shard_map/all_to_all | solution.py:41
  26.8 4.1 fusion.117
  32.4 5.3 fusion.90
  37.7 12.6 %all-to-all-done = bf16[64,128,128]{2,0,1:T(8,128)(2,1)} async-done(((bf16[64,128,128]{2,0,1:T(8,128)(2,1)}), bf16[64,128,128]{2,0,1:T(8,128)(2,1)}, u32[]{:S(2)}, u32[]{:S(2)}) %all-to-all-start) | async-done | bytes 2097184 | tf_op jit(solution)/shard_map/all_to_all | solution.py:41
  50.3 5.9 convolution_bitcast_fusion.8
  65.3 6.0 all-to-all-start.1
  82.7 5.3 fusion.93
  88.0 13.3 %all-to-all-done.1 = bf16[64,128,128]{2,0,1:T(8,128)(2,1)} async-done(((bf16[64,128,128]{2,0,1:T(8,128)(2,1)}), bf16[64,128,128]{2,0,1:T(8,128)(2,1)}, u32[]{:S(2)}, u32[]{:S(2)}) %all-to-all-start.1) | async-done | bytes 2097184 | tf_op jit(solution)/shard_map/all_to_all | solution.py:41
  101.3 5.9 convolution_bitcast_fusion.7
  116.5 6.2 all-to-all-start.2
  134.7 5.3 fusion.96
  140.1 12.6 %all-to-all-done.2 = bf16[64,128,128]{2,0,1:T(8,128)(2,1)} async-done(((bf16[64,128,128]{2,0,1:T(8,128)(2,1)}), bf16[64,128,128]{2,0,1:T(8,128)(2,1)}, u32[]{:S(2)}, u32[]{:S(2)}) %all-to-all-start.2) | async-done | bytes 2097184 | tf_op jit(solution)/shard_map/all_to_all | solution.py:41
  152.7 5.9 convolution_bitcast_fusion.6
  168.6 6.0 all-to-all-start.3
  178.5 4.6 fusion.126
  187.1 5.3 fusion.99
  192.4 12.2 %all-to-all-done.3 = bf16[64,128,128]{2,0,1:T(8,128)(2,1)} async-done(((bf16[64,128,128]{2,0,1:T(8,128)(2,1)}), bf16[64,128,128]{2,0,1:T(8,128)(2,1)}, u32[]{:S(2)}, u32[]{:S(2)}) %all-to-all-start.3) | async-done | bytes 2097184 | tf_op jit(solution)/shard_map/all_to_all | solution.py:41
  204.6 5.9 convolution_bitcast_fusion.5
  215.8 62.8 %psum.28 = f32[64,64]{0,1:T(8,128)S(1)} all-reduce(f32[64,64]{0,1:T(8,128)S(1)} %convolution_multiply_fusion.3), channel_id=1, replica_groups=mesh['dom'=128] {'dom'}, use_global_device_ids=true, to_apply=%region_0.3 | all-reduce | flops 4096 | bytes 32768 | tf_op jit(solution)/shard_map/psum | solution.py:69
  278.7 5.8 cholesky.44
  285.9 4.9 custom-call.6
  297.0 6.2 all-to-all-start.4
  314.8 5.3 fusion.102
  320.1 13.1 %all-to-all-done.4 = bf16[64,128,128]{2,0,1:T(8,128)(2,1)} async-done(((bf16[64,128,128]{2,0,1:T(8,128)(2,1)}), bf16[64,128,128]{2,0,1:T(8,128)(2,1)}, u32[]{:S(2)}, u32[]{:S(2)}) %all-to-all-start.4) | async-done | bytes 2097184 | tf_op jit(solution)/shard_map/all_to_all | solution.py:41
  333.3 5.8 convolution_bitcast_fusion.4
  343.2 62.8 %psum.29 = f32[64,64]{0,1:T(8,128)S(1)} all-reduce(f32[64,64]{0,1:T(8,128)S(1)} %convolution_multiply_fusion.2), channel_id=1, replica_groups=mesh['dom'=128] {'dom'}, use_global_device_ids=true, to_apply=%region_3.8 | all-reduce | flops 4096 | bytes 32768 | tf_op jit(solution)/shard_map/psum | solution.py:86
  413.4 6.0 all-to-all-start.5
  425.2 4.1 fusion.132
  430.8 5.3 fusion.105
  436.1 13.3 %all-to-all-done.5 = bf16[64,128,128]{2,0,1:T(8,128)(2,1)} async-done(((bf16[64,128,128]{2,0,1:T(8,128)(2,1)}), bf16[64,128,128]{2,0,1:T(8,128)(2,1)}, u32[]{:S(2)}, u32[]{:S(2)}) %all-to-all-start.5) | async-done | bytes 2097184 | tf_op jit(solution)/shard_map/all_to_all | solution.py:41
  449.4 5.9 convolution_bitcast_fusion.3
  464.6 6.0 all-to-all-start.6
  482.7 5.3 fusion.108
  488.0 12.6 %all-to-all-done.6 = bf16[64,128,128]{2,0,1:T(8,128)(2,1)} async-done(((bf16[64,128,128]{2,0,1:T(8,128)(2,1)}), bf16[64,128,128]{2,0,1:T(8,128)(2,1)}, u32[]{:S(2)}, u32[]{:S(2)}) %all-to-all-start.6) | async-done | bytes 2097184 | tf_op jit(solution)/shard_map/all_to_all | solution.py:41
  500.6 5.9 convolution_bitcast_fusion.2
  516.6 6.2 all-to-all-start.7
  526.7 4.6 fusion.138
  535.3 5.3 fusion.111
  540.6 12.2 %all-to-all-done.7 = bf16[64,128,128]{2,0,1:T(8,128)(2,1)} async-done(((bf16[64,128,128]{2,0,1:T(8,128)(2,1)}), bf16[64,128,128]{2,0,1:T(8,128)(2,1)}, u32[]{:S(2)}, u32[]{:S(2)}) %all-to-all-start.7) | async-done | bytes 2097184 | tf_op jit(solution)/shard_map/all_to_all | solution.py:41
  552.8 5.9 convolution_bitcast_fusion.1
  563.9 63.0 %psum.30 = f32[64,64]{0,1:T(8,128)S(1)} all-reduce(f32[64,64]{0,1:T(8,128)S(1)} %convolution_multiply_fusion.1), channel_id=1, replica_groups=mesh['dom'=128] {'dom'}, use_global_device_ids=true, to_apply=%region_5.10 | all-reduce | flops 4096 | bytes 32768 | tf_op jit(solution)/shard_map/psum | solution.py:69
  627.0 5.8 cholesky.55
  634.2 4.9 custom-call.7
  645.4 5.8 all-to-all-start.8
  662.5 5.3 fusion.114
  667.9 13.3 %all-to-all-done.8 = bf16[64,128,128]{2,0,1:T(8,128)(2,1)} async-done(((bf16[64,128,128]{2,0,1:T(8,128)(2,1)}), bf16[64,128,128]{2,0,1:T(8,128)(2,1)}, u32[]{:S(2)}, u32[]{:S(2)}) %all-to-all-start.8) | async-done | bytes 2097184 | tf_op jit(solution)/shard_map/all_to_all | solution.py:41
  681.2 5.9 convolution_bitcast_fusion
  691.2 62.8 %psum.31 = f32[64,64]{0,1:T(8,128)S(1)} all-reduce(f32[64,64]{0,1:T(8,128)S(1)} %convolution_multiply_fusion), channel_id=1, replica_groups=mesh['dom'=128] {'dom'}, use_global_device_ids=true, to_apply=%region_6.11 | all-reduce | flops 4096 | bytes 32768 | tf_op jit(solution)/shard_map/psum | solution.py:88
  (217 shorter events, 185.6 us)
Async XLA Ops:
  0.6 24.3 %copy-start = (bf16[32,128,128]{2,1,0:T(8,128)(2,1)S(1)}, bf16[32,128,128]{2,1,0:T(8,128)(2,1)}, u32[]{:S(2)}) copy-start(bf16[32,128,128]{2,1,0:T(8,128)(2,1)} %param.15) | copy-start | bytes 3145732
  8.6 11.7 %copy-start.48 = (s32[1,96,2]{1,2,0:T(2,128)S(1)}, s32[1,96,2]{1,2,0:T(2,128)}, u32[]{:S(2)}) copy-start(s32[1,96,2]{1,2,0:T(2,128)} %param.19) | copy-start | bytes 2308
  8.6 41.7 %all-to-all-start = ((bf16[64,128,128]{2,0,1:T(8,128)(2,1)}), bf16[64,128,128]{2,0,1:T(8,128)(2,1)}, u32[]{:S(2)}, u32[]{:S(2)}) async-start(bf16[64,128,128]{2,0,1:T(8,128)(2,1)} %select_bitcast_fusion.8), calls=%async_computation | async-start | bytes 4194304 | tf_op jit(solution)/shard_map/all_to_all | solution.py:41
  22.9 2.0 copy-start.8
  24.9 1.9 copy-start.32
  37.7 18.5 %copy-start.47 = (s32[1,128]{1,0:T(1,128)S(1)}, s32[1,128]{1,0:T(1,128)}, u32[]{:S(2)}) copy-start(s32[1,128]{1,0:T(1,128)} %param.18) | copy-start | bytes 1540
  50.3 5.9 copy-start.16
  65.3 36.0 %all-to-all-start.1 = ((bf16[64,128,128]{2,0,1:T(8,128)(2,1)}), bf16[64,128,128]{2,0,1:T(8,128)(2,1)}, u32[]{:S(2)}, u32[]{:S(2)}) async-start(bf16[64,128,128]{2,0,1:T(8,128)(2,1)} %select_bitcast_fusion.7), calls=%async_computation.1 | async-start | bytes 4194304 | tf_op jit(solution)/shard_map/all_to_all | solution.py:41
  75.2 1.9 copy-start.42
  101.3 5.9 copy-start.17
  107.2 1.8 copy-start.24
  116.5 36.2 %all-to-all-start.2 = ((bf16[64,128,128]{2,0,1:T(8,128)(2,1)}), bf16[64,128,128]{2,0,1:T(8,128)(2,1)}, u32[]{:S(2)}, u32[]{:S(2)}) async-start(bf16[64,128,128]{2,0,1:T(8,128)(2,1)} %select_bitcast_fusion.6), calls=%async_computation.2 | async-start | bytes 4194304 | tf_op jit(solution)/shard_map/all_to_all | solution.py:41
  126.6 1.9 copy-start.43
  132.6 2.1 copy-start.35
  152.7 5.9 copy-start.18
  158.6 1.8 copy-start.11
  158.6 1.8 copy-start.25
  168.6 36.0 %all-to-all-start.3 = ((bf16[64,128,128]{2,0,1:T(8,128)(2,1)}), bf16[64,128,128]{2,0,1:T(8,128)(2,1)}, u32[]{:S(2)}, u32[]{:S(2)}) async-start(bf16[64,128,128]{2,0,1:T(8,128)(2,1)} %select_bitcast_fusion.5), calls=%async_computation.3 | async-start | bytes 4194304 | tf_op jit(solution)/shard_map/all_to_all | solution.py:41
  183.2 2.1 copy-start.5
  185.2 1.9 copy-start.36
  204.6 5.9 copy-start.21
  210.5 1.8 copy-start.9
  210.5 1.8 copy-start.26
  297.0 36.2 %all-to-all-start.4 = ((bf16[64,128,128]{2,0,1:T(8,128)(2,1)}), bf16[64,128,128]{2,0,1:T(8,128)(2,1)}, u32[]{:S(2)}, u32[]{:S(2)}) async-start(bf16[64,128,128]{2,0,1:T(8,128)(2,1)} %select_bitcast_fusion.4), calls=%async_computation.4 | async-start | bytes 4194304 | tf_op jit(solution)/shard_map/all_to_all | solution.py:41
  312.7 2.1 copy-start.37
  339.0 1.8 copy-start.12
  339.1 1.8 copy-start.27
  413.4 36.0 %all-to-all-start.5 = ((bf16[64,128,128]{2,0,1:T(8,128)(2,1)}), bf16[64,128,128]{2,0,1:T(8,128)(2,1)}, u32[]{:S(2)}, u32[]{:S(2)}) async-start(bf16[64,128,128]{2,0,1:T(8,128)(2,1)} %select_bitcast_fusion.3), calls=%async_computation.5 | async-start | bytes 4194304 | tf_op jit(solution)/shard_map/all_to_all | solution.py:41
  423.3 1.9 copy-start.45
  449.4 5.9 copy-start.19
  455.3 1.8 copy-start.28
  464.6 36.0 %all-to-all-start.6 = ((bf16[64,128,128]{2,0,1:T(8,128)(2,1)}), bf16[64,128,128]{2,0,1:T(8,128)(2,1)}, u32[]{:S(2)}, u32[]{:S(2)}) async-start(bf16[64,128,128]{2,0,1:T(8,128)(2,1)} %select_bitcast_fusion.2), calls=%async_computation.6 | async-start | bytes 4194304 | tf_op jit(solution)/shard_map/all_to_all | solution.py:41
  474.5 1.9 copy-start.46
  480.6 2.1 copy-start.39
  500.6 5.9 copy-start.20
  506.5 1.8 copy-start.13
  506.5 1.8 copy-start.29
  516.6 36.3 %all-to-all-start.7 = ((bf16[64,128,128]{2,0,1:T(8,128)(2,1)}), bf16[64,128,128]{2,0,1:T(8,128)(2,1)}, u32[]{:S(2)}, u32[]{:S(2)}) async-start(bf16[64,128,128]{2,0,1:T(8,128)(2,1)} %select_bitcast_fusion.1), calls=%async_computation.7 | async-start | bytes 4194304 | tf_op jit(solution)/shard_map/all_to_all | solution.py:41
  531.3 2.1 copy-start.2
  533.4 1.9 copy-start.40
  552.8 5.9 copy-start.14
  558.7 1.8 copy-start.10
  558.7 1.8 copy-start.30
  639.9 50.1 %copy-start.7 = (bf16[64,4096]{1,0:T(8,128)(2,1)}, bf16[64,4096]{1,0:T(8,128)(2,1)S(1)}, u32[]{:S(2)}) copy-start(bf16[64,4096]{1,0:T(8,128)(2,1)S(1)} %convolution_convert_fusion) | copy-start | bytes 1572868
  645.4 35.8 %all-to-all-start.8 = ((bf16[64,128,128]{2,0,1:T(8,128)(2,1)}), bf16[64,128,128]{2,0,1:T(8,128)(2,1)}, u32[]{:S(2)}, u32[]{:S(2)}) async-start(bf16[64,128,128]{2,0,1:T(8,128)(2,1)} %select_bitcast_fusion), calls=%async_computation.8 | async-start | bytes 4194304 | tf_op jit(solution)/shard_map/all_to_all | solution.py:41
  655.1 1.9 copy-start.41
  681.2 5.9 copy-start.15
  687.1 1.8 copy-start.22
  (10 other events, 13.4 us)
where the time goes:
time: 766 us; the launch traced here: 755 us
  blocking collectives  251 us (33%)
  matrix products  200 us (26%)
  waiting for transfers between devices  115 us (15%)
  other arithmetic  63.2 us (8%)
  local copies, waits for them, and re-layouts  61.7 us (8%)
  starting transfers between devices  59.9 us (8%)
    psum x2, blocking collectives, subspace_step(): gram_matrix = lax.psum(partial_value, 'dom')  126 us
    all_to_all x9, waiting for transfers between devices, operator(): lax.all_to_all(outgoing, 'dom', split_axis=1, concat_axis=1, tiled=True)  115 us
    psum x1, blocking collectives, local(): mean_ritz = jnp.trace(lax.psum(partial_one, 'dom')) / vec_width  62.8 us
    psum x1, blocking collectives, local(): ritz = lax.psum(partial_two, 'dom')  62.8 us
    all_to_all x9, starting transfers between devices, operator(): lax.all_to_all(outgoing, 'dom', split_axis=1, concat_axis=1, tiled=True)  59.9 us
    dot_general x9, matrix products, halo_terms(): jnp.einsum('kpj,pij->kpi', arrived, halo_tiles, preferred_element_type=jn...  52.8 us
    dot_general x9, matrix products, operator(): jnp.einsum('kej,eij->kei', from_cols, pair_tiles[:, 0], preferred_element...  47.8 us
    dot_general x9, matrix products, operator(): jnp.einsum('kej,eij->kei', from_rows, pair_tiles[:, 1], preferred_element...  38.2 us
  transfers between devices with their start and end apart: 9, of which 9 were waited for; matrix products, arithmetic and copies ran while one was open for 20% of the time, Pallas kernels for 0%

commit v1 on v0

v1 whole, which is shorter than its diff:
```python
import functools

import jax
import jax.numpy as jnp
from jax import lax
from jax.experimental import pallas as pl
from jax.experimental.pallas import tpu as pltpu
from jax.sharding import PartitionSpec as P

FIRST_CENTRE = -0.5
F32, BF16 = jnp.float32, jnp.bfloat16
HI = lax.Precision.HIGHEST
VM = pl.BlockSpec(memory_space=pltpu.VMEM)
SM = pl.BlockSpec(memory_space=pltpu.SMEM)
UNROLL = 8


def held(x):
    return pltpu.with_memory_space_constraint(x, pltpu.VMEM)


def call(body, outs, ins, flops, moved, scratch=()):
    return pl.pallas_call(
        body,
        out_shape=[pltpu.VMEM(s, d) for s, d in outs],
        in_specs=[SM if kind == "s" else VM for _, kind in ins],
        out_specs=[VM for _ in outs],
        scratch_shapes=list(scratch),
        cost_estimate=pl.CostEstimate(flops=flops, bytes_accessed=moved, transcendentals=0),
        compiler_params=pltpu.CompilerParams(vmem_limit_bytes=30 << 20),
    )(*[held(x) if kind == "v" else x for x, kind in ins])


def mm(a, b):
    return jnp.dot(a, b, preferred_element_type=F32)


def mm_t(a, b, precision=None):
    return lax.dot_general(a, b, (((1,), (1,)), ((), ())), precision=precision, preferred_element_type=F32)


def spread(rows_ref, blocks_ref, out_ref):
    peers = out_ref.shape[0]

    def step(i, _):
        for u in range(UNROLL):
            p = i * UNROLL + u
            out_ref[p] = blocks_ref[rows_ref[p]]
        return _

    lax.fori_loop(0, peers // UNROLL, step, 0)


def start_kernel(rows_ref, vec_ref, cur_ref, out_ref):
    width = cur_ref.shape[2]
    for r in range(cur_ref.shape[0]):
        cur_ref[r] = vec_ref[:, r * width : (r + 1) * width]
    spread(rows_ref, cur_ref, out_ref)


def tile_kernel(tiles_ref, out_ref):
    def step(i, _):
        for u in range(4):
            out_ref[i * 4 + u] = tiles_ref[i * 4 + u].T
        return _

    lax.fori_loop(0, out_ref.shape[0] // 4, step, 0)


def pair_sums(first_ref, second_ref, count_ref, cur_ref, pair_ref, acc_ref):
    count = count_ref[0]
    group = 4

    def step(i, _):
        parts = []
        for u in range(group):
            e = i * group + u
            live = jnp.where(e < count, 1.0, 0.0).astype(F32)
            r, c = first_ref[e], second_ref[e]
            parts.append((r, mm(cur_ref[c], pair_ref[e, 1]) * live))
            parts.append((c, mm(cur_ref[r], pair_ref[e, 0]) * live))
        for at, value in parts:
            acc_ref[at] += value
        return _

    lax.fori_loop(0, lax.div(count + (group - 1), group), step, 0)


def local_kernel(mode, total, first_ref, second_ref, count_ref, *refs):
    if mode == "second":
        cur_ref, diag_ref, pair_ref, image_ref, prev_ref, trace_ref, acc_ref, y_ref, c_ref = refs
        centre = jnp.sum(trace_ref[...]) / (total * prev_ref.shape[1]) - 1.0
        c_ref[...] = jnp.full(c_ref.shape, centre, F32)
    elif mode == "filter":
        centre_ref, cur_ref, diag_ref, pair_ref, prev_ref, acc_ref = refs
        centre = centre_ref[0, 0]
    else:
        cur_ref, diag_ref, pair_ref, acc_ref = refs
        centre = FIRST_CENTRE

    def own(r, _):
        block = cur_ref[r]
        value = mm(block, diag_ref[r])
        if mode == "start":
            value = value - centre * block.astype(F32)
        if mode == "filter":
            value = value - centre * block.astype(F32) - 0.5 * prev_ref[r].astype(F32)
        if mode == "second":
            image, prev = image_ref[r], prev_ref[r].astype(F32)
            y = (image - centre * prev).astype(BF16)
            y_ref[r] = y
            value = value - centre * (image + y.astype(F32)) - 0.5 * prev
        acc_ref[r] = value
        return _

    lax.fori_loop(0, cur_ref.shape[0], own, 0, unroll=4)
    pair_sums(first_ref, second_ref, count_ref, cur_ref, pair_ref, acc_ref)


def halo_sums(rows_ref, arrived_ref, tiles_ref, acc_ref):
    def step(i, _):
        parts = []
        for u in range(UNROLL):
            p = i * UNROLL + u
            parts.append((rows_ref[p], mm(arrived_ref[p], tiles_ref[p])))
        for at, value in parts:
            acc_ref[at] += value
        return _

    lax.fori_loop(0, arrived_ref.shape[0] // UNROLL, step, 0)


def halo_kernel(mode, rows_ref, arrived_ref, tiles_ref, part_ref, *refs):
    acc_ref = refs[-1]
    acc_ref[...] = part_ref[...]
    halo_sums(rows_ref, arrived_ref, tiles_ref, acc_ref)
    blocks = acc_ref.shape[0]
    if mode == "image":
        inverse_ref, image_ref, cur_ref, out_ref, _ = refs
        for r in range(blocks):
            image = jnp.dot(inverse_ref[...], acc_ref[r], precision=HI, preferred_element_type=F32)
            image_ref[r] = image
            cur_ref[r] = image.astype(BF16)
        spread(rows_ref, cur_ref, out_ref)
    elif mode == "last":
        filtered_ref, sum_ref, _ = refs
        value = jnp.zeros(sum_ref.shape, F32)
        for r in range(blocks):
            value = value + mm_t(filtered_ref[r].astype(F32), acc_ref[r], HI)
        sum_ref[...] = value
    else:
        cur_ref, out_ref, _ = refs
        factor = 1.0 if mode == "start" else 2.0
        cur_ref[...] = (factor * acc_ref[...]).astype(BF16)
        spread(rows_ref, cur_ref, out_ref)


def gram_kernel(total, cur_ref, gram_ref):
    value = jnp.zeros(gram_ref.shape, F32)
    for r in range(cur_ref.shape[0]):
        block = cur_ref[r]
        value = value + mm_t(block, block)
    gram_ref[...] = value / total


def factor_kernel(flat, gram_ref, cur_ref, inverse_ref, next_ref):
    n = gram_ref.shape[0]
    row = lax.broadcasted_iota(jnp.int32, (n, n), 0)
    col = lax.broadcasted_iota(jnp.int32, (n, n), 1)
    work = jnp.concatenate([gram_ref[...], jnp.where(row == col, 1.0, 0.0).astype(F32)], axis=1)
    at = lax.broadcasted_iota(jnp.int32, (n, 1), 0)
    for j in range(n - 1):
        times = jnp.where(at > j, work[:, j : j + 1] / work[j : j + 1, j : j + 1], 0.0)
        work = work - times * work[j : j + 1, :]
    pivots = jnp.sum(jnp.where(row == col, work[:, :n], 0.0), axis=1, keepdims=True)
    inverse = work[:, n:] / jnp.sqrt(pivots)
    inverse_ref[...] = inverse
    width = cur_ref.shape[2]
    for r in range(cur_ref.shape[0]):
        block = jnp.dot(inverse, cur_ref[r].astype(F32), precision=HI, preferred_element_type=F32).astype(BF16)
        if flat:
            next_ref[:, r * width : (r + 1) * width] = block
        else:
            next_ref[r] = block


def trace_kernel(image_ref, next_ref, out_ref):
    value = jnp.zeros(image_ref.shape[1:], F32)
    for r in range(image_ref.shape[0]):
        value = value + image_ref[r] * next_ref[r].astype(F32)
    out_ref[...] = jnp.sum(value.reshape(-1, 8, value.shape[1]), axis=0)


def ritz_kernel(total, inverse_ref, sum_ref, ritz_ref):
    inverse = inverse_ref[...]
    half = jnp.dot(inverse, sum_ref[...], precision=HI, preferred_element_type=F32)
    ritz_ref[...] = mm_t(half, inverse, HI) / total


def everywhere(x, devices):
    step = 1
    while step < devices:
        x = x + lax.ppermute(x, "dom", [(i, i ^ step) for i in range(devices)])
        step *= 2
    return x


def local(vectors, diag_tiles, pair_tiles, halo_tiles, halo_rows, pair_index, pair_count):
    k, own_rows = vectors.shape
    blocks, size, _ = diag_tiles.shape
    edges, peers = pair_index.shape[1], halo_rows.shape[1]
    total = float(own_rows * peers)
    rows = halo_rows[0]
    index = ((pair_index[0, :, 0], "s"), (pair_index[0, :, 1], "s"), (pair_count, "s"))
    block = ((blocks, k, size), BF16)
    wide = ((blocks, k, size), F32)
    spots = ((peers, k, size), BF16)
    square = ((k, k), F32)
    unit = 2 * k * size * size

    [tiles] = call(tile_kernel, [((peers, size, size), BF16)], [(halo_tiles, "v")], 1 << 20, 8 << 20)

    def exchange(out):
        return lax.all_to_all(out, "dom", 0, 0, tiled=True)

    def own(mode, cur, extra=(), ahead=(), outs=()):
        ins = [*index, *ahead, (cur, "v"), (diag_tiles, "v"), (pair_tiles.reshape(edges, 2, size, size), "v"), *extra]
        return call(functools.partial(local_kernel, mode, total), [wide, *outs], ins, unit * (blocks + 2 * edges), 9 << 20)

    def halo(mode, arrived, part, outs, extra=()):
        ins = [(rows, "s"), (arrived, "v"), (tiles, "v"), (part, "v"), *extra]
        scratch = [pltpu.VMEM((blocks, k, size), F32)]
        return call(functools.partial(halo_kernel, mode), outs, ins, unit * peers, 10 << 20, scratch)

    def gram(cur):
        [value] = call(functools.partial(gram_kernel, total), [square], [(cur, "v")], 2 * k * k * own_rows, 1 << 20)
        return everywhere(value, peers)

    def factor(total_gram, cur, flat):
        outs = [square, ((k, own_rows), BF16) if flat else block]
        return call(functools.partial(factor_kernel, flat), outs, [(total_gram, "v"), (cur, "v")], 1 << 24, 2 << 20)

    def filtered(prev, cur, out, centre, steps):
        for _ in range(steps):
            arrived = exchange(out)
            [part] = own("filter", cur, [(prev, "v")], [(centre, "s")])
            prev, (cur, out) = cur, halo("filter", arrived, part, [block, spots])
        return cur, out

    start, out = call(start_kernel, [block, spots], [(rows, "s"), (vectors, "v")], 1 << 20, 4 << 20)
    arrived = exchange(out)
    [part] = own("start", start)
    cur, out = halo("start", arrived, part, [block, spots])
    cur, out = filtered(start, cur, out, jnp.full((1, 1), FIRST_CENTRE, F32), 3)

    arrived = exchange(out)
    inverse, basis_one = factor(gram(cur), cur, False)
    [part] = own("image", cur)
    image, cur, out = halo("image", arrived, part, [wide, block, spots], [(inverse, "v")])

    arrived = exchange(out)
    [trace] = call(trace_kernel, [((8, size), F32)], [(image, "v"), (basis_one, "v")], 1 << 20, 2 << 20)
    extra = [(image, "v"), (basis_one, "v"), (everywhere(trace, peers), "v")]
    part, first, centre = own("second", cur, extra, (), [block, ((8, size), F32)])
    cur, out = halo("filter", arrived, part, [block, spots])
    cur, out = filtered(first, cur, out, centre, 2)

    arrived = exchange(out)
    inverse, basis = factor(gram(cur), cur, True)
    [part] = own("image", cur)
    [partial] = halo("last", arrived, part, [square], [(cur, "v")])
    [ritz] = call(
        functools.partial(ritz_kernel, total), [square], [(inverse, "v"), (everywhere(partial, peers), "v")], 1 << 20, 1 << 16
    )
    return basis, ritz


def solution(mesh):
    return jax.shard_map(
        local,
        mesh=mesh,
        in_specs=(
            P(None, "dom"),
            P("dom", None, None),
            P("dom", None, None, None),
            P("dom", None, None),
            P("dom", None),
            P("dom", None, None),
            P("dom"),
        ),
        out_specs=(P(None, "dom"), P()),
        check_vma=False,
    )
```

time: 766 us -> 532 us (0.69); the launches traced: 755 us -> 530 us
  blocking collectives: 251 us -> 0 us
  matrix products: 200 us -> 0 us
  waiting for transfers between devices: 115 us -> 213 us
  Pallas kernels: 0 us -> 88.6 us
  other arithmetic: 63.2 us -> 0.13 us
  starting transfers between devices: 59.9 us -> 118 us
  local copies, waits for them, and re-layouts: 61.7 us -> 108 us
    psum x4 -> x0, blocking collectives: 251 us -> none  [the longest x2 126 us: subspace_step(): gram_matrix = lax.psum(partial_value, 'dom')]
    dot_general x69 -> x0, matrix products: 200 us -> none  [the longest x9 52.8 us: halo_terms(): jnp.einsum('kpj,pij->kpi', arrived, halo_tiles, preferred_element_type=jn...]
    unnamed x99 -> x166, local copies, waits for them, and re-layouts: 4.97 us -> 108 us
    pallas_call x0 -> x26, Pallas kernels: none -> 88.6 us  [call(): pl.pallas_call(body, out_shape=[pltpu.VMEM(s, d) for s, d in outs], in_sp...]
    ppermute x0 -> x28, waiting for transfers between devices: none -> 64.4 us  [everywhere(): x = x + lax.ppermute(x, 'dom', [(i, i ^ step) for i in range(devices)])]
    gather x27 -> x0, local copies, waits for them, and re-layouts: 54.6 us -> none  [the longest x9 19.3 us: operator(): outgoing = jnp.take(blocked, send_rows, axis=1)]
    ppermute x0 -> x28, starting transfers between devices: none -> 53 us  [everywhere(): x = x + lax.ppermute(x, 'dom', [(i, i ^ step) for i in range(devices)])]
    all_to_all x9, waiting for transfers between devices: 115 us -> 148 us  [exchange(): return lax.all_to_all(out, 'dom', 0, 0, tiled=True)]
  transfers between devices with their start and end apart: 9 -> 37, of which waited for: 9 -> 32; matrix products, arithmetic and copies ran while one was open for 20% -> 0% of each run, Pallas kernels for 0% -> 10%
where the time goes in v1:
time: 532 us; the launch traced here: 530 us
  waiting for transfers between devices  213 us (40%)
  starting transfers between devices  118 us (22%)
  local copies, waits for them, and re-layouts  108 us (20%)
  Pallas kernels  88.6 us (17%)
    all_to_all x9, waiting for transfers between devices, exchange(): return lax.all_to_all(out, 'dom', 0, 0, tiled=True)  148 us
    unnamed x166, local copies, waits for them, and re-layouts  108 us
    pallas_call x26, Pallas kernels, call(): pl.pallas_call(body, out_shape=[pltpu.VMEM(s, d) for s, d in outs], in_sp...  88.6 us
    all_to_all x9, starting transfers between devices, exchange(): return lax.all_to_all(out, 'dom', 0, 0, tiled=True)  65.1 us
    ppermute x28, waiting for transfers between devices, everywhere(): x = x + lax.ppermute(x, 'dom', [(i, i ^ step) for i in range(devices)])  64.4 us
    ppermute x28, starting transfers between devices, everywhere(): x = x + lax.ppermute(x, 'dom', [(i, i ^ step) for i in range(devices)])  53 us
  transfers between devices with their start and end apart: 37, of which 32 were waited for; matrix products, arithmetic and copies ran while one was open for 0% of the time, Pallas kernels for 10%

profile of v1, /device:TPU:0, one launch (start us, length us, event | category | flops | bytes accessed | tf_op | source)
XLA Modules:
  0.0 530.0 jit_solution(9753225608758380311)
XLA Ops:
  5.4 11.7 %all-to-all-start = ((bf16[128,64,128]{2,1,0:T(8,128)(2,1)}), bf16[128,64,128]{2,1,0:T(8,128)(2,1)}, u32[]{:S(2)}, u32[]{:S(2)}) async-start(bf16[128,64,128]{2,1,0:T(8,128)(2,1)} %copy-done.60), calls=%async_computation | async-start | bytes 4194304 | tf_op jit(solution)/shard_map/all_to_all | solution.py:224
  19.9 2.8 shard_map.87.tiles_ref
  24.8 3.1 shard_map.88.part_ref
  28.9 18.1 %all-to-all-done.arrived_ref = bf16[128,64,128]{2,1,0:T(8,128)(2,1)} async-done(((bf16[128,64,128]{2,1,0:T(8,128)(2,1)}), bf16[128,64,128]{2,1,0:T(8,128)(2,1)}, u32[]{:S(2)}, u32[]{:S(2)}) %all-to-all-start) | async-done | bytes 2097184 | tf_op jit(solution)/shard_map/all_to_all | solution.py:224
  50.5 5.3 shard_map.89
  57.9 4.6 all-to-all-start.1
  67.4 3.1 shard_map.90.part_ref
  71.6 21.3 %all-to-all-done.1.arrived_ref = bf16[128,64,128]{2,1,0:T(8,128)(2,1)S(1)} async-done(((bf16[128,64,128]{2,1,0:T(8,128)(2,1)}), bf16[128,64,128]{2,1,0:T(8,128)(2,1)S(1)}, u32[]{:S(2)}, u32[]{:S(2)}) %all-to-all-start.1) | async-done | bytes 2097184 | tf_op jit(solution)/shard_map/all_to_all | solution.py:224
  96.4 4.2 shard_map.91
  102.8 4.6 all-to-all-start.2
  112.3 3.1 shard_map.92.part_ref
  116.5 21.4 %all-to-all-done.2.arrived_ref = bf16[128,64,128]{2,1,0:T(8,128)(2,1)S(1)} async-done(((bf16[128,64,128]{2,1,0:T(8,128)(2,1)}), bf16[128,64,128]{2,1,0:T(8,128)(2,1)S(1)}, u32[]{:S(2)}, u32[]{:S(2)}) %all-to-all-start.2) | async-done | bytes 2097184 | tf_op jit(solution)/shard_map/all_to_all | solution.py:224
  141.3 4.2 shard_map.93
  147.7 4.6 all-to-all-start.3
  157.2 3.1 shard_map.94.part_ref
  161.4 21.3 %all-to-all-done.3.arrived_ref = bf16[128,64,128]{2,1,0:T(8,128)(2,1)S(1)} async-done(((bf16[128,64,128]{2,1,0:T(8,128)(2,1)}), bf16[128,64,128]{2,1,0:T(8,128)(2,1)S(1)}, u32[]{:S(2)}, u32[]{:S(2)}) %all-to-all-start.3) | async-done | bytes 2097184 | tf_op jit(solution)/shard_map/all_to_all | solution.py:224
  186.2 4.2 shard_map.95
  192.5 4.6 all-to-all-start.4
  201.0 11.9 %collective-permute-done.1 = f32[64,64]{1,0:T(8,128)S(1)} collective-permute-done((f32[64,64]{1,0:T(8,128)S(1)}, f32[64,64]{1,0:T(8,128)S(1)}, u32[]{:S(2)}, u32[]{:S(2)}) %collective-permute-start.1) | collective-permute-done | bytes 16416 | tf_op jit(solution)/shard_map/ppermute | solution.py:203
  215.7 9.3 %collective-permute-done.2 = f32[64,64]{1,0:T(8,128)S(1)} collective-permute-done((f32[64,64]{1,0:T(8,128)S(1)}, f32[64,64]{1,0:T(8,128)S(1)}, u32[]{:S(2)}, u32[]{:S(2)}) %collective-permute-start.2) | collective-permute-done | bytes 16416 | tf_op jit(solution)/shard_map/ppermute | solution.py:203
  228.9 4.8 collective-permute-start.4
  239.6 4.1 collective-permute-start.6
  243.7 2.8 copy-done.3
  247.5 3.1 shard_map.96.part_ref
  251.7 6.4 %shard_map.98 = (f32[64,64]{1,0:T(8,128)S(1)}, bf16[32,64,128]{2,1,0:T(8,128)(2,1)S(1)}) custom-call(f32[64,64]{1,0:T(8,128)S(1)} %add.90.gram_ref, bf16[32,64,128]{2,1,0:T(8,128)(2,1)S(1)} %copy-done.23), custom_call_target="tpu_custom_call" | custom-call | flops 16777216 | bytes 2097152 | tf_op jit(solution)/shard_map/pallas_call | solution.py:23
  262.4 5.1 shard_map.99
  270.7 11.1 %all-to-all-start.5 = ((bf16[128,64,128]{2,1,0:T(8,128)(2,1)}), bf16[128,64,128]{2,1,0:T(8,128)(2,1)S(1)}, u32[]{:S(2)}, u32[]{:S(2)}) async-start(bf16[128,64,128]{2,1,0:T(8,128)(2,1)} %copy-done.57), calls=%async_computation.5 | async-start | bytes 4194304 | tf_op jit(solution)/shard_map/all_to_all | solution.py:224
  286.5 2.8 collective-permute-done.8
  291.9 6.6 %collective-permute-done.9 = f32[8,128]{1,0:T(8,128)S(1)} collective-permute-done((f32[8,128]{1,0:T(8,128)S(1)}, f32[8,128]{1,0:T(8,128)S(1)}, u32[]{:S(2)}, u32[]{:S(2)}) %collective-permute-start.9) | collective-permute-done | bytes 4128 | tf_op jit(solution)/shard_map/ppermute | solution.py:203
  300.6 5.0 collective-permute-done.10
  310.8 9.9 %collective-permute-start.12 = (f32[8,128]{1,0:T(8,128)S(1)}, f32[8,128]{1,0:T(8,128)S(1)}, u32[]{:S(2)}, u32[]{:S(2)}) collective-permute-start(f32[8,128]{1,0:T(8,128)S(1)} %add.95), channel_id=1, source_target_pairs={{0,32},{1,33},{2,34},{3,35},{4,36},{5,37},{6,38},{7,39},{8,40},{9,... | collective-permute-start | bytes 12296 | tf_op jit(solution)/shard_map/ppermute | solution.py:203
  322.2 4.2 collective-permute-start.13
  332.9 3.2 shard_map.101
  341.4 4.2 shard_map.102
  347.8 13.3 %all-to-all-start.6 = ((bf16[128,64,128]{2,1,0:T(8,128)(2,1)}), bf16[128,64,128]{2,1,0:T(8,128)(2,1)S(1)}, u32[]{:S(2)}, u32[]{:S(2)}) async-start(bf16[128,64,128]{2,1,0:T(8,128)(2,1)} %copy-done.62), calls=%async_computation.6 | async-start | bytes 4194304 | tf_op jit(solution)/shard_map/all_to_all | solution.py:224
  366.0 3.2 shard_map.103.part_ref
  370.3 21.3 %all-to-all-done.6.arrived_ref = bf16[128,64,128]{2,1,0:T(8,128)(2,1)S(1)} async-done(((bf16[128,64,128]{2,1,0:T(8,128)(2,1)}), bf16[128,64,128]{2,1,0:T(8,128)(2,1)S(1)}, u32[]{:S(2)}, u32[]{:S(2)}) %all-to-all-start.6) | async-done | bytes 2097184 | tf_op jit(solution)/shard_map/all_to_all | solution.py:224
  395.0 4.2 shard_map.104
  401.4 4.6 all-to-all-start.7
  410.9 3.2 shard_map.105.part_ref
  415.2 21.3 %all-to-all-done.7.arrived_ref = bf16[128,64,128]{2,1,0:T(8,128)(2,1)S(1)} async-done(((bf16[128,64,128]{2,1,0:T(8,128)(2,1)}), bf16[128,64,128]{2,1,0:T(8,128)(2,1)S(1)}, u32[]{:S(2)}, u32[]{:S(2)}) %all-to-all-start.7) | async-done | bytes 2097184 | tf_op jit(solution)/shard_map/all_to_all | solution.py:224
  442.8 4.2 shard_map.106
  448.4 5.8 %all-to-all-start.8 = ((bf16[128,64,128]{2,1,0:T(8,128)(2,1)}), bf16[128,64,128]{2,1,0:T(8,128)(2,1)}, u32[]{:S(2)}, u32[]{:S(2)}) async-start(bf16[128,64,128]{2,1,0:T(8,128)(2,1)} %copy-done.59), calls=%async_computation.8 | async-start | bytes 4194304 | tf_op jit(solution)/shard_map/all_to_all | solution.py:224
  457.5 3.1 shard_map.109.part_ref
  460.6 23.6 %all-to-all-done.8.arrived_ref = bf16[128,64,128]{2,1,0:T(8,128)(2,1)} async-done(((bf16[128,64,128]{2,1,0:T(8,128)(2,1)}), bf16[128,64,128]{2,1,0:T(8,128)(2,1)}, u32[]{:S(2)}, u32[]{:S(2)}) %all-to-all-start.8) | async-done | bytes 2097184 | tf_op jit(solution)/shard_map/all_to_all | solution.py:224
  486.4 6.7 %shard_map.110 = f32[64,64]{1,0:T(8,128)S(1)} custom-call(s32[128]{0:T(128)S(1)} %bitcast.16, bf16[128,64,128]{2,1,0:T(8,128)(2,1)} %all-to-all-done.8.arrived_ref, bf16[128,128,128]{2,1,0:T(8,128)(2,1)S(1)} %copy-done.17, f32[32,64,128]{2,1,0:T(8,128)S(1)} %shard_map.109.part_ref, bf16[32,64,128]{2,1,0:T(8,128)(2,1)S(1)} %get-tuple-element.50.cur_ref.refs_0_), custom_call_target="tpu_custom_call" | custom-call | flops 268435456 | bytes 10485760 | tf_op jit(solution)/shard_map/pallas_call | solution.py:23
  517.2 2.9 collective-permute-start.27
  521.8 6.4 %shard_map.108 = (f32[64,64]{1,0:T(8,128)S(1)}, bf16[64,4096]{1,0:T(8,128)(2,1)S(1)}) custom-call(f32[64,64]{1,0:T(8,128)S(1)} %add.104.gram_ref, bf16[32,64,128]{2,1,0:T(8,128)(2,1)S(1)} %get-tuple-element.50.cur_ref.refs_0_), custom_call_target="tpu_custom_call" | custom-call | flops 16777216 | bytes 2097152 | tf_op jit(solution)/shard_map/pallas_call | solution.py:23
  (248 shorter events, 163.8 us)
Async XLA Ops:
  5.4 19.4 %slice-start = ((s8[6291456]{0:T(1024)(128)(4,1)}), s8[2097152]{0:T(1024)(128)(4,1)S(1)}, s32[]{:S(2)}) async-start(s8[6291456]{0:T(1024)(128)(4,1)} %bitcast.5), calls=%async_computation.9 | async-start | bytes 4194304
  5.4 41.7 %all-to-all-start = ((bf16[128,64,128]{2,1,0:T(8,128)(2,1)}), bf16[128,64,128]{2,1,0:T(8,128)(2,1)}, u32[]{:S(2)}, u32[]{:S(2)}) async-start(bf16[128,64,128]{2,1,0:T(8,128)(2,1)} %copy-done.60), calls=%async_computation | async-start | bytes 4194304 | tf_op jit(solution)/shard_map/all_to_all | solution.py:224
  19.9 4.8 copy-start.79
  19.9 4.9 slice-start.1
  19.9 4.9 copy-start.18
  19.9 4.9 copy-start.46
  24.8 22.3 %copy-start.78 = (s32[1,128]{1,0:T(1,128)S(1)}, s32[1,128]{1,0:T(1,128)}, u32[]{:S(2)}) copy-start(s32[1,128]{1,0:T(1,128)} %param.11) | copy-start | bytes 1540
  57.9 35.1 %all-to-all-start.1 = ((bf16[128,64,128]{2,1,0:T(8,128)(2,1)}), bf16[128,64,128]{2,1,0:T(8,128)(2,1)S(1)}, u32[]{:S(2)}, u32[]{:S(2)}) async-start(bf16[128,64,128]{2,1,0:T(8,128)(2,1)} %copy-done.64), calls=%async_computation.1 | async-start | bytes 4194304 | tf_op jit(solution)/shard_map/all_to_all | solution.py:224
  62.5 2.8 copy-start
  102.8 35.1 %all-to-all-start.2 = ((bf16[128,64,128]{2,1,0:T(8,128)(2,1)}), bf16[128,64,128]{2,1,0:T(8,128)(2,1)S(1)}, u32[]{:S(2)}, u32[]{:S(2)}) async-start(bf16[128,64,128]{2,1,0:T(8,128)(2,1)} %copy-done.65), calls=%async_computation.2 | async-start | bytes 4194304 | tf_op jit(solution)/shard_map/all_to_all | solution.py:224
  147.7 35.1 %all-to-all-start.3 = ((bf16[128,64,128]{2,1,0:T(8,128)(2,1)}), bf16[128,64,128]{2,1,0:T(8,128)(2,1)S(1)}, u32[]{:S(2)}, u32[]{:S(2)}) async-start(bf16[128,64,128]{2,1,0:T(8,128)(2,1)} %copy-done.61), calls=%async_computation.3 | async-start | bytes 4194304 | tf_op jit(solution)/shard_map/all_to_all | solution.py:224
  152.3 2.8 copy-start.2
  192.5 66.4 %all-to-all-start.4 = ((bf16[128,64,128]{2,1,0:T(8,128)(2,1)}), bf16[128,64,128]{2,1,0:T(8,128)(2,1)S(1)}, u32[]{:S(2)}, u32[]{:S(2)}) async-start(bf16[128,64,128]{2,1,0:T(8,128)(2,1)} %copy-done.58), calls=%async_computation.4 | async-start | bytes 4194304 | tf_op jit(solution)/shard_map/all_to_all | solution.py:224
  198.6 1.3 collective-permute-start
  199.9 13.0 %collective-permute-start.1 = (f32[64,64]{1,0:T(8,128)S(1)}, f32[64,64]{1,0:T(8,128)S(1)}, u32[]{:S(2)}, u32[]{:S(2)}) collective-permute-start(f32[64,64]{1,0:T(8,128)S(1)} %add.84), channel_id=1, source_target_pairs={{0,2},{1,3},{2,0},{3,1},{4,6},{5,7},{6,4},{7,5},{8,10},{9,11},{10,... | collective-permute-start | bytes 49160 | tf_op jit(solution)/shard_map/ppermute | solution.py:203
  212.9 12.1 %collective-permute-start.2 = (f32[64,64]{1,0:T(8,128)S(1)}, f32[64,64]{1,0:T(8,128)S(1)}, u32[]{:S(2)}, u32[]{:S(2)}) collective-permute-start(f32[64,64]{1,0:T(8,128)S(1)} %add.85), channel_id=1, source_target_pairs={{0,4},{1,5},{2,6},{3,7},{4,0},{5,1},{6,2},{7,3},{8,12},{9,13},{10,... | collective-permute-start | bytes 49160 | tf_op jit(solution)/shard_map/ppermute | solution.py:203
  225.0 3.9 collective-permute-start.3
  228.9 6.7 %collective-permute-start.4 = (f32[64,64]{1,0:T(8,128)S(1)}, f32[64,64]{1,0:T(8,128)S(1)}, u32[]{:S(2)}, u32[]{:S(2)}) collective-permute-start(f32[64,64]{1,0:T(8,128)S(1)} %add.87), channel_id=1, source_target_pairs={{0,16},{1,17},{2,18},{3,19},{4,20},{5,21},{6,22},{7,23},{8,24},{9,... | collective-permute-start | bytes 49160 | tf_op jit(solution)/shard_map/ppermute | solution.py:203
  235.6 4.0 collective-permute-start.5
  239.6 12.1 %collective-permute-start.6 = (f32[64,64]{1,0:T(8,128)S(1)}, f32[64,64]{1,0:T(8,128)S(1)}, u32[]{:S(2)}, u32[]{:S(2)}) collective-permute-start(f32[64,64]{1,0:T(8,128)S(1)} %add.89), channel_id=1, source_target_pairs={{0,64},{1,65},{2,66},{3,67},{4,68},{5,69},{6,70},{7,71},{8,72},{9,... | collective-permute-start | bytes 49160 | tf_op jit(solution)/shard_map/ppermute | solution.py:203
  270.7 67.3 %all-to-all-start.5 = ((bf16[128,64,128]{2,1,0:T(8,128)(2,1)}), bf16[128,64,128]{2,1,0:T(8,128)(2,1)S(1)}, u32[]{:S(2)}, u32[]{:S(2)}) async-start(bf16[128,64,128]{2,1,0:T(8,128)(2,1)} %copy-done.57), calls=%async_computation.5 | async-start | bytes 4194304 | tf_op jit(solution)/shard_map/all_to_all | solution.py:224
  284.1 43.9 %copy-start.26 = (f32[32,64,128]{2,1,0:T(8,128)S(1)}, f32[32,64,128]{2,1,0:T(8,128)}, u32[]{:S(2)}) copy-start(f32[32,64,128]{2,1,0:T(8,128)} %copy-done.24) | copy-start | bytes 3145732
  284.2 1.2 collective-permute-start.7
  285.4 3.9 collective-permute-start.8
  289.3 9.2 %collective-permute-start.9 = (f32[8,128]{1,0:T(8,128)S(1)}, f32[8,128]{1,0:T(8,128)S(1)}, u32[]{:S(2)}, u32[]{:S(2)}) collective-permute-start(f32[8,128]{1,0:T(8,128)S(1)} %add.92), channel_id=1, source_target_pairs={{0,4},{1,5},{2,6},{3,7},{4,0},{5,1},{6,2},{7,3},{8,12},{9,13},{10,... | collective-permute-start | bytes 12296 | tf_op jit(solution)/shard_map/ppermute | solution.py:203
  298.5 7.1 %collective-permute-start.10 = (f32[8,128]{1,0:T(8,128)S(1)}, f32[8,128]{1,0:T(8,128)S(1)}, u32[]{:S(2)}, u32[]{:S(2)}) collective-permute-start(f32[8,128]{1,0:T(8,128)S(1)} %add.93), channel_id=1, source_target_pairs={{0,8},{1,9},{2,10},{3,11},{4,12},{5,13},{6,14},{7,15},{8,0},{9,1},... | collective-permute-start | bytes 12296 | tf_op jit(solution)/shard_map/ppermute | solution.py:203
  305.7 5.1 collective-permute-start.11
  310.8 11.4 %collective-permute-start.12 = (f32[8,128]{1,0:T(8,128)S(1)}, f32[8,128]{1,0:T(8,128)S(1)}, u32[]{:S(2)}, u32[]{:S(2)}) collective-permute-start(f32[8,128]{1,0:T(8,128)S(1)} %add.95), channel_id=1, source_target_pairs={{0,32},{1,33},{2,34},{3,35},{4,36},{5,37},{6,38},{7,39},{8,40},{9,... | collective-permute-start | bytes 12296 | tf_op jit(solution)/shard_map/ppermute | solution.py:203
  322.2 5.8 %collective-permute-start.13 = (f32[8,128]{1,0:T(8,128)S(1)}, f32[8,128]{1,0:T(8,128)S(1)}, u32[]{:S(2)}, u32[]{:S(2)}) collective-permute-start(f32[8,128]{1,0:T(8,128)S(1)} %add.96), channel_id=1, source_target_pairs={{0,64},{1,65},{2,66},{3,67},{4,68},{5,69},{6,70},{7,71},{8,72},{9,... | collective-permute-start | bytes 12296 | tf_op jit(solution)/shard_map/ppermute | solution.py:203
  347.8 43.8 %all-to-all-start.6 = ((bf16[128,64,128]{2,1,0:T(8,128)(2,1)}), bf16[128,64,128]{2,1,0:T(8,128)(2,1)S(1)}, u32[]{:S(2)}, u32[]{:S(2)}) async-start(bf16[128,64,128]{2,1,0:T(8,128)(2,1)} %copy-done.62), calls=%async_computation.6 | async-start | bytes 4194304 | tf_op jit(solution)/shard_map/all_to_all | solution.py:224
  361.1 2.8 copy-start.5
  401.4 35.1 %all-to-all-start.7 = ((bf16[128,64,128]{2,1,0:T(8,128)(2,1)}), bf16[128,64,128]{2,1,0:T(8,128)(2,1)S(1)}, u32[]{:S(2)}, u32[]{:S(2)}) async-start(bf16[128,64,128]{2,1,0:T(8,128)(2,1)} %copy-done.63), calls=%async_computation.7 | async-start | bytes 4194304 | tf_op jit(solution)/shard_map/all_to_all | solution.py:224
  406.0 2.8 copy-start.6
  448.4 35.8 %all-to-all-start.8 = ((bf16[128,64,128]{2,1,0:T(8,128)(2,1)}), bf16[128,64,128]{2,1,0:T(8,128)(2,1)}, u32[]{:S(2)}, u32[]{:S(2)}) async-start(bf16[128,64,128]{2,1,0:T(8,128)(2,1)} %copy-done.59), calls=%async_computation.8 | async-start | bytes 4194304 | tf_op jit(solution)/shard_map/all_to_all | solution.py:224
  454.6 38.7 %collective-permute-start.14 = (f32[64,64]{1,0:T(8,128)S(1)}, f32[64,64]{1,0:T(8,128)S(1)}, u32[]{:S(2)}, u32[]{:S(2)}) collective-permute-start(f32[64,64]{1,0:T(8,128)S(1)} %shard_map.107), channel_id=1, source_target_pairs={{0,1},{1,0},{2,3},{3,2},{4,5},{5,4},{6,7},{7,6},{8,9},{9,8},{10,11... | collective-permute-start | bytes 49160 | tf_op jit(solution)/shard_map/ppermute | solution.py:203
  493.1 1.3 collective-permute-start.21
  493.3 4.1 collective-permute-start.15
  494.4 4.1 collective-permute-start.22
  497.3 5.4 %collective-permute-start.16 = (f32[64,64]{1,0:T(8,128)S(1)}, f32[64,64]{1,0:T(8,128)S(1)}, u32[]{:S(2)}, u32[]{:S(2)}) collective-permute-start(f32[64,64]{1,0:T(8,128)S(1)} %add.99), channel_id=1, source_target_pairs={{0,4},{1,5},{2,6},{3,7},{4,0},{5,1},{6,2},{7,3},{8,12},{9,13},{10,... | collective-permute-start | bytes 49160 | tf_op jit(solution)/shard_map/ppermute | solution.py:203
  498.5 5.4 %collective-permute-start.23 = (f32[64,64]{1,0:T(8,128)S(1)}, f32[64,64]{1,0:T(8,128)S(1)}, u32[]{:S(2)}, u32[]{:S(2)}) collective-permute-start(f32[64,64]{1,0:T(8,128)S(1)} %add.106), channel_id=1, source_target_pairs={{0,4},{1,5},{2,6},{3,7},{4,0},{5,1},{6,2},{7,3},{8,12},{9,13},{10,... | collective-permute-start | bytes 49160 | tf_op jit(solution)/shard_map/ppermute | solution.py:203
  502.7 4.0 collective-permute-start.17
  503.9 3.9 collective-permute-start.24
  506.8 5.4 %collective-permute-start.18 = (f32[64,64]{1,0:T(8,128)S(1)}, f32[64,64]{1,0:T(8,128)S(1)}, u32[]{:S(2)}, u32[]{:S(2)}) collective-permute-start(f32[64,64]{1,0:T(8,128)S(1)} %add.101), channel_id=1, source_target_pairs={{0,16},{1,17},{2,18},{3,19},{4,20},{5,21},{6,22},{7,23},{8,24},{9,... | collective-permute-start | bytes 49160 | tf_op jit(solution)/shard_map/ppermute | solution.py:203
  507.8 5.4 %collective-permute-start.25 = (f32[64,64]{1,0:T(8,128)S(1)}, f32[64,64]{1,0:T(8,128)S(1)}, u32[]{:S(2)}, u32[]{:S(2)}) collective-permute-start(f32[64,64]{1,0:T(8,128)S(1)} %add.108), channel_id=1, source_target_pairs={{0,16},{1,17},{2,18},{3,19},{4,20},{5,21},{6,22},{7,23},{8,24},{9,... | collective-permute-start | bytes 49160 | tf_op jit(solution)/shard_map/ppermute | solution.py:203
  512.2 4.2 collective-permute-start.19
  513.3 3.9 collective-permute-start.26
  516.4 5.4 %collective-permute-start.20 = (f32[64,64]{1,0:T(8,128)S(1)}, f32[64,64]{1,0:T(8,128)S(1)}, u32[]{:S(2)}, u32[]{:S(2)}) collective-permute-start(f32[64,64]{1,0:T(8,128)S(1)} %add.103), channel_id=1, source_target_pairs={{0,64},{1,65},{2,66},{3,67},{4,68},{5,69},{6,70},{7,71},{8,72},{9,... | collective-permute-start | bytes 49160 | tf_op jit(solution)/shard_map/ppermute | solution.py:203
  517.2 11.9 %collective-permute-start.27 = (f32[64,64]{1,0:T(8,128)S(1)}, f32[64,64]{1,0:T(8,128)S(1)}, u32[]{:S(2)}, u32[]{:S(2)}) collective-permute-start(f32[64,64]{1,0:T(8,128)S(1)} %add.110), channel_id=1, source_target_pairs={{0,64},{1,65},{2,66},{3,67},{4,68},{5,69},{6,70},{7,71},{8,72},{9,... | collective-permute-start | bytes 49160 | tf_op jit(solution)/shard_map/ppermute | solution.py:203
  (71 other events, 96.0 us)

commit v2 on v0

v2 whole, which is shorter than its diff:
```python
import functools

import jax
import jax.numpy as jnp
from jax import lax
from jax.experimental import pallas as pl
from jax.experimental.pallas import tpu as pltpu
from jax.sharding import PartitionSpec as P

FIRST_CENTRE = -0.5
F32, BF16 = jnp.float32, jnp.bfloat16
HI = lax.Precision.HIGHEST
VM = pl.BlockSpec(memory_space=pltpu.VMEM)
SM = pl.BlockSpec(memory_space=pltpu.SMEM)


HBM = pl.BlockSpec(memory_space=pltpu.HBM)
NODE = 8


def call(body, outs, ins, flops, moved, scratch=()):
    place = {"a": pltpu.HBM, "v": pltpu.VMEM}
    spec = {"a": HBM, "v": VM, "h": VM, "s": SM}
    return pl.pallas_call(
        body,
        out_shape=[(place[kind] if kind in place else jax.ShapeDtypeStruct)(shape, dtype) for shape, dtype, kind in outs],
        in_specs=[spec[kind] for _, kind in ins],
        out_specs=[spec[kind] for _, _, kind in outs],
        scratch_shapes=list(scratch),
        cost_estimate=pl.CostEstimate(flops=flops, bytes_accessed=moved, transcendentals=0),
        compiler_params=pltpu.CompilerParams(vmem_limit_bytes=30 << 20),
    )(*[pltpu.with_memory_space_constraint(x, place[kind]) if kind in place else x for x, kind in ins])


def mm(a, b):
    return jnp.dot(a, b, preferred_element_type=F32)


def mm_t(a, b, precision=None):
    return lax.dot_general(a, b, (((1,), (1,)), ((), ())), precision=precision, preferred_element_type=F32)


def thirds(x):
    high = x.astype(BF16)
    rest = x - high.astype(F32)
    middle = rest.astype(BF16)
    return high, middle, (rest - middle.astype(F32)).astype(BF16)


def begin(source, target, sem):
    copy = pltpu.make_async_copy(source, target, sem)
    copy.start()
    return copy


def spread(rows_ref, blocks_ref, slots_ref, out_ref, sems):
    half = slots_ref.shape[0] // 2
    copies = []
    for g in range(2):
        for p in range(g * half, (g + 1) * half):
            slots_ref[p] = blocks_ref[rows_ref[p]]
        copies.append(begin(slots_ref.at[pl.ds(g * half, half)], out_ref.at[pl.ds(g * half, half)], sems.at[g]))
    return copies


def start_kernel(rows_ref, vec_ref, cur_ref, out_ref, slots, sems):
    width = cur_ref.shape[2]
    for r in range(cur_ref.shape[0]):
        cur_ref[r] = vec_ref[:, r * width : (r + 1) * width]
    for copy in spread(rows_ref, cur_ref, slots, out_ref, sems):
        copy.wait()


def tile_kernel(tiles_ref, out_ref):
    def step(i, _):
        for u in range(4):
            out_ref[i * 4 + u] = tiles_ref[i * 4 + u].T
        return _

    lax.fori_loop(0, out_ref.shape[0] // 4, step, 0)


def local_kernel(mode, first_ref, second_ref, count_ref, *refs):
    if mode == "filter":
        centre_ref, cur_ref, diag_ref, pair_ref, prev_ref, acc_ref = refs
        centre = centre_ref[0, 0]
    else:
        cur_ref, diag_ref, pair_ref, acc_ref = refs
        centre = FIRST_CENTRE

    def own(r, _):
        block = cur_ref[r]
        value = mm(block, diag_ref[r])
        if mode != "image":
            value = value - centre * block.astype(F32)
        if mode == "filter":
            value = value - 0.5 * prev_ref[r].astype(F32)
        acc_ref[r] = value
        return _

    lax.fori_loop(0, cur_ref.shape[0], own, 0, unroll=4)
    count = count_ref[0]
    group = 4

    def step(i, _):
        parts = []
        for u in range(group):
            e = i * group + u
            live = jnp.where(e < count, 1.0, 0.0).astype(F32)
            r, c = first_ref[e], second_ref[e]
            parts.append((r, mm(cur_ref[c], pair_ref[e, 1]) * live))
            parts.append((c, mm(cur_ref[r], pair_ref[e, 0]) * live))
        for at, value in parts:
            acc_ref[at] += value
        return _

    lax.fori_loop(0, lax.div(count + (group - 1), group), step, 0)


def halo_sums(rows_ref, arrived_ref, tiles_ref, acc_ref):
    parts = []
    for p in range(arrived_ref.shape[0]):
        parts.append((rows_ref[p], mm(arrived_ref[p], tiles_ref[p])))
        if len(parts) > 8:
            at, value = parts.pop(0)
            acc_ref[at] += value
    for at, value in parts:
        acc_ref[at] += value


def halo_kernel(factor, rows_ref, arrived_ref, tiles_ref, part_ref, cur_ref, out_ref, tiles, part, acc, block, slots, sems):
    coming = begin(tiles_ref, tiles, sems.at[0])
    also = begin(part_ref, part, sems.at[1])
    acc[...] = jnp.zeros(acc.shape, F32)
    coming.wait()
    halo_sums(rows_ref, arrived_ref, tiles, acc)
    also.wait()
    block[...] = (factor * (acc[...] + part[...])).astype(BF16)
    going = [begin(block, cur_ref, sems.at[2])]
    going += spread(rows_ref, block, slots, out_ref, sems)
    for copy in going:
        copy.wait()


def gram_kernel(cur_ref, gram_ref):
    value = jnp.zeros(gram_ref.shape, F32)
    for r in range(cur_ref.shape[0]):
        block = cur_ref[r]
        value = value + mm_t(block, block)
    gram_ref[...] = value


def sums_kernel(keep, rows_ref, arrived_ref, tiles_ref, part_ref, cur_ref, gram_ref, *refs):
    if keep:
        image_ref, sums_ref, tiles, acc, halo, cur, sems = refs
    else:
        sums_ref, tiles, acc, halo, cur, sems = refs
    coming = begin(tiles_ref, tiles, sems.at[0])
    also = begin(part_ref, acc, sems.at[1])
    more = begin(cur_ref, cur, sems.at[2])
    halo[...] = jnp.zeros(halo.shape, F32)
    coming.wait()
    halo_sums(rows_ref, arrived_ref, tiles, halo)
    also.wait()
    acc[...] += halo[...]
    if keep:
        going = begin(acc, image_ref, sems.at[0])
    more.wait()
    k = gram_ref.shape[0]
    value = jnp.zeros((k, k), F32)
    for r in range(acc.shape[0]):
        block = cur[r]
        for third in thirds(acc[r]):
            value = value + mm_t(block, third)
    sums_ref[...] = jnp.concatenate([gram_ref[...], value], axis=1)
    if keep:
        going.wait()


def inverse_factor(gram):
    n = gram.shape[0]
    row = lax.broadcasted_iota(jnp.int32, (n, n), 0)
    col = lax.broadcasted_iota(jnp.int32, (n, n), 1)
    work = jnp.concatenate([gram, jnp.where(row == col, 1.0, 0.0).astype(F32)], axis=1)
    at = lax.broadcasted_iota(jnp.int32, work.shape, 0)
    for j in range(0, n, 2):
        first = jnp.broadcast_to(work[:, j : j + 1], work.shape)
        second = jnp.broadcast_to(work[:, j + 1 : j + 2], work.shape)
        over = 1.0 / first[j : j + 1]
        low = first[j + 1 : j + 2] * over
        upper = second[j : j + 1]
        under = 1.0 / (second[j + 1 : j + 2] - low * upper)
        below = work[j + 1 : j + 2] - low * work[j : j + 1]
        times = first * over
        again = jnp.where(at > j + 1, (second - times * upper) * under, 0.0)
        work = work - jnp.where(at > j, times, 0.0) * work[j : j + 1] - again * below
    pivots = jnp.sum(jnp.where(row == col, work[:, :n], 0.0), axis=1, keepdims=True)
    return work[:, n:] / jnp.sqrt(pivots)


def apply_square(parts, block):
    return mm(parts[0], block) + (mm(parts[1], block) + mm(parts[2], block))


def turn_kernel(total, rows_ref, sums_ref, cur_ref, image_ref, next_ref, y_ref, out_ref, centre_ref, cur, image, start, block, slots, sems):
    coming = begin(cur_ref, cur, sems.at[0])
    also = begin(image_ref, image, sems.at[1])
    k = sums_ref.shape[0]
    inverse = inverse_factor(sums_ref[:, :k] / total)
    half = jnp.dot(inverse, sums_ref[:, k:] / total, precision=HI, preferred_element_type=F32)
    centre = jnp.sum(half * inverse) / k - 1.0
    centre_ref[0, 0] = centre
    parts = thirds(inverse)
    coming.wait()
    also.wait()
    for r in range(cur.shape[0]):
        begun = apply_square(parts, cur[r]).astype(BF16)
        start[r] = begun
        turned = jnp.dot(inverse, image[r], precision=HI, preferred_element_type=F32)
        block[r] = (turned - centre * begun.astype(F32)).astype(BF16)
    going = [begin(start, next_ref, sems.at[2]), begin(block, y_ref, sems.at[3])]
    going += spread(rows_ref, block, slots, out_ref, sems)
    for copy in going:
        copy.wait()


def end_kernel(total, sums_ref, cur_ref, basis_ref, ritz_ref, cur, sems):
    coming = begin(cur_ref, cur, sems.at[0])
    k, width = sums_ref.shape[0], cur.shape[2]
    inverse = inverse_factor(sums_ref[:, :k] / total)
    half = jnp.dot(inverse, sums_ref[:, k:] / total, precision=HI, preferred_element_type=F32)
    ritz_ref[...] = mm_t(half, inverse, HI)
    parts = thirds(inverse)
    coming.wait()
    for r in range(cur.shape[0]):
        basis_ref[:, r * width : (r + 1) * width] = apply_square(parts, cur[r]).astype(BF16)


def local(vectors, diag_tiles, pair_tiles, halo_tiles, halo_rows, pair_index, pair_count):
    k, own_rows = vectors.shape
    blocks, size, _ = diag_tiles.shape
    edges, peers = pair_index.shape[1], halo_rows.shape[1]
    total = float(own_rows * peers)
    rows = halo_rows[0]
    index = ((pair_index[0, :, 0], "s"), (pair_index[0, :, 1], "s"), (pair_count, "s"))
    block, spots, square = (blocks, k, size), (peers, k, size), (k, k)
    pair_tiles = pair_tiles.reshape(edges, 2, size, size)
    unit = 2 * k * size * size

    def room(shape, dtype):
        return pltpu.VMEM(shape, dtype)

    sems = pltpu.SemaphoreType.DMA((4,))
    [tiles] = call(tile_kernel, [((peers, size, size), BF16, "h")], [(halo_tiles, "h")], 1 << 20, 8 << 20)

    def exchange(out):
        return lax.all_to_all(out, "dom", 0, 0, tiled=True)

    def own(mode, cur, extra=(), ahead=()):
        ins = [*index, *ahead, (cur, "h"), (diag_tiles, "h"), (pair_tiles, "h"), *extra]
        [part] = call(functools.partial(local_kernel, mode), [(block, F32, "h")], ins, unit * (blocks + 2 * edges), 9 << 20)
        return part

    def halo(factor, arrived, part):
        return call(
            functools.partial(halo_kernel, factor),
            [(block, BF16, "a"), (spots, BF16, "a")],
            [(rows, "s"), (arrived, "v"), (tiles, "a"), (part, "a")],
            unit * peers,
            10 << 20,
            [room(tiles.shape, BF16), room(block, F32), room(block, F32), room(block, BF16), room(spots, BF16), sems],
        )

    def everywhere(x):
        near = [list(range(g, g + NODE)) for g in range(0, peers, NODE)]
        far = [list(range(g, peers, NODE)) for g in range(NODE)]
        for groups in (near, far):
            many = jnp.broadcast_to(x[None], (len(groups[0]), *x.shape))
            x = jnp.sum(lax.all_to_all(many, "dom", 0, 0, axis_index_groups=groups, tiled=True), axis=0)
        return x

    def sums(cur, arrived, part, keep):
        [gram] = call(gram_kernel, [(square, F32, "h")], [(cur, "h")], 2 * k * k * own_rows, 1 << 20)
        outs = [(block, F32, "a")] * keep + [((k, 2 * k), F32, "h")]
        ins = [(rows, "s"), (arrived, "v"), (tiles, "a"), (part, "a"), (cur, "a"), (gram, "h")]
        scratch = [room(tiles.shape, BF16), room(block, F32), room(block, F32), room(block, BF16), sems]
        *image, value = call(functools.partial(sums_kernel, keep), outs, ins, unit * peers, 10 << 20, scratch)
        return *image, everywhere(value)

    def filtered(prev, cur, out, centre):
        for _ in range(3):
            arrived = exchange(out)
            part = own("filter", cur, [(prev, "h")], [(centre, "s")])
            prev, (cur, out) = cur, halo(2.0, arrived, part)
        return cur, out

    start, out = call(
        start_kernel,
        [(block, BF16, "h"), (spots, BF16, "a")],
        [(rows, "s"), (vectors, "h")],
        1 << 20,
        4 << 20,
        [room(spots, BF16), sems],
    )
    arrived = exchange(out)
    cur, out = halo(1.0, arrived, own("start", start))
    cur, out = filtered(start, cur, out, jnp.full((1, 1), FIRST_CENTRE, F32))

    arrived = exchange(out)
    image, value = sums(cur, arrived, own("image", cur), 1)
    begun, cur, out, centre = call(
        functools.partial(turn_kernel, total),
        [(block, BF16, "a"), (block, BF16, "a"), (spots, BF16, "a"), ((1, 1), F32, "s")],
        [(rows, "s"), (value, "h"), (cur, "a"), (image, "a")],
        1 << 24,
        4 << 20,
        [room(block, BF16), room(block, F32), room(block, BF16), room(block, BF16), room(spots, BF16), sems],
    )
    cur, out = filtered(begun, cur, out, centre)

    arrived = exchange(out)
    [value] = sums(cur, arrived, own("image", cur), 0)
    return call(
        functools.partial(end_kernel, total),
        [((k, own_rows), BF16, "h"), (square, F32, "h")],
        [(value, "h"), (cur, "a")],
        1 << 24,
        2 << 20,
        [room(block, BF16), sems],
    )


def solution(mesh):
    return jax.shard_map(
        local,
        mesh=mesh,
        in_specs=(
            P(None, "dom"),
            P("dom", None, None),
            P("dom", None, None, None),
            P("dom", None, None),
            P("dom", None),
            P("dom", None, None),
            P("dom"),
        ),
        out_specs=(P(None, "dom"), P()),
        check_vma=False,
    )
```

time: 766 us -> 451 us (0.59); the launches traced: 755 us -> 449 us
  blocking collectives: 251 us -> 48 us
  matrix products: 200 us -> 0 us
  Pallas kernels: 0 us -> 108 us
  waiting for transfers between devices: 115 us -> 190 us
  other arithmetic: 63.2 us -> 0.11 us
  local copies, waits for them, and re-layouts: 61.7 us -> 50.2 us
  starting transfers between devices: 59.9 us -> 51.5 us
    psum x4 -> x0, blocking collectives: 251 us -> none  [the longest x2 126 us: subspace_step(): gram_matrix = lax.psum(partial_value, 'dom')]
    dot_general x69 -> x0, matrix products: 200 us -> none  [the longest x9 52.8 us: halo_terms(): jnp.einsum('kpj,pij->kpi', arrived, halo_tiles, preferred_element_type=jn...]
    pallas_call x0 -> x24, Pallas kernels: none -> 108 us  [call(): pl.pallas_call(body, out_shape=[(place[kind] if kind in place else jax.Sh...]
    all_to_all x9, waiting for transfers between devices: 115 us -> 190 us  [exchange(): return lax.all_to_all(out, 'dom', 0, 0, tiled=True)]
    gather x27 -> x0, local copies, waits for them, and re-layouts: 54.6 us -> none  [the longest x9 19.3 us: operator(): outgoing = jnp.take(blocked, send_rows, axis=1)]
    all_to_all x0 -> x4, blocking collectives: none -> 48 us  [everywhere(): lax.all_to_all(many, 'dom', 0, 0, axis_index_groups=groups, tiled=True)]
    unnamed x99 -> x84, local copies, waits for them, and re-layouts: 4.97 us -> 50.1 us
    select_n x10 -> x0, other arithmetic: 29.4 us -> none  [operator(): outgoing = jnp.take(blocked, send_rows, axis=1)]
  transfers between devices with their start and end apart: 9 -> 9, of which waited for: 9 -> 9; matrix products, arithmetic and copies ran while one was open for 20% -> 0% of each run, Pallas kernels for 0% -> 8%
where the time goes in v2:
time: 451 us; the launch traced here: 449 us
  waiting for transfers between devices  190 us (42%)
  Pallas kernels  108 us (24%)
  starting transfers between devices  51.5 us (11%)
  local copies, waits for them, and re-layouts  50.2 us (11%)
  blocking collectives  48 us (11%)
    all_to_all x9, waiting for transfers between devices, exchange(): return lax.all_to_all(out, 'dom', 0, 0, tiled=True)  190 us
    pallas_call x24, Pallas kernels, call(): pl.pallas_call(body, out_shape=[(place[kind] if kind in place else jax.Sh...  108 us
    all_to_all x9, starting transfers between devices, exchange(): return lax.all_to_all(out, 'dom', 0, 0, tiled=True)  51.5 us
    unnamed x84, local copies, waits for them, and re-layouts  50.1 us
    all_to_all x4, blocking collectives, everywhere(): lax.all_to_all(many, 'dom', 0, 0, axis_index_groups=groups, tiled=True)  48 us
  transfers between devices with their start and end apart: 9, of which 9 were waited for; matrix products, arithmetic and copies ran while one was open for 0% of the time, Pallas kernels for 8%

profile of v2, /device:TPU:0, one launch (start us, length us, event | category | flops | bytes accessed | tf_op | source)
XLA Modules:
  0.0 449.3 jit_solution(14379024143992751733)
XLA Ops:
  5.2 11.7 %all-to-all-start = ((bf16[128,64,128]{2,1,0:T(8,128)(2,1)}), bf16[128,64,128]{2,1,0:T(8,128)(2,1)}, u32[]{:S(2)}, u32[]{:S(2)}) async-start(bf16[128,64,128]{2,1,0:T(8,128)(2,1)} %get-tuple-element.24), calls=%async_computation | async-start | bytes 4194304 | tf_op jit(solution)/shard_map/all_to_all | solution.py:257
  19.8 2.8 shard_map.87.tiles_ref
  24.7 3.2 shard_map.88.part_ref
  28.8 18.1 %all-to-all-done.arrived_ref = bf16[128,64,128]{2,1,0:T(8,128)(2,1)} async-done(((bf16[128,64,128]{2,1,0:T(8,128)(2,1)}), bf16[128,64,128]{2,1,0:T(8,128)(2,1)}, u32[]{:S(2)}, u32[]{:S(2)}) %all-to-all-start) | async-done | bytes 2097184 | tf_op jit(solution)/shard_map/all_to_all | solution.py:257
  46.9 6.8 %shard_map.89 = (bf16[32,64,128]{2,1,0:T(8,128)(2,1)}, bf16[128,64,128]{2,1,0:T(8,128)(2,1)}) custom-call(s32[128]{0:T(128)S(1)} %bitcast.8, bf16[128,64,128]{2,1,0:T(8,128)(2,1)} %all-to-all-done.arrived_ref, bf16[128,128,128]{2,1,0:T(8,128)(2,1)} %copy-done.8, f32[32,64,128]{2,1,0:T(8,128)} %copy-done.21), custom_call_target="tpu_custom_call" | custom-call | flops 268435456 | bytes 10485760 | tf_op jit(solution)/shard_map/pallas_call | solution.py:24
  53.7 4.7 %all-to-all-start.1 = ((bf16[128,64,128]{2,1,0:T(8,128)(2,1)}), bf16[128,64,128]{2,1,0:T(8,128)(2,1)S(1)}, u32[]{:S(2)}, u32[]{:S(2)}) async-start(bf16[128,64,128]{2,1,0:T(8,128)(2,1)} %get-tuple-element.26), calls=%async_computation.1 | async-start | bytes 4194304 | tf_op jit(solution)/shard_map/all_to_all | solution.py:257
  58.4 2.8 copy-done
  63.2 3.2 shard_map.90.part_ref
  67.4 21.4 %all-to-all-done.1.arrived_ref = bf16[128,64,128]{2,1,0:T(8,128)(2,1)S(1)} async-done(((bf16[128,64,128]{2,1,0:T(8,128)(2,1)}), bf16[128,64,128]{2,1,0:T(8,128)(2,1)S(1)}, u32[]{:S(2)}, u32[]{:S(2)}) %all-to-all-start.1) | async-done | bytes 2097184 | tf_op jit(solution)/shard_map/all_to_all | solution.py:257
  88.8 5.7 %shard_map.91 = (bf16[32,64,128]{2,1,0:T(8,128)(2,1)}, bf16[128,64,128]{2,1,0:T(8,128)(2,1)}) custom-call(s32[128]{0:T(128)S(1)} %bitcast.9, bf16[128,64,128]{2,1,0:T(8,128)(2,1)S(1)} %all-to-all-done.1.arrived_ref, bf16[128,128,128]{2,1,0:T(8,128)(2,1)} %copy-done.8, f32[32,64,128]{2,1,0:T(8,128)} %copy-done.17), custom_call_target="tpu_custom_call" | custom-call | flops 268435456 | bytes 10485760 | tf_op jit(solution)/shard_map/pallas_call | solution.py:24
  94.6 4.7 %all-to-all-start.2 = ((bf16[128,64,128]{2,1,0:T(8,128)(2,1)}), bf16[128,64,128]{2,1,0:T(8,128)(2,1)S(1)}, u32[]{:S(2)}, u32[]{:S(2)}) async-start(bf16[128,64,128]{2,1,0:T(8,128)(2,1)} %get-tuple-element.28), calls=%async_computation.2 | async-start | bytes 4194304 | tf_op jit(solution)/shard_map/all_to_all | solution.py:257
  99.2 2.8 copy-done.1
  104.1 3.2 shard_map.92.part_ref
  108.3 21.4 %all-to-all-done.2.arrived_ref = bf16[128,64,128]{2,1,0:T(8,128)(2,1)S(1)} async-done(((bf16[128,64,128]{2,1,0:T(8,128)(2,1)}), bf16[128,64,128]{2,1,0:T(8,128)(2,1)S(1)}, u32[]{:S(2)}, u32[]{:S(2)}) %all-to-all-start.2) | async-done | bytes 2097184 | tf_op jit(solution)/shard_map/all_to_all | solution.py:257
  129.7 5.7 %shard_map.93 = (bf16[32,64,128]{2,1,0:T(8,128)(2,1)}, bf16[128,64,128]{2,1,0:T(8,128)(2,1)}) custom-call(s32[128]{0:T(128)S(1)} %bitcast.10, bf16[128,64,128]{2,1,0:T(8,128)(2,1)S(1)} %all-to-all-done.2.arrived_ref, bf16[128,128,128]{2,1,0:T(8,128)(2,1)} %copy-done.8, f32[32,64,128]{2,1,0:T(8,128)} %copy-done.18), custom_call_target="tpu_custom_call" | custom-call | flops 268435456 | bytes 10485760 | tf_op jit(solution)/shard_map/pallas_call | solution.py:24
  135.4 4.7 %all-to-all-start.3 = ((bf16[128,64,128]{2,1,0:T(8,128)(2,1)}), bf16[128,64,128]{2,1,0:T(8,128)(2,1)S(1)}, u32[]{:S(2)}, u32[]{:S(2)}) async-start(bf16[128,64,128]{2,1,0:T(8,128)(2,1)} %get-tuple-element.30), calls=%async_computation.3 | async-start | bytes 4194304 | tf_op jit(solution)/shard_map/all_to_all | solution.py:257
  145.0 3.2 shard_map.94.part_ref
  149.1 21.4 %all-to-all-done.3.arrived_ref = bf16[128,64,128]{2,1,0:T(8,128)(2,1)S(1)} async-done(((bf16[128,64,128]{2,1,0:T(8,128)(2,1)}), bf16[128,64,128]{2,1,0:T(8,128)(2,1)S(1)}, u32[]{:S(2)}, u32[]{:S(2)}) %all-to-all-start.3) | async-done | bytes 2097184 | tf_op jit(solution)/shard_map/all_to_all | solution.py:257
  170.5 5.8 %shard_map.95 = (bf16[32,64,128]{2,1,0:T(8,128)(2,1)}, bf16[128,64,128]{2,1,0:T(8,128)(2,1)}) custom-call(s32[128]{0:T(128)S(1)} %bitcast.11, bf16[128,64,128]{2,1,0:T(8,128)(2,1)S(1)} %all-to-all-done.3.arrived_ref, bf16[128,128,128]{2,1,0:T(8,128)(2,1)} %copy-done.8, f32[32,64,128]{2,1,0:T(8,128)} %copy-done.15), custom_call_target="tpu_custom_call" | custom-call | flops 268435456 | bytes 10485760 | tf_op jit(solution)/shard_map/pallas_call | solution.py:24
  176.3 5.9 %all-to-all-start.4 = ((bf16[128,64,128]{2,1,0:T(8,128)(2,1)}), bf16[128,64,128]{2,1,0:T(8,128)(2,1)}, u32[]{:S(2)}, u32[]{:S(2)}) async-start(bf16[128,64,128]{2,1,0:T(8,128)(2,1)} %get-tuple-element.32), calls=%async_computation.4 | async-start | bytes 4194304 | tf_op jit(solution)/shard_map/all_to_all | solution.py:257
  182.7 2.8 copy-done.3
  185.5 3.3 shard_map.96.part_ref
  189.8 22.5 %all-to-all-done.4.arrived_ref = bf16[128,64,128]{2,1,0:T(8,128)(2,1)} async-done(((bf16[128,64,128]{2,1,0:T(8,128)(2,1)}), bf16[128,64,128]{2,1,0:T(8,128)(2,1)}, u32[]{:S(2)}, u32[]{:S(2)}) %all-to-all-start.4) | async-done | bytes 2097184 | tf_op jit(solution)/shard_map/all_to_all | solution.py:257
  212.3 7.8 %shard_map.98 = (f32[32,64,128]{2,1,0:T(8,128)}, f32[64,128]{1,0:T(8,128)S(1)}) custom-call(s32[128]{0:T(128)S(1)} %bitcast.12, bf16[128,64,128]{2,1,0:T(8,128)(2,1)} %all-to-all-done.4.arrived_ref, bf16[128,128,128]{2,1,0:T(8,128)(2,1)} %copy-done.8, f32[32,64,128]{2,1,0:T(8,128)} %copy-done.13, bf16[32,64,128]{2,1,0:T(8,128)(2,1)} %get-tuple-element.33.refs_0_.cur_ref, ...), custom_call_target="tpu_custom_call" | custom-call | flops 268435456 | bytes 10485760 | tf_op jit(solution)/shard_map/pallas_call | solution.py:24
  220.1 9.9 %all_to_all.65 = f32[8,64,128]{2,1,0:T(8,128)S(1)} all-to-all(f32[8,64,128]{2,1,0:T(8,128)S(1)} %broadcast_in_dim.8), channel_id=1, replica_groups={{0,1,2,3,4,5,6,7},{8,9,10,11,12,13,14,15},{16,17,18,19,20,21,22,23},{24..., dimensions={0} | all-to-all | bytes 524288 | tf_op jit(solution)/shard_map/all_to_all | solution.py:279
  230.1 14.1 %all_to_all.66 = f32[16,64,128]{2,1,0:T(8,128)S(1)} all-to-all(f32[16,64,128]{2,1,0:T(8,128)S(1)} %broadcast_in_dim.9), channel_id=1, replica_groups={{0,8,16,24,32,40,48,56,64,72,80,88,96,104,112,120},{1,9,17,25,33,41,49,..., dimensions={0} | all-to-all | bytes 1048576 | tf_op jit(solution)/shard_map/all_to_all | solution.py:279
  244.2 8.5 %shard_map.99 = (bf16[32,64,128]{2,1,0:T(8,128)(2,1)}, bf16[32,64,128]{2,1,0:T(8,128)(2,1)}, bf16[128,64,128]{2,1,0:T(8,128)(2,1)}, f32[1,1]{1,0:T(1,128)}) custom-call(s32[128]{0:T(128)S(1)} %bitcast.13, f32[64,128]{1,0:T(8,128)S(1)} %reduce_sum.37.sums_ref, bf16[32,64,128]{2,1,0:T(8,128)(2,1)} %get-tuple-element.33.refs_0_.cur_ref, ...), custom_call_target="tpu_custom_call" | custom-call | flops 16777216 | bytes 4194304 | tf_op jit(solution)/shard_map/pallas_call | solution.py:24
  252.7 4.7 %all-to-all-start.7 = ((bf16[128,64,128]{2,1,0:T(8,128)(2,1)}), bf16[128,64,128]{2,1,0:T(8,128)(2,1)S(1)}, u32[]{:S(2)}, u32[]{:S(2)}) async-start(bf16[128,64,128]{2,1,0:T(8,128)(2,1)} %get-tuple-element.36), calls=%async_computation.7 | async-start | bytes 4194304 | tf_op jit(solution)/shard_map/all_to_all | solution.py:257
  257.4 2.8 copy-done.4
  262.3 3.8 shard_map.100.part_ref
  267.1 20.8 %all-to-all-done.7.arrived_ref = bf16[128,64,128]{2,1,0:T(8,128)(2,1)S(1)} async-done(((bf16[128,64,128]{2,1,0:T(8,128)(2,1)}), bf16[128,64,128]{2,1,0:T(8,128)(2,1)S(1)}, u32[]{:S(2)}, u32[]{:S(2)}) %all-to-all-start.7) | async-done | bytes 2097184 | tf_op jit(solution)/shard_map/all_to_all | solution.py:257
  287.9 5.7 %shard_map.101 = (bf16[32,64,128]{2,1,0:T(8,128)(2,1)}, bf16[128,64,128]{2,1,0:T(8,128)(2,1)}) custom-call(s32[128]{0:T(128)S(1)} %bitcast.14, bf16[128,64,128]{2,1,0:T(8,128)(2,1)S(1)} %all-to-all-done.7.arrived_ref, bf16[128,128,128]{2,1,0:T(8,128)(2,1)} %copy-done.8, f32[32,64,128]{2,1,0:T(8,128)} %copy-done.19), custom_call_target="tpu_custom_call" | custom-call | flops 268435456 | bytes 10485760 | tf_op jit(solution)/shard_map/pallas_call | solution.py:24
  293.6 4.7 %all-to-all-start.8 = ((bf16[128,64,128]{2,1,0:T(8,128)(2,1)}), bf16[128,64,128]{2,1,0:T(8,128)(2,1)S(1)}, u32[]{:S(2)}, u32[]{:S(2)}) async-start(bf16[128,64,128]{2,1,0:T(8,128)(2,1)} %get-tuple-element.40), calls=%async_computation.8 | async-start | bytes 4194304 | tf_op jit(solution)/shard_map/all_to_all | solution.py:257
  303.1 3.8 shard_map.102.part_ref
  307.9 20.8 %all-to-all-done.8.arrived_ref = bf16[128,64,128]{2,1,0:T(8,128)(2,1)S(1)} async-done(((bf16[128,64,128]{2,1,0:T(8,128)(2,1)}), bf16[128,64,128]{2,1,0:T(8,128)(2,1)S(1)}, u32[]{:S(2)}, u32[]{:S(2)}) %all-to-all-start.8) | async-done | bytes 2097184 | tf_op jit(solution)/shard_map/all_to_all | solution.py:257
  328.7 5.7 %shard_map.103 = (bf16[32,64,128]{2,1,0:T(8,128)(2,1)}, bf16[128,64,128]{2,1,0:T(8,128)(2,1)}) custom-call(s32[128]{0:T(128)S(1)} %bitcast.15, bf16[128,64,128]{2,1,0:T(8,128)(2,1)S(1)} %all-to-all-done.8.arrived_ref, bf16[128,128,128]{2,1,0:T(8,128)(2,1)} %copy-done.8, f32[32,64,128]{2,1,0:T(8,128)} %copy-done.20), custom_call_target="tpu_custom_call" | custom-call | flops 268435456 | bytes 10485760 | tf_op jit(solution)/shard_map/pallas_call | solution.py:24
  334.4 4.7 %all-to-all-start.9 = ((bf16[128,64,128]{2,1,0:T(8,128)(2,1)}), bf16[128,64,128]{2,1,0:T(8,128)(2,1)S(1)}, u32[]{:S(2)}, u32[]{:S(2)}) async-start(bf16[128,64,128]{2,1,0:T(8,128)(2,1)} %get-tuple-element.42), calls=%async_computation.9 | async-start | bytes 4194304 | tf_op jit(solution)/shard_map/all_to_all | solution.py:257
  344.0 4.0 shard_map.104.part_ref
  349.0 20.5 %all-to-all-done.9.arrived_ref = bf16[128,64,128]{2,1,0:T(8,128)(2,1)S(1)} async-done(((bf16[128,64,128]{2,1,0:T(8,128)(2,1)}), bf16[128,64,128]{2,1,0:T(8,128)(2,1)S(1)}, u32[]{:S(2)}, u32[]{:S(2)}) %all-to-all-start.9) | async-done | bytes 2097184 | tf_op jit(solution)/shard_map/all_to_all | solution.py:257
  369.6 5.8 %shard_map.105 = (bf16[32,64,128]{2,1,0:T(8,128)(2,1)}, bf16[128,64,128]{2,1,0:T(8,128)(2,1)}) custom-call(s32[128]{0:T(128)S(1)} %bitcast.16, bf16[128,64,128]{2,1,0:T(8,128)(2,1)S(1)} %all-to-all-done.9.arrived_ref, bf16[128,128,128]{2,1,0:T(8,128)(2,1)} %copy-done.8, f32[32,64,128]{2,1,0:T(8,128)} %copy-done.16), custom_call_target="tpu_custom_call" | custom-call | flops 268435456 | bytes 10485760 | tf_op jit(solution)/shard_map/pallas_call | solution.py:24
  375.3 5.9 %all-to-all-start.10 = ((bf16[128,64,128]{2,1,0:T(8,128)(2,1)}), bf16[128,64,128]{2,1,0:T(8,128)(2,1)}, u32[]{:S(2)}, u32[]{:S(2)}) async-start(bf16[128,64,128]{2,1,0:T(8,128)(2,1)} %get-tuple-element.44), calls=%async_computation.10 | async-start | bytes 4194304 | tf_op jit(solution)/shard_map/all_to_all | solution.py:257
  381.7 2.8 copy-done.7
  384.5 3.1 shard_map.106.part_ref
  388.6 22.7 %all-to-all-done.10.arrived_ref = bf16[128,64,128]{2,1,0:T(8,128)(2,1)} async-done(((bf16[128,64,128]{2,1,0:T(8,128)(2,1)}), bf16[128,64,128]{2,1,0:T(8,128)(2,1)}, u32[]{:S(2)}, u32[]{:S(2)}) %all-to-all-start.10) | async-done | bytes 2097184 | tf_op jit(solution)/shard_map/all_to_all | solution.py:257
  411.3 7.8 %shard_map.108 = f32[64,128]{1,0:T(8,128)S(1)} custom-call(s32[128]{0:T(128)S(1)} %bitcast.17, bf16[128,64,128]{2,1,0:T(8,128)(2,1)} %all-to-all-done.10.arrived_ref, bf16[128,128,128]{2,1,0:T(8,128)(2,1)} %copy-done.8, f32[32,64,128]{2,1,0:T(8,128)} %copy-done.12, bf16[32,64,128]{2,1,0:T(8,128)(2,1)} %get-tuple-element.45.refs_0_.cur_ref, ...), custom_call_target="tpu_custom_call" | custom-call | flops 268435456 | bytes 10485760 | tf_op jit(solution)/shard_map/pallas_call | solution.py:24
  419.1 9.9 %all_to_all.67 = f32[8,64,128]{2,1,0:T(8,128)S(1)} all-to-all(f32[8,64,128]{2,1,0:T(8,128)S(1)} %broadcast_in_dim.10), channel_id=1, replica_groups={{0,1,2,3,4,5,6,7},{8,9,10,11,12,13,14,15},{16,17,18,19,20,21,22,23},{24..., dimensions={0} | all-to-all | bytes 524288 | tf_op jit(solution)/shard_map/all_to_all | solution.py:279
  429.1 14.1 %all_to_all.68 = f32[16,64,128]{2,1,0:T(8,128)S(1)} all-to-all(f32[16,64,128]{2,1,0:T(8,128)S(1)} %broadcast_in_dim.11), channel_id=1, replica_groups={{0,8,16,24,32,40,48,56,64,72,80,88,96,104,112,120},{1,9,17,25,33,41,49,..., dimensions={0} | all-to-all | bytes 1048576 | tf_op jit(solution)/shard_map/all_to_all | solution.py:279
  443.2 5.9 %shard_map.109 = (bf16[64,4096]{1,0:T(8,128)(2,1)}, f32[64,64]{1,0:T(8,128)}) custom-call(f32[64,128]{1,0:T(8,128)S(1)} %reduce_sum.39.sums_ref, bf16[32,64,128]{2,1,0:T(8,128)(2,1)} %get-tuple-element.45.refs_0_.cur_ref), custom_call_target="tpu_custom_call" | custom-call | flops 16777216 | bytes 2097152 | tf_op jit(solution)/shard_map/pallas_call | solution.py:24
  (92 shorter events, 39.3 us)
Async XLA Ops:
  0.6 1.0 copy-start.36
  5.2 19.4 %slice-start = ((s8[6291456]{0:T(1024)(128)(4,1)}), s8[2097152]{0:T(1024)(128)(4,1)S(1)}, s32[]{:S(2)}) async-start(s8[6291456]{0:T(1024)(128)(4,1)} %bitcast.5), calls=%async_computation.13 | async-start | bytes 4194304
  5.2 41.7 %all-to-all-start = ((bf16[128,64,128]{2,1,0:T(8,128)(2,1)}), bf16[128,64,128]{2,1,0:T(8,128)(2,1)}, u32[]{:S(2)}, u32[]{:S(2)}) async-start(bf16[128,64,128]{2,1,0:T(8,128)(2,1)} %get-tuple-element.24), calls=%async_computation | async-start | bytes 4194304 | tf_op jit(solution)/shard_map/all_to_all | solution.py:257
  17.6 2.2 copy-start.14
  19.8 4.8 %copy-start.39 = (s32[1,96,2]{1,2,0:T(2,128)S(1)}, s32[1,96,2]{1,2,0:T(2,128)}, u32[]{:S(2)}) copy-start(s32[1,96,2]{1,2,0:T(2,128)} %param.12) | copy-start | bytes 2308
  19.8 4.8 %slice-start.1 = ((s8[6291456]{0:T(1024)(128)(4,1)}), s8[4194304]{0:T(1024)(128)(4,1)S(1)}, s32[]{:S(2)}) async-start(s8[6291456]{0:T(1024)(128)(4,1)} %bitcast.5), calls=%async_computation.14 | async-start | bytes 8388608
  19.8 4.8 %copy-start.9 = (bf16[32,128,128]{2,1,0:T(8,128)(2,1)S(1)}, bf16[32,128,128]{2,1,0:T(8,128)(2,1)}, u32[]{:S(2)}) copy-start(bf16[32,128,128]{2,1,0:T(8,128)(2,1)} %refs_1_.5) | copy-start | bytes 3145732
  19.8 4.8 %copy-start.23 = (bf16[32,64,128]{2,1,0:T(8,128)(2,1)S(1)}, bf16[32,64,128]{2,1,0:T(8,128)(2,1)}, u32[]{:S(2)}) copy-start(bf16[32,64,128]{2,1,0:T(8,128)(2,1)} %copy-done.22) | copy-start | bytes 1572868
  22.6 2.0 copy-start.8
  24.6 22.3 %copy-start.38 = (s32[1,128]{1,0:T(1,128)S(1)}, s32[1,128]{1,0:T(1,128)}, u32[]{:S(2)}) copy-start(s32[1,128]{1,0:T(1,128)} %param.11) | copy-start | bytes 1540
  27.8 1.0 copy-start.21
  53.7 35.1 %all-to-all-start.1 = ((bf16[128,64,128]{2,1,0:T(8,128)(2,1)}), bf16[128,64,128]{2,1,0:T(8,128)(2,1)S(1)}, u32[]{:S(2)}, u32[]{:S(2)}) async-start(bf16[128,64,128]{2,1,0:T(8,128)(2,1)} %get-tuple-element.26), calls=%async_computation.1 | async-start | bytes 4194304 | tf_op jit(solution)/shard_map/all_to_all | solution.py:257
  58.4 2.8 copy-start
  61.2 1.0 copy-start.24
  62.2 1.0 copy-start.31
  66.4 1.0 copy-start.17
  94.6 35.1 %all-to-all-start.2 = ((bf16[128,64,128]{2,1,0:T(8,128)(2,1)}), bf16[128,64,128]{2,1,0:T(8,128)(2,1)S(1)}, u32[]{:S(2)}, u32[]{:S(2)}) async-start(bf16[128,64,128]{2,1,0:T(8,128)(2,1)} %get-tuple-element.28), calls=%async_computation.2 | async-start | bytes 4194304 | tf_op jit(solution)/shard_map/all_to_all | solution.py:257
  99.2 2.8 copy-start.1
  102.0 1.0 copy-start.27
  103.1 1.0 copy-start.32
  107.3 1.0 copy-start.18
  135.4 35.1 %all-to-all-start.3 = ((bf16[128,64,128]{2,1,0:T(8,128)(2,1)}), bf16[128,64,128]{2,1,0:T(8,128)(2,1)S(1)}, u32[]{:S(2)}, u32[]{:S(2)}) async-start(bf16[128,64,128]{2,1,0:T(8,128)(2,1)} %get-tuple-element.30), calls=%async_computation.3 | async-start | bytes 4194304 | tf_op jit(solution)/shard_map/all_to_all | solution.py:257
  140.1 2.8 copy-start.2
  142.9 1.0 copy-start.28
  143.9 1.0 copy-start.34
  148.1 1.0 copy-start.15
  176.3 5.9 %copy-start.10 = (bf16[32,64,128]{2,1,0:T(8,128)(2,1)S(1)}, bf16[32,64,128]{2,1,0:T(8,128)(2,1)}, u32[]{:S(2)}) copy-start(bf16[32,64,128]{2,1,0:T(8,128)(2,1)} %get-tuple-element.33.refs_0_.cur_ref) | copy-start | bytes 1572868
  176.3 35.9 %all-to-all-start.4 = ((bf16[128,64,128]{2,1,0:T(8,128)(2,1)}), bf16[128,64,128]{2,1,0:T(8,128)(2,1)}, u32[]{:S(2)}, u32[]{:S(2)}) async-start(bf16[128,64,128]{2,1,0:T(8,128)(2,1)} %get-tuple-element.32), calls=%async_computation.4 | async-start | bytes 4194304 | tf_op jit(solution)/shard_map/all_to_all | solution.py:257
  182.7 2.8 copy-start.3
  188.8 1.0 copy-start.13
  252.7 35.1 %all-to-all-start.7 = ((bf16[128,64,128]{2,1,0:T(8,128)(2,1)}), bf16[128,64,128]{2,1,0:T(8,128)(2,1)S(1)}, u32[]{:S(2)}, u32[]{:S(2)}) async-start(bf16[128,64,128]{2,1,0:T(8,128)(2,1)} %get-tuple-element.36), calls=%async_computation.7 | async-start | bytes 4194304 | tf_op jit(solution)/shard_map/all_to_all | solution.py:257
  257.4 2.8 copy-start.4
  260.2 1.0 copy-start.25
  261.3 1.0 copy-start.33
  266.1 1.0 copy-start.19
  293.6 35.1 %all-to-all-start.8 = ((bf16[128,64,128]{2,1,0:T(8,128)(2,1)}), bf16[128,64,128]{2,1,0:T(8,128)(2,1)S(1)}, u32[]{:S(2)}, u32[]{:S(2)}) async-start(bf16[128,64,128]{2,1,0:T(8,128)(2,1)} %get-tuple-element.40), calls=%async_computation.8 | async-start | bytes 4194304 | tf_op jit(solution)/shard_map/all_to_all | solution.py:257
  298.3 2.8 copy-start.5
  301.1 1.0 copy-start.26
  302.1 1.0 copy-start.29
  307.0 1.0 copy-start.20
  334.4 35.1 %all-to-all-start.9 = ((bf16[128,64,128]{2,1,0:T(8,128)(2,1)}), bf16[128,64,128]{2,1,0:T(8,128)(2,1)S(1)}, u32[]{:S(2)}, u32[]{:S(2)}) async-start(bf16[128,64,128]{2,1,0:T(8,128)(2,1)} %get-tuple-element.42), calls=%async_computation.9 | async-start | bytes 4194304 | tf_op jit(solution)/shard_map/all_to_all | solution.py:257
  339.1 2.8 copy-start.6
  341.9 1.0 copy-start.30
  343.0 1.0 copy-start.35
  348.0 1.0 copy-start.16
  375.3 5.9 %copy-start.11 = (bf16[32,64,128]{2,1,0:T(8,128)(2,1)S(1)}, bf16[32,64,128]{2,1,0:T(8,128)(2,1)}, u32[]{:S(2)}) copy-start(bf16[32,64,128]{2,1,0:T(8,128)(2,1)} %get-tuple-element.45.refs_0_.cur_ref) | copy-start | bytes 1572868
  375.3 35.9 %all-to-all-start.10 = ((bf16[128,64,128]{2,1,0:T(8,128)(2,1)}), bf16[128,64,128]{2,1,0:T(8,128)(2,1)}, u32[]{:S(2)}, u32[]{:S(2)}) async-start(bf16[128,64,128]{2,1,0:T(8,128)(2,1)} %get-tuple-element.44), calls=%async_computation.10 | async-start | bytes 4194304 | tf_op jit(solution)/shard_map/all_to_all | solution.py:257
  381.7 2.8 copy-start.7
  (3 other events, 2.4 us)

commit v3 on v2

--- a/solution.py
+++ b/solution.py
@@ -85,7 +85,7 @@
         centre_ref, cur_ref, diag_ref, pair_ref, prev_ref, acc_ref = refs
         centre = centre_ref[0, 0]
     else:
-        cur_ref, diag_ref, pair_ref, acc_ref = refs
+        cur_ref, diag_ref, pair_ref, acc_ref = refs[0], refs[1], refs[2], refs[-1]
         centre = FIRST_CENTRE
 
     def own(r, _):
@@ -150,11 +150,20 @@
     gram_ref[...] = value
 
 
-def sums_kernel(keep, rows_ref, arrived_ref, tiles_ref, part_ref, cur_ref, gram_ref, *refs):
-    if keep:
-        image_ref, sums_ref, tiles, acc, halo, cur, sems = refs
+def product_kernel(cur_ref, image_ref, sum_ref):
+    value = jnp.zeros(sum_ref.shape, F32)
+    for r in range(cur_ref.shape[0]):
+        for third in thirds(image_ref[r]):
+            value = value + mm_t(cur_ref[r], third)
+    sum_ref[...] = value
+
+
+def image_kernel(last, rows_ref, arrived_ref, tiles_ref, part_ref, cur_ref, gram_ref, *refs):
+    del gram_ref
+    if last:
+        sum_ref, tiles, acc, halo, cur, sems = refs
     else:
-        sums_ref, tiles, acc, halo, cur, sems = refs
+        image_ref, z_ref, out_ref, tiles, acc, halo, cur, block, slots, sems = refs
     coming = begin(tiles_ref, tiles, sems.at[0])
     also = begin(part_ref, acc, sems.at[1])
     more = begin(cur_ref, cur, sems.at[2])
@@ -163,18 +172,15 @@
     halo_sums(rows_ref, arrived_ref, tiles, halo)
     also.wait()
     acc[...] += halo[...]
-    if keep:
-        going = begin(acc, image_ref, sems.at[0])
     more.wait()
-    k = gram_ref.shape[0]
-    value = jnp.zeros((k, k), F32)
-    for r in range(acc.shape[0]):
-        block = cur[r]
-        for third in thirds(acc[r]):
-            value = value + mm_t(block, third)
-    sums_ref[...] = jnp.concatenate([gram_ref[...], value], axis=1)
-    if keep:
-        going.wait()
+    if last:
+        product_kernel(cur, acc, sum_ref)
+    else:
+        block[...] = (acc[...] - FIRST_CENTRE * cur[...].astype(F32)).astype(BF16)
+        going = [begin(acc, image_ref, sems.at[2]), begin(block, z_ref, sems.at[3])]
+        going += spread(rows_ref, block, slots, out_ref, sems)
+        for copy in going:
+            copy.wait()
 
 
 def inverse_factor(gram):
@@ -202,38 +208,57 @@
     return mm(parts[0], block) + (mm(parts[1], block) + mm(parts[2], block))
 
 
-def turn_kernel(total, rows_ref, sums_ref, cur_ref, image_ref, next_ref, y_ref, out_ref, centre_ref, cur, image, start, block, slots, sems):
-    coming = begin(cur_ref, cur, sems.at[0])
-    also = begin(image_ref, image, sems.at[1])
-    k = sums_ref.shape[0]
-    inverse = inverse_factor(sums_ref[:, :k] / total)
-    half = jnp.dot(inverse, sums_ref[:, k:] / total, precision=HI, preferred_element_type=F32)
-    centre = jnp.sum(half * inverse) / k - 1.0
+def factor_kernel(total, flat, gram_ref, cur_ref, inverse_ref, next_ref):
+    width = cur_ref.shape[2]
+    inverse = inverse_factor(gram_ref[...] / total)
+    inverse_ref[...] = inverse
+    parts = thirds(inverse)
+    for r in range(cur_ref.shape[0]):
+        block = apply_square(parts, cur_ref[r]).astype(BF16)
+        if flat:
+            next_ref[:, r * width : (r + 1) * width] = block
+        else:
+            next_ref[r] = block
+
+
+def turn_kernel(total, rows_ref, arrived_ref, tiles_ref, part_ref, image_ref, z_ref, cur_ref, next_ref, inverse_ref, sum_ref, *refs):
+    y_ref, out_ref, centre_ref, tiles, acc, part, image, z, cur, begun, block, slots, sems, late = refs
+    coming = begin(tiles_ref, tiles, sems.at[0])
+    also = [
+        begin(source, target, late.at[i])
+        for i, (source, target) in enumerate(((part_ref, part), (image_ref, image), (z_ref, z), (cur_ref, cur), (next_ref, begun)))
+    ]
+    acc[...] = jnp.zeros(acc.shape, F32)
+    inverse = inverse_ref[...]
+    half = jnp.dot(inverse, sum_ref[...] / total, precision=HI, preferred_element_type=F32)
+    centre = jnp.sum(half * inverse) / inverse.shape[0] - 1.0
+    change = centre - FIRST_CENTRE
     centre_ref[0, 0] = centre
-    parts = thirds(inverse)
     coming.wait()
-    also.wait()
+    halo_sums(rows_ref, arrived_ref, tiles, acc)
+    for copy in also:
+        copy.wait()
     for r in range(cur.shape[0]):
-        begun = apply_square(parts, cur[r]).astype(BF16)
-        start[r] = begun
-        turned = jnp.dot(inverse, image[r], precision=HI, preferred_element_type=F32)
-        block[r] = (turned - centre * begun.astype(F32)).astype(BF16)
-    going = [begin(start, next_ref, sems.at[2]), begin(block, y_ref, sems.at[3])]
+        value = acc[r] + part[r] - change * image[r] - centre * (z[r].astype(F32) - change * cur[r].astype(F32))
+        turned = jnp.dot(inverse, 2.0 * value, precision=HI, preferred_element_type=F32)
+        block[r] = (turned - begun[r].astype(F32)).astype(BF16)
+    going = [begin(block, y_ref, sems.at[2])]
     going += spread(rows_ref, block, slots, out_ref, sems)
     for copy in going:
         copy.wait()
 
 
-def end_kernel(total, sums_ref, cur_ref, basis_ref, ritz_ref, cur, sems):
-    coming = begin(cur_ref, cur, sems.at[0])
-    k, width = sums_ref.shape[0], cur.shape[2]
-    inverse = inverse_factor(sums_ref[:, :k] / total)
-    half = jnp.dot(inverse, sums_ref[:, k:] / total, precision=HI, preferred_element_type=F32)
+def first_kernel(centre_ref, z_ref, cur_ref, inverse_ref, y_ref):
+    change = centre_ref[0, 0] - FIRST_CENTRE
+    for r in range(cur_ref.shape[0]):
+        value = z_ref[r].astype(F32) - change * cur_ref[r].astype(F32)
+        y_ref[r] = jnp.dot(inverse_ref[...], value, precision=HI, preferred_element_type=F32).astype(BF16)
+
+
+def ritz_kernel(total, inverse_ref, sum_ref, ritz_ref):
+    inverse = inverse_ref[...]
+    half = jnp.dot(inverse, sum_ref[...] / total, precision=HI, preferred_element_type=F32)
     ritz_ref[...] = mm_t(half, inverse, HI)
-    parts = thirds(inverse)
-    coming.wait()
-    for r in range(cur.shape[0]):
-        basis_ref[:, r * width : (r + 1) * width] = apply_square(parts, cur[r]).astype(BF16)
 
 
 def local(vectors, diag_tiles, pair_tiles, halo_tiles, halo_rows, pair_index, pair_count):
@@ -279,18 +304,36 @@
             x = jnp.sum(lax.all_to_all(many, "dom", 0, 0, axis_index_groups=groups, tiled=True), axis=0)
         return x
 
-    def sums(cur, arrived, part, keep):
-        [gram] = call(gram_kernel, [(square, F32, "h")], [(cur, "h")], 2 * k * k * own_rows, 1 << 20)
-        outs = [(block, F32, "a")] * keep + [((k, 2 * k), F32, "h")]
-        ins = [(rows, "s"), (arrived, "v"), (tiles, "a"), (part, "a"), (cur, "a"), (gram, "h")]
-        scratch = [room(tiles.shape, BF16), room(block, F32), room(block, F32), room(block, BF16), sems]
-        *image, value = call(functools.partial(sums_kernel, keep), outs, ins, unit * peers, 10 << 20, scratch)
-        return *image, everywhere(value)
-
-    def filtered(prev, cur, out, centre):
-        for _ in range(3):
+    def other(x, step):
+        return lax.ppermute(x, "dom", [(i, i ^ step) for i in range(peers)])
+
+    def beside(x, work):
+        x = x + other(x, 1)
+        result = work(x)
+        for step in (2, 8, 32):
+            x = (x + other(x, step)) + (other(x, 2 * step) + other(x, 3 * step))
+        return x, result
+
+    def gram(cur):
+        [value] = call(gram_kernel, [(square, F32, "h")], [(cur, "h")], 2 * k * k * own_rows, 1 << 20)
+        return value
+
+    def factor(value, cur, flat):
+        outs = [(square, F32, "h"), (((k, own_rows) if flat else block), BF16, "h")]
+        return call(functools.partial(factor_kernel, total, flat), outs, [(value, "h"), (cur, "h")], 1 << 24, 2 << 20)
+
+    def image(cur, arrived, part, value, last):
+        outs = [(square, F32, "h")] if last else [(block, F32, "a"), (block, BF16, "a"), (spots, BF16, "a")]
+        ins = [(rows, "s"), (arrived, "v"), (tiles, "a"), (part, "a"), (cur, "a"), (value, "a")]
+        scratch = [room(tiles.shape, BF16), room(block, F32), room(block, F32), room(block, BF16)]
+        if not last:
+            scratch += [room(block, BF16), room(spots, BF16)]
+        return call(functools.partial(image_kernel, last), outs, ins, unit * peers, 10 << 20, [*scratch, sems])
+
+    def filtered(prev, cur, out, centre, steps):
+        for _ in range(steps):
             arrived = exchange(out)
-            part = own("filter", cur, [(prev, "h")], [(centre, "s")])
+            part = own("filter", cur, [(prev() if callable(prev) else prev, "h")], [(centre, "s")])
             prev, (cur, out) = cur, halo(2.0, arrived, part)
         return cur, out
 
@@ -304,30 +347,41 @@
     )
     arrived = exchange(out)
     cur, out = halo(1.0, arrived, own("start", start))
-    cur, out = filtered(start, cur, out, jnp.full((1, 1), FIRST_CENTRE, F32))
+    cur, out = filtered(start, cur, out, jnp.full((1, 1), FIRST_CENTRE, F32), 3)
 
     arrived = exchange(out)
-    image, value = sums(cur, arrived, own("image", cur), 1)
-    begun, cur, out, centre = call(
+    value, part = beside(gram(cur), lambda x: own("image", cur, [(x, "a")]))
+    full, z, out = image(cur, arrived, part, value, False)
+
+    arrived = exchange(out)
+    inverse, begun = factor(value, cur, False)
+    [value] = call(product_kernel, [(square, F32, "h")], [(cur, "h"), (full, "h")], 6 * k * k * own_rows, 2 << 20)
+    value, part = beside(value, lambda x: own("image", z, [(x, "a")]))
+    wide = [room(block, F32)] * 3 + [room(block, BF16)] * 4
+    y, out, centre = call(
         functools.partial(turn_kernel, total),
-        [(block, BF16, "a"), (block, BF16, "a"), (spots, BF16, "a"), ((1, 1), F32, "s")],
-        [(rows, "s"), (value, "h"), (cur, "a"), (image, "a")],
+        [(block, BF16, "a"), (spots, BF16, "a"), ((1, 1), F32, "s")],
+        [(rows, "s"), (arrived, "v"), (tiles, "a"), (part, "a")]
+        + [(full, "a"), (z, "a"), (cur, "a"), (begun, "a"), (inverse, "h"), (value, "h")],
         1 << 24,
-        4 << 20,
-        [room(block, BF16), room(block, F32), room(block, BF16), room(block, BF16), room(spots, BF16), sems],
+        12 << 20,
+        [room(tiles.shape, BF16), *wide, room(spots, BF16), sems, pltpu.SemaphoreType.DMA((5,))],
     )
-    cur, out = filtered(begun, cur, out, centre)
+
+    def first():
+        ins = [(centre, "s"), (z, "h"), (cur, "h"), (inverse, "h")]
+        return call(first_kernel, [(block, BF16, "h")], ins, 1 << 24, 2 << 20)[0]
+
+    cur, out = filtered(first, y, out, centre, 2)
 
     arrived = exchange(out)
-    [value] = sums(cur, arrived, own("image", cur), 0)
-    return call(
-        functools.partial(end_kernel, total),
-        [((k, own_rows), BF16, "h"), (square, F32, "h")],
-        [(value, "h"), (cur, "a")],
-        1 << 24,
-        2 << 20,
-        [room(block, BF16), sems],
+    value, part = beside(gram(cur), lambda x: own("image", cur, [(x, "a")]))
+    [partial] = image(cur, arrived, part, value, True)
+    inverse, basis = factor(value, cur, True)
+    [ritz] = call(
+        functools.partial(ritz_kernel, total), [(square, F32, "h")], [(inverse, "h"), (everywhere(partial), "h")], 1 << 20, 1 << 16
     )
+    return basis, ritz
 
 
 def solution(mesh):

time: 451 us -> 498 us (1.10); the launches traced: 449 us -> 488 us
  starting transfers between devices: 51.5 us -> 108 us
  blocking collectives: 48 us -> 10.8 us
  Pallas kernels: 108 us -> 121 us
    all_to_all x9, waiting for transfers between devices: 190 us -> 116 us  [exchange(): return lax.all_to_all(out, 'dom', 0, 0, tiled=True)]
    ppermute x0 -> x30, waiting for transfers between devices: none -> 73.1 us  [other(): return lax.ppermute(x, 'dom', [(i, i ^ step) for i in range(peers)])]
    ppermute x0 -> x30, starting transfers between devices: none -> 44.5 us  [other(): return lax.ppermute(x, 'dom', [(i, i ^ step) for i in range(peers)])]
    all_to_all x4 -> x1, blocking collectives: 48 us -> 10.8 us  [everywhere(): lax.all_to_all(many, 'dom', 0, 0, axis_index_groups=groups, tiled=True)]
    pallas_call x24 -> x27, Pallas kernels: 108 us -> 121 us  [call(): pl.pallas_call(body, out_shape=[(place[kind] if kind in place else jax.Sh...]
    all_to_all x9, starting transfers between devices: 51.5 us -> 59.7 us  [exchange(): return lax.all_to_all(out, 'dom', 0, 0, tiled=True)]
    unnamed x84 -> x106, local copies, waits for them, and re-layouts: 50.1 us -> 48.7 us
  transfers between devices with their start and end apart: 9 -> 40, of which waited for: 9 -> 20; matrix products, arithmetic and copies ran while one was open for 0% -> 0% of each run, Pallas kernels for 8% -> 12%
where the time goes in v3:
time: 498 us; the launch traced here: 488 us
  waiting for transfers between devices  193 us (39%)
  Pallas kernels  121 us (24%)
  starting transfers between devices  108 us (22%)
  local copies, waits for them, and re-layouts  49.3 us (10%)
  blocking collectives  10.8 us (2%)
    pallas_call x27, Pallas kernels, call(): pl.pallas_call(body, out_shape=[(place[kind] if kind in place else jax.Sh...  121 us
    all_to_all x9, waiting for transfers between devices, exchange(): return lax.all_to_all(out, 'dom', 0, 0, tiled=True)  116 us
    ppermute x30, waiting for transfers between devices, other(): return lax.ppermute(x, 'dom', [(i, i ^ step) for i in range(peers)])  73.1 us
    all_to_all x9, starting transfers between devices, exchange(): return lax.all_to_all(out, 'dom', 0, 0, tiled=True)  59.7 us
    unnamed x106, local copies, waits for them, and re-layouts  48.7 us
    ppermute x30, starting transfers between devices, other(): return lax.ppermute(x, 'dom', [(i, i ^ step) for i in range(peers)])  44.5 us
    all_to_all x1, blocking collectives, everywhere(): lax.all_to_all(many, 'dom', 0, 0, axis_index_groups=groups, tiled=True)  10.8 us
  transfers between devices with their start and end apart: 40, of which 20 were waited for; matrix products, arithmetic and copies ran while one was open for 0% of the time, Pallas kernels for 12%

profile of v3, /device:TPU:0, one launch (start us, length us, event | category | flops | bytes accessed | tf_op | source)
XLA Modules:
  0.0 487.7 jit_solution(9711739134100127112)
XLA Ops:
  5.3 11.7 %all-to-all-start = ((bf16[128,64,128]{2,1,0:T(8,128)(2,1)}), bf16[128,64,128]{2,1,0:T(8,128)(2,1)}, u32[]{:S(2)}, u32[]{:S(2)}) async-start(bf16[128,64,128]{2,1,0:T(8,128)(2,1)} %get-tuple-element.26), calls=%async_computation | async-start | bytes 4194304 | tf_op jit(solution)/shard_map/all_to_all | solution.py:282
  19.8 2.8 shard_map.87.tiles_ref
  24.7 4.4 shard_map.88.part_ref
  30.1 16.8 %all-to-all-done.arrived_ref = bf16[128,64,128]{2,1,0:T(8,128)(2,1)} async-done(((bf16[128,64,128]{2,1,0:T(8,128)(2,1)}), bf16[128,64,128]{2,1,0:T(8,128)(2,1)}, u32[]{:S(2)}, u32[]{:S(2)}) %all-to-all-start) | async-done | bytes 2097184 | tf_op jit(solution)/shard_map/all_to_all | solution.py:282
  47.0 6.8 %shard_map.89 = (bf16[32,64,128]{2,1,0:T(8,128)(2,1)}, bf16[128,64,128]{2,1,0:T(8,128)(2,1)}) custom-call(s32[128]{0:T(128)S(1)} %bitcast.8, bf16[128,64,128]{2,1,0:T(8,128)(2,1)} %all-to-all-done.arrived_ref, bf16[128,128,128]{2,1,0:T(8,128)(2,1)} %copy-done.8, f32[32,64,128]{2,1,0:T(8,128)} %copy-done.27), custom_call_target="tpu_custom_call" | custom-call | flops 268435456 | bytes 10485760 | tf_op jit(solution)/shard_map/pallas_call | solution.py:24
  53.7 4.7 all-to-all-start.1
  63.3 4.4 shard_map.90.part_ref
  68.7 20.1 %all-to-all-done.1.arrived_ref = bf16[128,64,128]{2,1,0:T(8,128)(2,1)S(1)} async-done(((bf16[128,64,128]{2,1,0:T(8,128)(2,1)}), bf16[128,64,128]{2,1,0:T(8,128)(2,1)S(1)}, u32[]{:S(2)}, u32[]{:S(2)}) %all-to-all-start.1) | async-done | bytes 2097184 | tf_op jit(solution)/shard_map/all_to_all | solution.py:282
  88.8 5.7 %shard_map.91 = (bf16[32,64,128]{2,1,0:T(8,128)(2,1)}, bf16[128,64,128]{2,1,0:T(8,128)(2,1)}) custom-call(s32[128]{0:T(128)S(1)} %bitcast.9, bf16[128,64,128]{2,1,0:T(8,128)(2,1)S(1)} %all-to-all-done.1.arrived_ref, bf16[128,128,128]{2,1,0:T(8,128)(2,1)} %copy-done.8, f32[32,64,128]{2,1,0:T(8,128)} %copy-done.24), custom_call_target="tpu_custom_call" | custom-call | flops 268435456 | bytes 10485760 | tf_op jit(solution)/shard_map/pallas_call | solution.py:24
  94.5 4.7 all-to-all-start.2
  104.1 4.4 shard_map.92.part_ref
  109.6 20.1 %all-to-all-done.2.arrived_ref = bf16[128,64,128]{2,1,0:T(8,128)(2,1)S(1)} async-done(((bf16[128,64,128]{2,1,0:T(8,128)(2,1)}), bf16[128,64,128]{2,1,0:T(8,128)(2,1)S(1)}, u32[]{:S(2)}, u32[]{:S(2)}) %all-to-all-start.2) | async-done | bytes 2097184 | tf_op jit(solution)/shard_map/all_to_all | solution.py:282
  129.7 5.7 %shard_map.93 = (bf16[32,64,128]{2,1,0:T(8,128)(2,1)}, bf16[128,64,128]{2,1,0:T(8,128)(2,1)}) custom-call(s32[128]{0:T(128)S(1)} %bitcast.10, bf16[128,64,128]{2,1,0:T(8,128)(2,1)S(1)} %all-to-all-done.2.arrived_ref, bf16[128,128,128]{2,1,0:T(8,128)(2,1)} %copy-done.8, f32[32,64,128]{2,1,0:T(8,128)} %copy-done.25), custom_call_target="tpu_custom_call" | custom-call | flops 268435456 | bytes 10485760 | tf_op jit(solution)/shard_map/pallas_call | solution.py:24
  135.4 4.7 all-to-all-start.3
  144.9 4.4 shard_map.94.part_ref
  150.4 20.1 %all-to-all-done.3.arrived_ref = bf16[128,64,128]{2,1,0:T(8,128)(2,1)S(1)} async-done(((bf16[128,64,128]{2,1,0:T(8,128)(2,1)}), bf16[128,64,128]{2,1,0:T(8,128)(2,1)S(1)}, u32[]{:S(2)}, u32[]{:S(2)}) %all-to-all-start.3) | async-done | bytes 2097184 | tf_op jit(solution)/shard_map/all_to_all | solution.py:282
  170.5 5.7 %shard_map.95 = (bf16[32,64,128]{2,1,0:T(8,128)(2,1)}, bf16[128,64,128]{2,1,0:T(8,128)(2,1)}) custom-call(s32[128]{0:T(128)S(1)} %bitcast.11, bf16[128,64,128]{2,1,0:T(8,128)(2,1)S(1)} %all-to-all-done.3.arrived_ref, bf16[128,128,128]{2,1,0:T(8,128)(2,1)} %copy-done.8, f32[32,64,128]{2,1,0:T(8,128)} %copy-done.22), custom_call_target="tpu_custom_call" | custom-call | flops 268435456 | bytes 10485760 | tf_op jit(solution)/shard_map/pallas_call | solution.py:24
  176.2 5.9 %all-to-all-start.4 = ((bf16[128,64,128]{2,1,0:T(8,128)(2,1)}), bf16[128,64,128]{2,1,0:T(8,128)(2,1)}, u32[]{:S(2)}, u32[]{:S(2)}) async-start(bf16[128,64,128]{2,1,0:T(8,128)(2,1)} %get-tuple-element.34), calls=%async_computation.4 | async-start | bytes 4194304 | tf_op jit(solution)/shard_map/all_to_all | solution.py:282
  185.0 3.2 collective-permute-start.2
  188.7 16.2 %collective-permute-done.1 = f32[64,64]{1,0:T(8,128)S(1)} collective-permute-done((f32[64,64]{1,0:T(8,128)S(1)}, f32[64,64]{1,0:T(8,128)S(1)}, u32[]{:S(2)}, u32[]{:S(2)}) %collective-permute-start.1) | collective-permute-done | bytes 16416 | tf_op jit(solution)/shard_map/ppermute | solution.py:308
  205.0 4.1 collective-permute-done.2
  226.2 4.4 shard_map.97.part_ref
  232.2 7.1 %shard_map.98 = (f32[32,64,128]{2,1,0:T(8,128)}, bf16[32,64,128]{2,1,0:T(8,128)(2,1)}, bf16[128,64,128]{2,1,0:T(8,128)(2,1)}) custom-call(s32[128]{0:T(128)S(1)} %bitcast.12, bf16[128,64,128]{2,1,0:T(8,128)(2,1)} %all-to-all-done.4.arrived_ref, bf16[128,128,128]{2,1,0:T(8,128)(2,1)} %copy-done.8, f32[32,64,128]{2,1,0:T(8,128)} %copy-done.19, ...), custom_call_target="tpu_custom_call" | custom-call | flops 268435456 | bytes 10485760 | tf_op jit(solution)/shard_map/pallas_call | solution.py:24
  239.3 7.5 %all-to-all-start.5 = ((bf16[128,64,128]{2,1,0:T(8,128)(2,1)}), bf16[128,64,128]{2,1,0:T(8,128)(2,1)}, u32[]{:S(2)}, u32[]{:S(2)}) async-start(bf16[128,64,128]{2,1,0:T(8,128)(2,1)} %get-tuple-element.36), calls=%async_computation.5 | async-start | bytes 4194304 | tf_op jit(solution)/shard_map/all_to_all | solution.py:282
  250.2 3.2 collective-permute-start.12
  253.9 16.0 %collective-permute-done.11 = f32[64,64]{1,0:T(8,128)S(1)} collective-permute-done((f32[64,64]{1,0:T(8,128)S(1)}, f32[64,64]{1,0:T(8,128)S(1)}, u32[]{:S(2)}, u32[]{:S(2)}) %collective-permute-start.11) | collective-permute-done | bytes 16416 | tf_op jit(solution)/shard_map/ppermute | solution.py:308
  269.8 3.9 collective-permute-done.12
  278.8 4.6 shard_map.101
  291.9 4.6 shard_map.100.part_ref
  297.5 9.1 %shard_map.102 = (bf16[32,64,128]{2,1,0:T(8,128)(2,1)}, bf16[128,64,128]{2,1,0:T(8,128)(2,1)}, f32[1,1]{1,0:T(1,128)}) custom-call(s32[128]{0:T(128)S(1)} %bitcast.13, bf16[128,64,128]{2,1,0:T(8,128)(2,1)} %all-to-all-done.5.arrived_ref, bf16[128,128,128]{2,1,0:T(8,128)(2,1)} %copy-done.8, f32[32,64,128]{2,1,0:T(8,128)} %copy-done.17, ...), custom_call_target="tpu_custom_call" | custom-call | flops 16777216 | bytes 12582912 | tf_op jit(solution)/shard_map/pallas_call | solution.py:24
  306.7 10.0 %all-to-all-start.6 = ((bf16[128,64,128]{2,1,0:T(8,128)(2,1)}), bf16[128,64,128]{2,1,0:T(8,128)(2,1)}, u32[]{:S(2)}, u32[]{:S(2)}) async-start(bf16[128,64,128]{2,1,0:T(8,128)(2,1)} %get-tuple-element.41), calls=%async_computation.6 | async-start | bytes 4194304 | tf_op jit(solution)/shard_map/all_to_all | solution.py:282
  321.1 5.1 %shard_map.104.part_ref = f32[32,64,128]{2,1,0:T(8,128)S(1)} custom-call(s32[96]{0:T(128)S(1)} %get-tuple-element.51.first_ref, s32[96]{0:T(128)S(1)} %get-tuple-element.50.second_ref, s32[1]{0:T(128)S(6)} %copy.9.count_ref, f32[1,1]{1,0:T(1,128)} %get-tuple-element.42.centre_ref.refs_0_, bf16[32,64,128]{2,1,0:T(8,128)(2,1)S(1)} %copy-done.28, ...), custom_call_target="tpu_custom_call" | custom-call | flops 469762048 | bytes 9437184 | tf_op jit(solution)/shard_map/pallas_call | solution.py:24
  327.2 19.5 %all-to-all-done.6.arrived_ref = bf16[128,64,128]{2,1,0:T(8,128)(2,1)} async-done(((bf16[128,64,128]{2,1,0:T(8,128)(2,1)}), bf16[128,64,128]{2,1,0:T(8,128)(2,1)}, u32[]{:S(2)}, u32[]{:S(2)}) %all-to-all-start.6) | async-done | bytes 2097184 | tf_op jit(solution)/shard_map/all_to_all | solution.py:282
  346.7 6.7 %shard_map.105 = (bf16[32,64,128]{2,1,0:T(8,128)(2,1)}, bf16[128,64,128]{2,1,0:T(8,128)(2,1)}) custom-call(s32[128]{0:T(128)S(1)} %bitcast.14, bf16[128,64,128]{2,1,0:T(8,128)(2,1)} %all-to-all-done.6.arrived_ref, bf16[128,128,128]{2,1,0:T(8,128)(2,1)} %copy-done.8, f32[32,64,128]{2,1,0:T(8,128)} %copy-done.26), custom_call_target="tpu_custom_call" | custom-call | flops 268435456 | bytes 10485760 | tf_op jit(solution)/shard_map/pallas_call | solution.py:24
  353.5 4.7 all-to-all-start.7
  363.0 5.1 %shard_map.106.part_ref = f32[32,64,128]{2,1,0:T(8,128)S(1)} custom-call(s32[96]{0:T(128)S(1)} %get-tuple-element.51.first_ref, s32[96]{0:T(128)S(1)} %get-tuple-element.50.second_ref, s32[1]{0:T(128)S(6)} %copy.9.count_ref, f32[1,1]{1,0:T(1,128)} %get-tuple-element.42.centre_ref.refs_0_, bf16[32,64,128]{2,1,0:T(8,128)(2,1)S(1)} %copy-done.39, ...), custom_call_target="tpu_custom_call" | custom-call | flops 469762048 | bytes 9437184 | tf_op jit(solution)/shard_map/pallas_call | solution.py:24
  369.1 19.5 %all-to-all-done.7.arrived_ref = bf16[128,64,128]{2,1,0:T(8,128)(2,1)S(1)} async-done(((bf16[128,64,128]{2,1,0:T(8,128)(2,1)}), bf16[128,64,128]{2,1,0:T(8,128)(2,1)S(1)}, u32[]{:S(2)}, u32[]{:S(2)}) %all-to-all-start.7) | async-done | bytes 2097184 | tf_op jit(solution)/shard_map/all_to_all | solution.py:282
  388.6 5.7 %shard_map.107 = (bf16[32,64,128]{2,1,0:T(8,128)(2,1)}, bf16[128,64,128]{2,1,0:T(8,128)(2,1)}) custom-call(s32[128]{0:T(128)S(1)} %bitcast.15, bf16[128,64,128]{2,1,0:T(8,128)(2,1)S(1)} %all-to-all-done.7.arrived_ref, bf16[128,128,128]{2,1,0:T(8,128)(2,1)} %copy-done.8, f32[32,64,128]{2,1,0:T(8,128)} %copy-done.23), custom_call_target="tpu_custom_call" | custom-call | flops 268435456 | bytes 10485760 | tf_op jit(solution)/shard_map/pallas_call | solution.py:24
  394.3 5.9 %all-to-all-start.8 = ((bf16[128,64,128]{2,1,0:T(8,128)(2,1)}), bf16[128,64,128]{2,1,0:T(8,128)(2,1)}, u32[]{:S(2)}, u32[]{:S(2)}) async-start(bf16[128,64,128]{2,1,0:T(8,128)(2,1)} %get-tuple-element.49), calls=%async_computation.8 | async-start | bytes 4194304 | tf_op jit(solution)/shard_map/all_to_all | solution.py:282
  403.0 3.2 collective-permute-start.22
  406.7 16.4 %collective-permute-done.21 = f32[64,64]{1,0:T(8,128)S(1)} collective-permute-done((f32[64,64]{1,0:T(8,128)S(1)}, f32[64,64]{1,0:T(8,128)S(1)}, u32[]{:S(2)}, u32[]{:S(2)}) %collective-permute-start.21) | collective-permute-done | bytes 16416 | tf_op jit(solution)/shard_map/ppermute | solution.py:308
  423.1 4.0 collective-permute-done.22
  444.6 4.4 shard_map.110.part_ref
  450.6 7.7 %shard_map.111 = f32[64,64]{1,0:T(8,128)S(1)} custom-call(s32[128]{0:T(128)S(1)} %bitcast.16, bf16[128,64,128]{2,1,0:T(8,128)(2,1)} %all-to-all-done.8.arrived_ref, bf16[128,128,128]{2,1,0:T(8,128)(2,1)} %copy-done.8, f32[32,64,128]{2,1,0:T(8,128)} %copy-done.18, bf16[32,64,128]{2,1,0:T(8,128)(2,1)} %get-tuple-element.46.cur_ref.refs_0_, ...), custom_call_target="tpu_custom_call" | custom-call | flops 268435456 | bytes 10485760 | tf_op jit(solution)/shard_map/pallas_call | solution.py:24
  458.6 10.8 %all_to_all.55 = f32[8,1,4096]{2,1,0:T(1,128)S(1)} all-to-all(f32[8,1,4096]{2,1,0:T(1,128)S(1)} %reshape.6), channel_id=1, replica_groups={{0,1,2,3,4,5,6,7},{8,9,10,11,12,13,14,15},{16,17,18,19,20,21,22,23},{24..., dimensions={0} | all-to-all | bytes 262144 | tf_op jit(solution)/shard_map/all_to_all | solution.py:304
  472.0 4.0 all-to-all-start.10
  476.1 5.4 %shard_map.109 = (f32[64,64]{1,0:T(8,128)S(1)}, bf16[64,4096]{1,0:T(8,128)(2,1)}) custom-call(f32[64,64]{1,0:T(8,128)S(1)} %copy-done.42, bf16[32,64,128]{2,1,0:T(8,128)(2,1)S(1)} %copy-done.14), custom_call_target="tpu_custom_call" | custom-call | flops 16777216 | bytes 2097152 | tf_op jit(solution)/shard_map/pallas_call | solution.py:24
  481.5 3.3 all-to-all-done.10
  (187 shorter events, 106.7 us)
Async XLA Ops:
  5.3 19.4 %slice-start = ((s8[6291456]{0:T(1024)(128)(4,1)}), s8[2097152]{0:T(1024)(128)(4,1)S(1)}, s32[]{:S(2)}) async-start(s8[6291456]{0:T(1024)(128)(4,1)} %bitcast.5), calls=%async_computation.11 | async-start | bytes 4194304
  5.3 41.7 %all-to-all-start = ((bf16[128,64,128]{2,1,0:T(8,128)(2,1)}), bf16[128,64,128]{2,1,0:T(8,128)(2,1)}, u32[]{:S(2)}, u32[]{:S(2)}) async-start(bf16[128,64,128]{2,1,0:T(8,128)(2,1)} %get-tuple-element.26), calls=%async_computation | async-start | bytes 4194304 | tf_op jit(solution)/shard_map/all_to_all | solution.py:282
  24.7 22.3 %copy-start.44 = (s32[1,128]{1,0:T(1,128)S(1)}, s32[1,128]{1,0:T(1,128)}, u32[]{:S(2)}) copy-start(s32[1,128]{1,0:T(1,128)} %param.11) | copy-start | bytes 1540
  53.7 35.1 %all-to-all-start.1 = ((bf16[128,64,128]{2,1,0:T(8,128)(2,1)}), bf16[128,64,128]{2,1,0:T(8,128)(2,1)S(1)}, u32[]{:S(2)}, u32[]{:S(2)}) async-start(bf16[128,64,128]{2,1,0:T(8,128)(2,1)} %get-tuple-element.28), calls=%async_computation.1 | async-start | bytes 4194304 | tf_op jit(solution)/shard_map/all_to_all | solution.py:282
  94.5 35.1 %all-to-all-start.2 = ((bf16[128,64,128]{2,1,0:T(8,128)(2,1)}), bf16[128,64,128]{2,1,0:T(8,128)(2,1)S(1)}, u32[]{:S(2)}, u32[]{:S(2)}) async-start(bf16[128,64,128]{2,1,0:T(8,128)(2,1)} %get-tuple-element.30), calls=%async_computation.2 | async-start | bytes 4194304 | tf_op jit(solution)/shard_map/all_to_all | solution.py:282
  135.4 35.1 %all-to-all-start.3 = ((bf16[128,64,128]{2,1,0:T(8,128)(2,1)}), bf16[128,64,128]{2,1,0:T(8,128)(2,1)S(1)}, u32[]{:S(2)}, u32[]{:S(2)}) async-start(bf16[128,64,128]{2,1,0:T(8,128)(2,1)} %get-tuple-element.32), calls=%async_computation.3 | async-start | bytes 4194304 | tf_op jit(solution)/shard_map/all_to_all | solution.py:282
  176.2 56.0 %all-to-all-start.4 = ((bf16[128,64,128]{2,1,0:T(8,128)(2,1)}), bf16[128,64,128]{2,1,0:T(8,128)(2,1)}, u32[]{:S(2)}, u32[]{:S(2)}) async-start(bf16[128,64,128]{2,1,0:T(8,128)(2,1)} %get-tuple-element.34), calls=%async_computation.4 | async-start | bytes 4194304 | tf_op jit(solution)/shard_map/all_to_all | solution.py:282
  182.5 1.2 collective-permute-start
  183.8 39.6 %copy-start.47 = (f32[64,64]{1,0:T(8,128)}, f32[64,64]{1,0:T(8,128)S(1)}, u32[]{:S(2)}) copy-start(f32[64,64]{1,0:T(8,128)S(1)} %add.90.refs_3_) | copy-start | bytes 49156
  183.8 21.2 %collective-permute-start.1 = (f32[64,64]{1,0:T(8,128)S(1)}, f32[64,64]{1,0:T(8,128)S(1)}, u32[]{:S(2)}, u32[]{:S(2)}) collective-permute-start(f32[64,64]{1,0:T(8,128)S(1)} %add.90.refs_3_), channel_id=1, source_target_pairs={{0,2},{1,3},{2,0},{3,1},{4,6},{5,7},{6,4},{7,5},{8,10},{9,11},{10,... | collective-permute-start | bytes 49160 | tf_op jit(solution)/shard_map/ppermute | solution.py:308
  185.0 24.0 %collective-permute-start.2 = (f32[64,64]{1,0:T(8,128)S(1)}, f32[64,64]{1,0:T(8,128)S(1)}, u32[]{:S(2)}, u32[]{:S(2)}) collective-permute-start(f32[64,64]{1,0:T(8,128)S(1)} %add.90.refs_3_), channel_id=1, source_target_pairs={{0,4},{1,5},{2,6},{3,7},{4,0},{5,1},{6,2},{7,3},{8,12},{9,13},{10,... | collective-permute-start | bytes 49160 | tf_op jit(solution)/shard_map/ppermute | solution.py:308
  188.3 20.8 %collective-permute-start.3 = (f32[64,64]{1,0:T(8,128)S(1)}, f32[64,64]{1,0:T(8,128)S(1)}, u32[]{:S(2)}, u32[]{:S(2)}) collective-permute-start(f32[64,64]{1,0:T(8,128)S(1)} %add.90.refs_3_), channel_id=1, source_target_pairs={{0,6},{1,7},{2,4},{3,5},{4,2},{5,3},{6,0},{7,1},{8,14},{9,15},{10,... | collective-permute-start | bytes 49160 | tf_op jit(solution)/shard_map/ppermute | solution.py:308
  209.1 5.1 %collective-permute-start.4 = (f32[64,64]{1,0:T(8,128)S(1)}, f32[64,64]{1,0:T(8,128)S(1)}, u32[]{:S(2)}, u32[]{:S(2)}) collective-permute-start(f32[64,64]{1,0:T(8,128)S(1)} %add_add_fusion.8), channel_id=1, source_target_pairs={{0,8},{1,9},{2,10},{3,11},{4,12},{5,13},{6,14},{7,15},{8,0},{9,1},... | collective-permute-start | bytes 49160 | tf_op jit(solution)/shard_map/ppermute | solution.py:308
  211.4 5.4 %collective-permute-start.5 = (f32[64,64]{1,0:T(8,128)S(1)}, f32[64,64]{1,0:T(8,128)S(1)}, u32[]{:S(2)}, u32[]{:S(2)}) collective-permute-start(f32[64,64]{1,0:T(8,128)S(1)} %add_add_fusion.8), channel_id=1, source_target_pairs={{0,16},{1,17},{2,18},{3,19},{4,20},{5,21},{6,22},{7,23},{8,24},{9,... | collective-permute-start | bytes 49160 | tf_op jit(solution)/shard_map/ppermute | solution.py:308
  213.5 5.1 %collective-permute-start.6 = (f32[64,64]{1,0:T(8,128)S(1)}, f32[64,64]{1,0:T(8,128)S(1)}, u32[]{:S(2)}, u32[]{:S(2)}) collective-permute-start(f32[64,64]{1,0:T(8,128)S(1)} %add_add_fusion.8), channel_id=1, source_target_pairs={{0,24},{1,25},{2,26},{3,27},{4,28},{5,29},{6,30},{7,31},{8,16},{9,... | collective-permute-start | bytes 49160 | tf_op jit(solution)/shard_map/ppermute | solution.py:308
  218.6 12.9 %collective-permute-start.7 = (f32[64,64]{1,0:T(8,128)S(1)}, f32[64,64]{1,0:T(8,128)S(1)}, u32[]{:S(2)}, u32[]{:S(2)}) collective-permute-start(f32[64,64]{1,0:T(8,128)S(1)} %add_add_fusion.7), channel_id=1, source_target_pairs={{0,32},{1,33},{2,34},{3,35},{4,36},{5,37},{6,38},{7,39},{8,40},{9,... | collective-permute-start | bytes 49160 | tf_op jit(solution)/shard_map/ppermute | solution.py:308
  220.4 11.2 %collective-permute-start.8 = (f32[64,64]{1,0:T(8,128)S(1)}, f32[64,64]{1,0:T(8,128)S(1)}, u32[]{:S(2)}, u32[]{:S(2)}) collective-permute-start(f32[64,64]{1,0:T(8,128)S(1)} %add_add_fusion.7), channel_id=1, source_target_pairs={{0,64},{1,65},{2,66},{3,67},{4,68},{5,69},{6,70},{7,71},{8,72},{9,... | collective-permute-start | bytes 49160 | tf_op jit(solution)/shard_map/ppermute | solution.py:308
  222.8 8.7 %collective-permute-start.9 = (f32[64,64]{1,0:T(8,128)S(1)}, f32[64,64]{1,0:T(8,128)S(1)}, u32[]{:S(2)}, u32[]{:S(2)}) collective-permute-start(f32[64,64]{1,0:T(8,128)S(1)} %add_add_fusion.7), channel_id=1, source_target_pairs={{0,96},{1,97},{2,98},{3,99},{4,100},{5,101},{6,102},{7,103},{8,104... | collective-permute-start | bytes 49160 | tf_op jit(solution)/shard_map/ppermute | solution.py:308
  239.3 39.5 %copy-start.41 = (f32[64,64]{1,0:T(8,128)S(1)}, f32[64,64]{1,0:T(8,128)}, u32[]{:S(2)}) copy-start(f32[64,64]{1,0:T(8,128)} %add_add_fusion.6.gram_ref) | copy-start | bytes 49156
  239.3 58.2 %all-to-all-start.5 = ((bf16[128,64,128]{2,1,0:T(8,128)(2,1)}), bf16[128,64,128]{2,1,0:T(8,128)(2,1)}, u32[]{:S(2)}, u32[]{:S(2)}) async-start(bf16[128,64,128]{2,1,0:T(8,128)(2,1)} %get-tuple-element.36), calls=%async_computation.5 | async-start | bytes 4194304 | tf_op jit(solution)/shard_map/all_to_all | solution.py:282
  246.8 42.3 %copy-start.15 = (bf16[32,64,128]{2,1,0:T(8,128)(2,1)S(1)}, bf16[32,64,128]{2,1,0:T(8,128)(2,1)}, u32[]{:S(2)}) copy-start(bf16[32,64,128]{2,1,0:T(8,128)(2,1)} %get-tuple-element.37.refs_0_.z_ref) | copy-start | bytes 1572868
  247.8 1.3 collective-permute-start.10
  249.1 40.0 %copy-start.45 = (f32[64,64]{1,0:T(8,128)}, f32[64,64]{1,0:T(8,128)S(1)}, u32[]{:S(2)}) copy-start(f32[64,64]{1,0:T(8,128)S(1)} %add.100.refs_3_) | copy-start | bytes 49156
  249.1 20.8 %collective-permute-start.11 = (f32[64,64]{1,0:T(8,128)S(1)}, f32[64,64]{1,0:T(8,128)S(1)}, u32[]{:S(2)}, u32[]{:S(2)}) collective-permute-start(f32[64,64]{1,0:T(8,128)S(1)} %add.100.refs_3_), channel_id=1, source_target_pairs={{0,2},{1,3},{2,0},{3,1},{4,6},{5,7},{6,4},{7,5},{8,10},{9,11},{10,... | collective-permute-start | bytes 49160 | tf_op jit(solution)/shard_map/ppermute | solution.py:308
  250.2 23.6 %collective-permute-start.12 = (f32[64,64]{1,0:T(8,128)S(1)}, f32[64,64]{1,0:T(8,128)S(1)}, u32[]{:S(2)}, u32[]{:S(2)}) collective-permute-start(f32[64,64]{1,0:T(8,128)S(1)} %add.100.refs_3_), channel_id=1, source_target_pairs={{0,4},{1,5},{2,6},{3,7},{4,0},{5,1},{6,2},{7,3},{8,12},{9,13},{10,... | collective-permute-start | bytes 49160 | tf_op jit(solution)/shard_map/ppermute | solution.py:308
  253.4 20.4 %collective-permute-start.13 = (f32[64,64]{1,0:T(8,128)S(1)}, f32[64,64]{1,0:T(8,128)S(1)}, u32[]{:S(2)}, u32[]{:S(2)}) collective-permute-start(f32[64,64]{1,0:T(8,128)S(1)} %add.100.refs_3_), channel_id=1, source_target_pairs={{0,6},{1,7},{2,4},{3,5},{4,2},{5,3},{6,0},{7,1},{8,14},{9,15},{10,... | collective-permute-start | bytes 49160 | tf_op jit(solution)/shard_map/ppermute | solution.py:308
  273.8 10.5 %collective-permute-start.14 = (f32[64,64]{1,0:T(8,128)S(1)}, f32[64,64]{1,0:T(8,128)S(1)}, u32[]{:S(2)}, u32[]{:S(2)}) collective-permute-start(f32[64,64]{1,0:T(8,128)S(1)} %add_add_fusion.5), channel_id=1, source_target_pairs={{0,8},{1,9},{2,10},{3,11},{4,12},{5,13},{6,14},{7,15},{8,0},{9,1},... | collective-permute-start | bytes 49160 | tf_op jit(solution)/shard_map/ppermute | solution.py:308
  276.1 8.2 %collective-permute-start.15 = (f32[64,64]{1,0:T(8,128)S(1)}, f32[64,64]{1,0:T(8,128)S(1)}, u32[]{:S(2)}, u32[]{:S(2)}) collective-permute-start(f32[64,64]{1,0:T(8,128)S(1)} %add_add_fusion.5), channel_id=1, source_target_pairs={{0,16},{1,17},{2,18},{3,19},{4,20},{5,21},{6,22},{7,23},{8,24},{9,... | collective-permute-start | bytes 49160 | tf_op jit(solution)/shard_map/ppermute | solution.py:308
  278.2 6.1 %collective-permute-start.16 = (f32[64,64]{1,0:T(8,128)S(1)}, f32[64,64]{1,0:T(8,128)S(1)}, u32[]{:S(2)}, u32[]{:S(2)}) collective-permute-start(f32[64,64]{1,0:T(8,128)S(1)} %add_add_fusion.5), channel_id=1, source_target_pairs={{0,24},{1,25},{2,26},{3,27},{4,28},{5,29},{6,30},{7,31},{8,16},{9,... | collective-permute-start | bytes 49160 | tf_op jit(solution)/shard_map/ppermute | solution.py:308
  284.3 13.2 %collective-permute-start.17 = (f32[64,64]{1,0:T(8,128)S(1)}, f32[64,64]{1,0:T(8,128)S(1)}, u32[]{:S(2)}, u32[]{:S(2)}) collective-permute-start(f32[64,64]{1,0:T(8,128)S(1)} %add_add_fusion.4), channel_id=1, source_target_pairs={{0,32},{1,33},{2,34},{3,35},{4,36},{5,37},{6,38},{7,39},{8,40},{9,... | collective-permute-start | bytes 49160 | tf_op jit(solution)/shard_map/ppermute | solution.py:308
  285.5 12.0 %collective-permute-start.18 = (f32[64,64]{1,0:T(8,128)S(1)}, f32[64,64]{1,0:T(8,128)S(1)}, u32[]{:S(2)}, u32[]{:S(2)}) collective-permute-start(f32[64,64]{1,0:T(8,128)S(1)} %add_add_fusion.4), channel_id=1, source_target_pairs={{0,64},{1,65},{2,66},{3,67},{4,68},{5,69},{6,70},{7,71},{8,72},{9,... | collective-permute-start | bytes 49160 | tf_op jit(solution)/shard_map/ppermute | solution.py:308
  287.9 9.5 %collective-permute-start.19 = (f32[64,64]{1,0:T(8,128)S(1)}, f32[64,64]{1,0:T(8,128)S(1)}, u32[]{:S(2)}, u32[]{:S(2)}) collective-permute-start(f32[64,64]{1,0:T(8,128)S(1)} %add_add_fusion.4), channel_id=1, source_target_pairs={{0,96},{1,97},{2,98},{3,99},{4,100},{5,101},{6,102},{7,103},{8,104... | collective-permute-start | bytes 49160 | tf_op jit(solution)/shard_map/ppermute | solution.py:308
  306.7 40.1 %all-to-all-start.6 = ((bf16[128,64,128]{2,1,0:T(8,128)(2,1)}), bf16[128,64,128]{2,1,0:T(8,128)(2,1)}, u32[]{:S(2)}, u32[]{:S(2)}) async-start(bf16[128,64,128]{2,1,0:T(8,128)(2,1)} %get-tuple-element.41), calls=%async_computation.6 | async-start | bytes 4194304 | tf_op jit(solution)/shard_map/all_to_all | solution.py:282
  353.5 35.1 %all-to-all-start.7 = ((bf16[128,64,128]{2,1,0:T(8,128)(2,1)}), bf16[128,64,128]{2,1,0:T(8,128)(2,1)S(1)}, u32[]{:S(2)}, u32[]{:S(2)}) async-start(bf16[128,64,128]{2,1,0:T(8,128)(2,1)} %get-tuple-element.44), calls=%async_computation.7 | async-start | bytes 4194304 | tf_op jit(solution)/shard_map/all_to_all | solution.py:282
  394.3 56.3 %all-to-all-start.8 = ((bf16[128,64,128]{2,1,0:T(8,128)(2,1)}), bf16[128,64,128]{2,1,0:T(8,128)(2,1)}, u32[]{:S(2)}, u32[]{:S(2)}) async-start(bf16[128,64,128]{2,1,0:T(8,128)(2,1)} %get-tuple-element.49), calls=%async_computation.8 | async-start | bytes 4194304 | tf_op jit(solution)/shard_map/all_to_all | solution.py:282
  400.7 1.2 collective-permute-start.20
  401.9 39.9 %copy-start.46 = (f32[64,64]{1,0:T(8,128)}, f32[64,64]{1,0:T(8,128)S(1)}, u32[]{:S(2)}) copy-start(f32[64,64]{1,0:T(8,128)S(1)} %add.110.refs_3_) | copy-start | bytes 49156
  401.9 21.2 %collective-permute-start.21 = (f32[64,64]{1,0:T(8,128)S(1)}, f32[64,64]{1,0:T(8,128)S(1)}, u32[]{:S(2)}, u32[]{:S(2)}) collective-permute-start(f32[64,64]{1,0:T(8,128)S(1)} %add.110.refs_3_), channel_id=1, source_target_pairs={{0,2},{1,3},{2,0},{3,1},{4,6},{5,7},{6,4},{7,5},{8,10},{9,11},{10,... | collective-permute-start | bytes 49160 | tf_op jit(solution)/shard_map/ppermute | solution.py:308
  403.0 24.1 %collective-permute-start.22 = (f32[64,64]{1,0:T(8,128)S(1)}, f32[64,64]{1,0:T(8,128)S(1)}, u32[]{:S(2)}, u32[]{:S(2)}) collective-permute-start(f32[64,64]{1,0:T(8,128)S(1)} %add.110.refs_3_), channel_id=1, source_target_pairs={{0,4},{1,5},{2,6},{3,7},{4,0},{5,1},{6,2},{7,3},{8,12},{9,13},{10,... | collective-permute-start | bytes 49160 | tf_op jit(solution)/shard_map/ppermute | solution.py:308
  406.2 20.9 %collective-permute-start.23 = (f32[64,64]{1,0:T(8,128)S(1)}, f32[64,64]{1,0:T(8,128)S(1)}, u32[]{:S(2)}, u32[]{:S(2)}) collective-permute-start(f32[64,64]{1,0:T(8,128)S(1)} %add.110.refs_3_), channel_id=1, source_target_pairs={{0,6},{1,7},{2,4},{3,5},{4,2},{5,3},{6,0},{7,1},{8,14},{9,15},{10,... | collective-permute-start | bytes 49160 | tf_op jit(solution)/shard_map/ppermute | solution.py:308
  427.1 5.2 %collective-permute-start.24 = (f32[64,64]{1,0:T(8,128)S(1)}, f32[64,64]{1,0:T(8,128)S(1)}, u32[]{:S(2)}, u32[]{:S(2)}) collective-permute-start(f32[64,64]{1,0:T(8,128)S(1)} %add_add_fusion.2), channel_id=1, source_target_pairs={{0,8},{1,9},{2,10},{3,11},{4,12},{5,13},{6,14},{7,15},{8,0},{9,1},... | collective-permute-start | bytes 49160 | tf_op jit(solution)/shard_map/ppermute | solution.py:308
  429.5 5.4 %collective-permute-start.25 = (f32[64,64]{1,0:T(8,128)S(1)}, f32[64,64]{1,0:T(8,128)S(1)}, u32[]{:S(2)}, u32[]{:S(2)}) collective-permute-start(f32[64,64]{1,0:T(8,128)S(1)} %add_add_fusion.2), channel_id=1, source_target_pairs={{0,16},{1,17},{2,18},{3,19},{4,20},{5,21},{6,22},{7,23},{8,24},{9,... | collective-permute-start | bytes 49160 | tf_op jit(solution)/shard_map/ppermute | solution.py:308
  431.6 5.1 %collective-permute-start.26 = (f32[64,64]{1,0:T(8,128)S(1)}, f32[64,64]{1,0:T(8,128)S(1)}, u32[]{:S(2)}, u32[]{:S(2)}) collective-permute-start(f32[64,64]{1,0:T(8,128)S(1)} %add_add_fusion.2), channel_id=1, source_target_pairs={{0,24},{1,25},{2,26},{3,27},{4,28},{5,29},{6,30},{7,31},{8,16},{9,... | collective-permute-start | bytes 49160 | tf_op jit(solution)/shard_map/ppermute | solution.py:308
  436.8 13.2 %collective-permute-start.27 = (f32[64,64]{1,0:T(8,128)S(1)}, f32[64,64]{1,0:T(8,128)S(1)}, u32[]{:S(2)}, u32[]{:S(2)}) collective-permute-start(f32[64,64]{1,0:T(8,128)S(1)} %add_add_fusion.1), channel_id=1, source_target_pairs={{0,32},{1,33},{2,34},{3,35},{4,36},{5,37},{6,38},{7,39},{8,40},{9,... | collective-permute-start | bytes 49160 | tf_op jit(solution)/shard_map/ppermute | solution.py:308
  438.6 11.4 %collective-permute-start.28 = (f32[64,64]{1,0:T(8,128)S(1)}, f32[64,64]{1,0:T(8,128)S(1)}, u32[]{:S(2)}, u32[]{:S(2)}) collective-permute-start(f32[64,64]{1,0:T(8,128)S(1)} %add_add_fusion.1), channel_id=1, source_target_pairs={{0,64},{1,65},{2,66},{3,67},{4,68},{5,69},{6,70},{7,71},{8,72},{9,... | collective-permute-start | bytes 49160 | tf_op jit(solution)/shard_map/ppermute | solution.py:308
  441.0 9.0 %collective-permute-start.29 = (f32[64,64]{1,0:T(8,128)S(1)}, f32[64,64]{1,0:T(8,128)S(1)}, u32[]{:S(2)}, u32[]{:S(2)}) collective-permute-start(f32[64,64]{1,0:T(8,128)S(1)} %add_add_fusion.1), channel_id=1, source_target_pairs={{0,96},{1,97},{2,98},{3,99},{4,100},{5,101},{6,102},{7,103},{8,104... | collective-permute-start | bytes 49160 | tf_op jit(solution)/shard_map/ppermute | solution.py:308
  458.3 17.8 %copy-start.14 = (bf16[32,64,128]{2,1,0:T(8,128)(2,1)S(1)}, bf16[32,64,128]{2,1,0:T(8,128)(2,1)}, u32[]{:S(2)}) copy-start(bf16[32,64,128]{2,1,0:T(8,128)(2,1)} %get-tuple-element.46.cur_ref.refs_0_) | copy-start | bytes 1572868
  472.0 12.7 %all-to-all-start.10 = ((f32[16,1,4096]{2,1,0:T(1,128)}), f32[16,1,4096]{2,1,0:T(1,128)S(1)}, u32[]{:S(2)}, u32[]{:S(2)}) async-start(f32[16,1,4096]{2,1,0:T(1,128)} %reshape.8), calls=%async_computation.10 | async-start | bytes 524288 | tf_op jit(solution)/shard_map/all_to_all | solution.py:304
  (43 other events, 143.3 us)

commit v4 on v2

--- a/solution.py
+++ b/solution.py
@@ -16,6 +16,7 @@
 
 HBM = pl.BlockSpec(memory_space=pltpu.HBM)
 NODE = 8
+CHUNKS, WAVES = 8, 4
 
 
 def call(body, outs, ins, flops, moved, scratch=()):
@@ -53,31 +54,40 @@
     return copy
 
 
-def spread(rows_ref, blocks_ref, slots_ref, out_ref, sems):
-    half = slots_ref.shape[0] // 2
+def load(tiles_ref, tiles, sems):
+    some = tiles.shape[0] // CHUNKS
+    return [begin(tiles_ref.at[pl.ds(g * some, some)], tiles.at[pl.ds(g * some, some)], sems.at[g]) for g in range(CHUNKS)]
+
+
+def send(rows_ref, blocks, tiles, coming, slots, out_ref, sems):
+    some, ready = slots.shape[0] // WAVES, CHUNKS // WAVES
     copies = []
-    for g in range(2):
-        for p in range(g * half, (g + 1) * half):
-            slots_ref[p] = blocks_ref[rows_ref[p]]
-        copies.append(begin(slots_ref.at[pl.ds(g * half, half)], out_ref.at[pl.ds(g * half, half)], sems.at[g]))
+    for g in range(WAVES):
+        for copy in coming[g * ready : (g + 1) * ready]:
+            copy.wait()
+        for p in range(g * some, (g + 1) * some):
+            slots[p] = mm(blocks[rows_ref[0, p]], tiles[p]).astype(BF16)
+        copies.append(begin(slots.at[pl.ds(g * some, some)], out_ref.at[pl.ds(g * some, some)], sems.at[g]))
     return copies
 
 
-def start_kernel(rows_ref, vec_ref, cur_ref, out_ref, slots, sems):
-    width = cur_ref.shape[2]
-    for r in range(cur_ref.shape[0]):
-        cur_ref[r] = vec_ref[:, r * width : (r + 1) * width]
-    for copy in spread(rows_ref, cur_ref, slots, out_ref, sems):
+def receive(rows_ref, arrived_ref, acc):
+    acc[...] = jnp.zeros(acc.shape, F32)
+    for p in range(arrived_ref.shape[0]):
+        acc[rows_ref[0, p]] += arrived_ref[p].astype(F32)
+
+
+def start_kernel(rows_ref, vec_ref, tiles_ref, cur_ref, out_ref, tiles, vec, block, slots, loads, sems):
+    first = begin(vec_ref, vec, sems.at[WAVES])
+    coming = load(tiles_ref, tiles, loads)
+    first.wait()
+    width = block.shape[2]
+    for r in range(block.shape[0]):
+        block[r] = vec[:, r * width : (r + 1) * width]
+    going = [begin(block, cur_ref, sems.at[WAVES])]
+    going += send(rows_ref, block, tiles, coming, slots, out_ref, sems)
+    for copy in going:
         copy.wait()
-
-
-def tile_kernel(tiles_ref, out_ref):
-    def step(i, _):
-        for u in range(4):
-            out_ref[i * 4 + u] = tiles_ref[i * 4 + u].T
-        return _
-
-    lax.fori_loop(0, out_ref.shape[0] // 4, step, 0)
 
 
 def local_kernel(mode, first_ref, second_ref, count_ref, *refs):
@@ -117,27 +127,14 @@
     lax.fori_loop(0, lax.div(count + (group - 1), group), step, 0)
 
 
-def halo_sums(rows_ref, arrived_ref, tiles_ref, acc_ref):
-    parts = []
-    for p in range(arrived_ref.shape[0]):
-        parts.append((rows_ref[p], mm(arrived_ref[p], tiles_ref[p])))
-        if len(parts) > 8:
-            at, value = parts.pop(0)
-            acc_ref[at] += value
-    for at, value in parts:
-        acc_ref[at] += value
-
-
-def halo_kernel(factor, rows_ref, arrived_ref, tiles_ref, part_ref, cur_ref, out_ref, tiles, part, acc, block, slots, sems):
-    coming = begin(tiles_ref, tiles, sems.at[0])
-    also = begin(part_ref, part, sems.at[1])
-    acc[...] = jnp.zeros(acc.shape, F32)
-    coming.wait()
-    halo_sums(rows_ref, arrived_ref, tiles, acc)
+def halo_kernel(factor, rows_ref, arrived_ref, tiles_ref, part_ref, cur_ref, out_ref, tiles, part, acc, block, slots, loads, sems):
+    also = begin(part_ref, part, sems.at[WAVES])
+    coming = load(tiles_ref, tiles, loads)
+    receive(rows_ref, arrived_ref, acc)
     also.wait()
     block[...] = (factor * (acc[...] + part[...])).astype(BF16)
-    going = [begin(block, cur_ref, sems.at[2])]
-    going += spread(rows_ref, block, slots, out_ref, sems)
+    going = [begin(block, cur_ref, sems.at[WAVES])]
+    going += send(rows_ref, block, tiles, coming, slots, out_ref, sems)
     for copy in going:
         copy.wait()
 
@@ -150,21 +147,43 @@
     gram_ref[...] = value
 
 
-def sums_kernel(keep, rows_ref, arrived_ref, tiles_ref, part_ref, cur_ref, gram_ref, *refs):
+def corner(n):
+    return lax.broadcasted_iota(jnp.int32, (n, n), 0), lax.broadcasted_iota(jnp.int32, (n, n), 1)
+
+
+def packed(gram, product):
+    n = gram.shape[0]
+    row, col = corner(n)
+    both = jnp.where(col >= row, gram, product)
+    diagonal = jnp.sum(jnp.where(row == col, product, 0.0), axis=0, keepdims=True)
+    last = jnp.concatenate([diagonal, jnp.zeros((1, n), F32)], axis=1)
+    top = jnp.concatenate([both[: n // 2], both[n // 2 :]], axis=1)
+    return jnp.concatenate([top, jnp.broadcast_to(last, (8, 2 * n))], axis=0)
+
+
+def unpacked(sums):
+    n = sums.shape[1] // 2
+    row, col = corner(n)
+    both = jnp.concatenate([sums[: n // 2, :n], sums[: n // 2, n:]], axis=0)
+    turned = both.T
+    diagonal = sums[n // 2 : n // 2 + 1, :n]
+    gram = jnp.where(col >= row, both, turned)
+    product = jnp.where(col < row, both, jnp.where(row == col, jnp.broadcast_to(diagonal, (n, n)), turned))
+    return gram, product
+
+
+def sums_kernel(keep, rows_ref, arrived_ref, part_ref, cur_ref, gram_ref, *refs):
     if keep:
-        image_ref, sums_ref, tiles, acc, halo, cur, sems = refs
+        image_ref, sums_ref, part, acc, cur, sems = refs
     else:
-        sums_ref, tiles, acc, halo, cur, sems = refs
-    coming = begin(tiles_ref, tiles, sems.at[0])
-    also = begin(part_ref, acc, sems.at[1])
-    more = begin(cur_ref, cur, sems.at[2])
-    halo[...] = jnp.zeros(halo.shape, F32)
-    coming.wait()
-    halo_sums(rows_ref, arrived_ref, tiles, halo)
+        sums_ref, part, acc, cur, sems = refs
+    also = begin(part_ref, part, sems.at[0])
+    more = begin(cur_ref, cur, sems.at[1])
+    receive(rows_ref, arrived_ref, acc)
     also.wait()
-    acc[...] += halo[...]
+    acc[...] += part[...]
     if keep:
-        going = begin(acc, image_ref, sems.at[0])
+        going = begin(acc, image_ref, sems.at[2])
     more.wait()
     k = gram_ref.shape[0]
     value = jnp.zeros((k, k), F32)
@@ -172,7 +191,7 @@
         block = cur[r]
         for third in thirds(acc[r]):
             value = value + mm_t(block, third)
-    sums_ref[...] = jnp.concatenate([gram_ref[...], value], axis=1)
+    sums_ref[...] = packed(gram_ref[...], value)
     if keep:
         going.wait()
 
@@ -202,38 +221,41 @@
     return mm(parts[0], block) + (mm(parts[1], block) + mm(parts[2], block))
 
 
-def turn_kernel(total, rows_ref, sums_ref, cur_ref, image_ref, next_ref, y_ref, out_ref, centre_ref, cur, image, start, block, slots, sems):
-    coming = begin(cur_ref, cur, sems.at[0])
-    also = begin(image_ref, image, sems.at[1])
-    k = sums_ref.shape[0]
-    inverse = inverse_factor(sums_ref[:, :k] / total)
-    half = jnp.dot(inverse, sums_ref[:, k:] / total, precision=HI, preferred_element_type=F32)
-    centre = jnp.sum(half * inverse) / k - 1.0
+def turn_kernel(total, rows_ref, sums_ref, cur_ref, image_ref, tiles_ref, next_ref, y_ref, out_ref, centre_ref, *scratch):
+    cur, image, begun, block, tiles, slots, loads, sems = scratch
+    first = begin(cur_ref, cur, sems.at[0])
+    second = begin(image_ref, image, sems.at[1])
+    coming = load(tiles_ref, tiles, loads)
+    gram, product = unpacked(sums_ref[...])
+    inverse = inverse_factor(gram / total)
+    half = jnp.dot(inverse, product / total, precision=HI, preferred_element_type=F32)
+    centre = jnp.sum(half * inverse) / inverse.shape[0] - 1.0
     centre_ref[0, 0] = centre
     parts = thirds(inverse)
-    coming.wait()
-    also.wait()
+    first.wait()
+    second.wait()
     for r in range(cur.shape[0]):
-        begun = apply_square(parts, cur[r]).astype(BF16)
-        start[r] = begun
+        value = apply_square(parts, cur[r]).astype(BF16)
+        begun[r] = value
         turned = jnp.dot(inverse, image[r], precision=HI, preferred_element_type=F32)
-        block[r] = (turned - centre * begun.astype(F32)).astype(BF16)
-    going = [begin(start, next_ref, sems.at[2]), begin(block, y_ref, sems.at[3])]
-    going += spread(rows_ref, block, slots, out_ref, sems)
+        block[r] = (turned - centre * value.astype(F32)).astype(BF16)
+    going = [begin(begun, next_ref, sems.at[WAVES]), begin(block, y_ref, sems.at[WAVES + 1])]
+    going += send(rows_ref, block, tiles, coming, slots, out_ref, sems)
     for copy in going:
         copy.wait()
 
 
 def end_kernel(total, sums_ref, cur_ref, basis_ref, ritz_ref, cur, sems):
     coming = begin(cur_ref, cur, sems.at[0])
-    k, width = sums_ref.shape[0], cur.shape[2]
-    inverse = inverse_factor(sums_ref[:, :k] / total)
-    half = jnp.dot(inverse, sums_ref[:, k:] / total, precision=HI, preferred_element_type=F32)
-    ritz_ref[...] = mm_t(half, inverse, HI)
+    width = cur.shape[2]
+    gram, product = unpacked(sums_ref[...])
+    inverse = inverse_factor(gram / total)
     parts = thirds(inverse)
     coming.wait()
     for r in range(cur.shape[0]):
         basis_ref[:, r * width : (r + 1) * width] = apply_square(parts, cur[r]).astype(BF16)
+    half = jnp.dot(inverse, product / total, precision=HI, preferred_element_type=F32)
+    ritz_ref[...] = mm_t(half, inverse, HI)
 
 
 def local(vectors, diag_tiles, pair_tiles, halo_tiles, halo_rows, pair_index, pair_count):
@@ -241,7 +263,6 @@
     blocks, size, _ = diag_tiles.shape
     edges, peers = pair_index.shape[1], halo_rows.shape[1]
     total = float(own_rows * peers)
-    rows = halo_rows[0]
     index = ((pair_index[0, :, 0], "s"), (pair_index[0, :, 1], "s"), (pair_count, "s"))
     block, spots, square = (blocks, k, size), (peers, k, size), (k, k)
     pair_tiles = pair_tiles.reshape(edges, 2, size, size)
@@ -250,8 +271,7 @@
     def room(shape, dtype):
         return pltpu.VMEM(shape, dtype)
 
-    sems = pltpu.SemaphoreType.DMA((4,))
-    [tiles] = call(tile_kernel, [((peers, size, size), BF16, "h")], [(halo_tiles, "h")], 1 << 20, 8 << 20)
+    loads, sems = pltpu.SemaphoreType.DMA((CHUNKS,)), pltpu.SemaphoreType.DMA((WAVES + 2,))
 
     def exchange(out):
         return lax.all_to_all(out, "dom", 0, 0, tiled=True)
@@ -265,10 +285,10 @@
         return call(
             functools.partial(halo_kernel, factor),
             [(block, BF16, "a"), (spots, BF16, "a")],
-            [(rows, "s"), (arrived, "v"), (tiles, "a"), (part, "a")],
+            [(halo_rows, "s"), (arrived, "v"), (halo_tiles, "a"), (part, "a")],
             unit * peers,
             10 << 20,
-            [room(tiles.shape, BF16), room(block, F32), room(block, F32), room(block, BF16), room(spots, BF16), sems],
+            [room(halo_tiles.shape, BF16), room(block, F32), room(block, F32), room(block, BF16), room(spots, BF16), loads, sems],
         )
 
     def everywhere(x):
@@ -281,9 +301,9 @@
 
     def sums(cur, arrived, part, keep):
         [gram] = call(gram_kernel, [(square, F32, "h")], [(cur, "h")], 2 * k * k * own_rows, 1 << 20)
-        outs = [(block, F32, "a")] * keep + [((k, 2 * k), F32, "h")]
-        ins = [(rows, "s"), (arrived, "v"), (tiles, "a"), (part, "a"), (cur, "a"), (gram, "h")]
-        scratch = [room(tiles.shape, BF16), room(block, F32), room(block, F32), room(block, BF16), sems]
+        outs = [(block, F32, "a")] * keep + [((k // 2 + 8, 2 * k), F32, "h")]
+        ins = [(halo_rows, "s"), (arrived, "v"), (part, "a"), (cur, "a"), (gram, "h")]
+        scratch = [room(block, F32), room(block, F32), room(block, BF16), sems]
         *image, value = call(functools.partial(sums_kernel, keep), outs, ins, unit * peers, 10 << 20, scratch)
         return *image, everywhere(value)
 
@@ -296,11 +316,11 @@
 
     start, out = call(
         start_kernel,
-        [(block, BF16, "h"), (spots, BF16, "a")],
-        [(rows, "s"), (vectors, "h")],
-        1 << 20,
-        4 << 20,
-        [room(spots, BF16), sems],
+        [(block, BF16, "a"), (spots, BF16, "a")],
+        [(halo_rows, "s"), (vectors, "a"), (halo_tiles, "a")],
+        unit * peers,
+        8 << 20,
+        [room(halo_tiles.shape, BF16), room(vectors.shape, BF16), room(block, BF16), room(spots, BF16), loads, sems],
     )
     arrived = exchange(out)
     cur, out = halo(1.0, arrived, own("start", start))
@@ -311,10 +331,11 @@
     begun, cur, out, centre = call(
         functools.partial(turn_kernel, total),
         [(block, BF16, "a"), (block, BF16, "a"), (spots, BF16, "a"), ((1, 1), F32, "s")],
-        [(rows, "s"), (value, "h"), (cur, "a"), (image, "a")],
+        [(halo_rows, "s"), (value, "h"), (cur, "a"), (image, "a"), (halo_tiles, "a")],
         1 << 24,
         4 << 20,
-        [room(block, BF16), room(block, F32), room(block, BF16), room(block, BF16), room(spots, BF16), sems],
+        [room(block, BF16), room(block, F32), room(block, BF16), room(block, BF16)]
+        + [room(halo_tiles.shape, BF16), room(spots, BF16), loads, sems],
     )
     cur, out = filtered(begun, cur, out, centre)
 

time: 451 us -> 437 us (0.969)
  Pallas kernels: 108 us -> 98.8 us
  blocking collectives: 48 us -> 41.9 us
    pallas_call x24 -> x23, Pallas kernels: 108 us -> 98.8 us  [call(): pl.pallas_call(body, out_shape=[(place[kind] if kind in place else jax.Sh...]
    all_to_all x4, blocking collectives: 48 us -> 41.9 us  [everywhere(): lax.all_to_all(many, 'dom', 0, 0, axis_index_groups=groups, tiled=True)]
    unnamed x84 -> x76, local copies, waits for them, and re-layouts: 50.1 us -> 50.1 us
  transfers between devices with their start and end apart: 9 -> 9, of which waited for: 9 -> 9; matrix products, arithmetic and copies ran while one was open for 0% -> 0% of each run, Pallas kernels for 8% -> 7%
where the time goes in v4:
time: 437 us; the launch traced here: 435 us
  waiting for transfers between devices  192 us (44%)
  Pallas kernels  98.8 us (23%)
  local copies, waits for them, and re-layouts  50.1 us (11%)
  starting transfers between devices  50 us (11%)
  blocking collectives  41.9 us (10%)
    all_to_all x9, waiting for transfers between devices, exchange(): return lax.all_to_all(out, 'dom', 0, 0, tiled=True)  192 us
    pallas_call x23, Pallas kernels, call(): pl.pallas_call(body, out_shape=[(place[kind] if kind in place else jax.Sh...  98.8 us
    unnamed x76, local copies, waits for them, and re-layouts  50.1 us
    all_to_all x9, starting transfers between devices, exchange(): return lax.all_to_all(out, 'dom', 0, 0, tiled=True)  50 us
    all_to_all x4, blocking collectives, everywhere(): lax.all_to_all(many, 'dom', 0, 0, axis_index_groups=groups, tiled=True)  41.9 us
  transfers between devices with their start and end apart: 9, of which 9 were waited for; matrix products, arithmetic and copies ran while one was open for 0% of the time, Pallas kernels for 7%

profile of v4, /device:TPU:0, one launch (start us, length us, event | category | flops | bytes accessed | tf_op | source)
XLA Modules:
  0.0 434.6 jit_solution(6210117930154538118)
XLA Ops:
  1.3 5.4 %shard_map.86 = (bf16[32,64,128]{2,1,0:T(8,128)(2,1)}, bf16[128,64,128]{2,1,0:T(8,128)(2,1)}) custom-call(s32[1,128]{1,0:T(1,128)S(1)} %copy-done.35, bf16[64,4096]{1,0:T(8,128)(2,1)} %vec_ref.1, bf16[128,128,128]{2,1,0:T(8,128)(2,1)} %tiles_ref.17), custom_call_target="tpu_custom_call" | custom-call | flops 268435456 | bytes 8388608 | tf_op jit(solution)/shard_map/pallas_call | solution.py:25
  6.7 11.2 %all-to-all-start = ((bf16[128,64,128]{2,1,0:T(8,128)(2,1)}), bf16[128,64,128]{2,1,0:T(8,128)(2,1)S(1)}, u32[]{:S(2)}, u32[]{:S(2)}) async-start(bf16[128,64,128]{2,1,0:T(8,128)(2,1)} %get-tuple-element.24), calls=%async_computation | async-start | bytes 4194304 | tf_op jit(solution)/shard_map/all_to_all | solution.py:277
  18.6 2.8 copy-done
  22.4 3.2 shard_map.87.part_ref
  26.5 21.8 %all-to-all-done.arrived_ref = bf16[128,64,128]{2,1,0:T(8,128)(2,1)S(1)} async-done(((bf16[128,64,128]{2,1,0:T(8,128)(2,1)}), bf16[128,64,128]{2,1,0:T(8,128)(2,1)S(1)}, u32[]{:S(2)}, u32[]{:S(2)}) %all-to-all-start) | async-done | bytes 2097184 | tf_op jit(solution)/shard_map/all_to_all | solution.py:277
  48.3 5.6 %shard_map.88 = (bf16[32,64,128]{2,1,0:T(8,128)(2,1)}, bf16[128,64,128]{2,1,0:T(8,128)(2,1)}) custom-call(s32[1,128]{1,0:T(1,128)S(1)} %copy-done.36, bf16[128,64,128]{2,1,0:T(8,128)(2,1)S(1)} %all-to-all-done.arrived_ref, bf16[128,128,128]{2,1,0:T(8,128)(2,1)} %tiles_ref.17, f32[32,64,128]{2,1,0:T(8,128)} %copy-done.21), custom_call_target="tpu_custom_call" | custom-call | flops 268435456 | bytes 10485760 | tf_op jit(solution)/shard_map/pallas_call | solution.py:25
  53.9 4.7 %all-to-all-start.1 = ((bf16[128,64,128]{2,1,0:T(8,128)(2,1)}), bf16[128,64,128]{2,1,0:T(8,128)(2,1)S(1)}, u32[]{:S(2)}, u32[]{:S(2)}) async-start(bf16[128,64,128]{2,1,0:T(8,128)(2,1)} %get-tuple-element.26), calls=%async_computation.1 | async-start | bytes 4194304 | tf_op jit(solution)/shard_map/all_to_all | solution.py:277
  58.6 2.8 copy-done.1
  63.4 3.2 shard_map.89.part_ref
  67.6 21.4 %all-to-all-done.1.arrived_ref = bf16[128,64,128]{2,1,0:T(8,128)(2,1)S(1)} async-done(((bf16[128,64,128]{2,1,0:T(8,128)(2,1)}), bf16[128,64,128]{2,1,0:T(8,128)(2,1)S(1)}, u32[]{:S(2)}, u32[]{:S(2)}) %all-to-all-start.1) | async-done | bytes 2097184 | tf_op jit(solution)/shard_map/all_to_all | solution.py:277
  89.0 5.6 %shard_map.90 = (bf16[32,64,128]{2,1,0:T(8,128)(2,1)}, bf16[128,64,128]{2,1,0:T(8,128)(2,1)}) custom-call(s32[1,128]{1,0:T(1,128)S(1)} %copy-done.36, bf16[128,64,128]{2,1,0:T(8,128)(2,1)S(1)} %all-to-all-done.1.arrived_ref, bf16[128,128,128]{2,1,0:T(8,128)(2,1)} %tiles_ref.17, f32[32,64,128]{2,1,0:T(8,128)} %copy-done.17), custom_call_target="tpu_custom_call" | custom-call | flops 268435456 | bytes 10485760 | tf_op jit(solution)/shard_map/pallas_call | solution.py:25
  94.6 4.7 %all-to-all-start.2 = ((bf16[128,64,128]{2,1,0:T(8,128)(2,1)}), bf16[128,64,128]{2,1,0:T(8,128)(2,1)S(1)}, u32[]{:S(2)}, u32[]{:S(2)}) async-start(bf16[128,64,128]{2,1,0:T(8,128)(2,1)} %get-tuple-element.28), calls=%async_computation.2 | async-start | bytes 4194304 | tf_op jit(solution)/shard_map/all_to_all | solution.py:277
  99.3 2.8 copy-done.2
  104.1 3.2 shard_map.91.part_ref
  108.3 21.4 %all-to-all-done.2.arrived_ref = bf16[128,64,128]{2,1,0:T(8,128)(2,1)S(1)} async-done(((bf16[128,64,128]{2,1,0:T(8,128)(2,1)}), bf16[128,64,128]{2,1,0:T(8,128)(2,1)S(1)}, u32[]{:S(2)}, u32[]{:S(2)}) %all-to-all-start.2) | async-done | bytes 2097184 | tf_op jit(solution)/shard_map/all_to_all | solution.py:277
  129.7 5.6 %shard_map.92 = (bf16[32,64,128]{2,1,0:T(8,128)(2,1)}, bf16[128,64,128]{2,1,0:T(8,128)(2,1)}) custom-call(s32[1,128]{1,0:T(1,128)S(1)} %copy-done.36, bf16[128,64,128]{2,1,0:T(8,128)(2,1)S(1)} %all-to-all-done.2.arrived_ref, bf16[128,128,128]{2,1,0:T(8,128)(2,1)} %tiles_ref.17, f32[32,64,128]{2,1,0:T(8,128)} %copy-done.18), custom_call_target="tpu_custom_call" | custom-call | flops 268435456 | bytes 10485760 | tf_op jit(solution)/shard_map/pallas_call | solution.py:25
  135.3 4.7 %all-to-all-start.3 = ((bf16[128,64,128]{2,1,0:T(8,128)(2,1)}), bf16[128,64,128]{2,1,0:T(8,128)(2,1)S(1)}, u32[]{:S(2)}, u32[]{:S(2)}) async-start(bf16[128,64,128]{2,1,0:T(8,128)(2,1)} %get-tuple-element.30), calls=%async_computation.3 | async-start | bytes 4194304 | tf_op jit(solution)/shard_map/all_to_all | solution.py:277
  144.9 3.4 shard_map.93.part_ref
  149.2 21.2 %all-to-all-done.3.arrived_ref = bf16[128,64,128]{2,1,0:T(8,128)(2,1)S(1)} async-done(((bf16[128,64,128]{2,1,0:T(8,128)(2,1)}), bf16[128,64,128]{2,1,0:T(8,128)(2,1)S(1)}, u32[]{:S(2)}, u32[]{:S(2)}) %all-to-all-start.3) | async-done | bytes 2097184 | tf_op jit(solution)/shard_map/all_to_all | solution.py:277
  170.4 5.6 %shard_map.94 = (bf16[32,64,128]{2,1,0:T(8,128)(2,1)}, bf16[128,64,128]{2,1,0:T(8,128)(2,1)}) custom-call(s32[1,128]{1,0:T(1,128)S(1)} %copy-done.36, bf16[128,64,128]{2,1,0:T(8,128)(2,1)S(1)} %all-to-all-done.3.arrived_ref, bf16[128,128,128]{2,1,0:T(8,128)(2,1)} %tiles_ref.17, f32[32,64,128]{2,1,0:T(8,128)} %copy-done.15), custom_call_target="tpu_custom_call" | custom-call | flops 268435456 | bytes 10485760 | tf_op jit(solution)/shard_map/pallas_call | solution.py:25
  176.0 4.7 %all-to-all-start.4 = ((bf16[128,64,128]{2,1,0:T(8,128)(2,1)}), bf16[128,64,128]{2,1,0:T(8,128)(2,1)S(1)}, u32[]{:S(2)}, u32[]{:S(2)}) async-start(bf16[128,64,128]{2,1,0:T(8,128)(2,1)} %get-tuple-element.32), calls=%async_computation.4 | async-start | bytes 4194304 | tf_op jit(solution)/shard_map/all_to_all | solution.py:277
  182.1 2.8 copy-done.4
  186.0 3.1 shard_map.95.part_ref
  190.1 21.0 %all-to-all-done.4.arrived_ref = bf16[128,64,128]{2,1,0:T(8,128)(2,1)S(1)} async-done(((bf16[128,64,128]{2,1,0:T(8,128)(2,1)}), bf16[128,64,128]{2,1,0:T(8,128)(2,1)S(1)}, u32[]{:S(2)}, u32[]{:S(2)}) %all-to-all-start.4) | async-done | bytes 2097184 | tf_op jit(solution)/shard_map/all_to_all | solution.py:277
  211.1 3.0 shard_map.97
  214.1 8.9 %all_to_all.65 = f32[8,40,128]{2,1,0:T(8,128)S(1)} all-to-all(f32[8,40,128]{2,1,0:T(8,128)S(1)} %broadcast_in_dim.8), channel_id=1, replica_groups={{0,1,2,3,4,5,6,7},{8,9,10,11,12,13,14,15},{16,17,18,19,20,21,22,23},{24..., dimensions={0} | all-to-all | bytes 327680 | tf_op jit(solution)/shard_map/all_to_all | solution.py:299
  223.0 12.1 %all_to_all.66 = f32[16,40,128]{2,1,0:T(8,128)S(1)} all-to-all(f32[16,40,128]{2,1,0:T(8,128)S(1)} %broadcast_in_dim.9), channel_id=1, replica_groups={{0,8,16,24,32,40,48,56,64,72,80,88,96,104,112,120},{1,9,17,25,33,41,49,..., dimensions={0} | all-to-all | bytes 655360 | tf_op jit(solution)/shard_map/all_to_all | solution.py:299
  235.1 10.3 %shard_map.98 = (bf16[32,64,128]{2,1,0:T(8,128)(2,1)}, bf16[32,64,128]{2,1,0:T(8,128)(2,1)}, bf16[128,64,128]{2,1,0:T(8,128)(2,1)}, f32[1,1]{1,0:T(1,128)}) custom-call(s32[1,128]{1,0:T(1,128)S(1)} %copy-done.36, f32[40,128]{1,0:T(8,128)S(1)} %reduce_sum.37.sums_ref, bf16[32,64,128]{2,1,0:T(8,128)(2,1)} %get-tuple-element.33.refs_0_.cur_ref, ...), custom_call_target="tpu_custom_call" | custom-call | flops 16777216 | bytes 4194304 | tf_op jit(solution)/shard_map/pallas_call | solution.py:25
  245.4 4.7 %all-to-all-start.7 = ((bf16[128,64,128]{2,1,0:T(8,128)(2,1)}), bf16[128,64,128]{2,1,0:T(8,128)(2,1)S(1)}, u32[]{:S(2)}, u32[]{:S(2)}) async-start(bf16[128,64,128]{2,1,0:T(8,128)(2,1)} %get-tuple-element.36), calls=%async_computation.7 | async-start | bytes 4194304 | tf_op jit(solution)/shard_map/all_to_all | solution.py:277
  255.0 3.8 shard_map.99.part_ref
  259.8 20.8 %all-to-all-done.7.arrived_ref = bf16[128,64,128]{2,1,0:T(8,128)(2,1)S(1)} async-done(((bf16[128,64,128]{2,1,0:T(8,128)(2,1)}), bf16[128,64,128]{2,1,0:T(8,128)(2,1)S(1)}, u32[]{:S(2)}, u32[]{:S(2)}) %all-to-all-start.7) | async-done | bytes 2097184 | tf_op jit(solution)/shard_map/all_to_all | solution.py:277
  280.6 5.6 %shard_map.100 = (bf16[32,64,128]{2,1,0:T(8,128)(2,1)}, bf16[128,64,128]{2,1,0:T(8,128)(2,1)}) custom-call(s32[1,128]{1,0:T(1,128)S(1)} %copy-done.36, bf16[128,64,128]{2,1,0:T(8,128)(2,1)S(1)} %all-to-all-done.7.arrived_ref, bf16[128,128,128]{2,1,0:T(8,128)(2,1)} %tiles_ref.17, f32[32,64,128]{2,1,0:T(8,128)} %copy-done.19), custom_call_target="tpu_custom_call" | custom-call | flops 268435456 | bytes 10485760 | tf_op jit(solution)/shard_map/pallas_call | solution.py:25
  286.2 4.9 %all-to-all-start.8 = ((bf16[128,64,128]{2,1,0:T(8,128)(2,1)}), bf16[128,64,128]{2,1,0:T(8,128)(2,1)S(1)}, u32[]{:S(2)}, u32[]{:S(2)}) async-start(bf16[128,64,128]{2,1,0:T(8,128)(2,1)} %get-tuple-element.40), calls=%async_computation.8 | async-start | bytes 4194304 | tf_op jit(solution)/shard_map/all_to_all | solution.py:277
  295.9 3.8 shard_map.101.part_ref
  300.7 20.8 %all-to-all-done.8.arrived_ref = bf16[128,64,128]{2,1,0:T(8,128)(2,1)S(1)} async-done(((bf16[128,64,128]{2,1,0:T(8,128)(2,1)}), bf16[128,64,128]{2,1,0:T(8,128)(2,1)S(1)}, u32[]{:S(2)}, u32[]{:S(2)}) %all-to-all-start.8) | async-done | bytes 2097184 | tf_op jit(solution)/shard_map/all_to_all | solution.py:277
  321.5 5.6 %shard_map.102 = (bf16[32,64,128]{2,1,0:T(8,128)(2,1)}, bf16[128,64,128]{2,1,0:T(8,128)(2,1)}) custom-call(s32[1,128]{1,0:T(1,128)S(1)} %copy-done.36, bf16[128,64,128]{2,1,0:T(8,128)(2,1)S(1)} %all-to-all-done.8.arrived_ref, bf16[128,128,128]{2,1,0:T(8,128)(2,1)} %tiles_ref.17, f32[32,64,128]{2,1,0:T(8,128)} %copy-done.20), custom_call_target="tpu_custom_call" | custom-call | flops 268435456 | bytes 10485760 | tf_op jit(solution)/shard_map/pallas_call | solution.py:25
  327.1 4.7 %all-to-all-start.9 = ((bf16[128,64,128]{2,1,0:T(8,128)(2,1)}), bf16[128,64,128]{2,1,0:T(8,128)(2,1)S(1)}, u32[]{:S(2)}, u32[]{:S(2)}) async-start(bf16[128,64,128]{2,1,0:T(8,128)(2,1)} %get-tuple-element.42), calls=%async_computation.9 | async-start | bytes 4194304 | tf_op jit(solution)/shard_map/all_to_all | solution.py:277
  336.6 3.8 shard_map.103.part_ref
  341.4 20.8 %all-to-all-done.9.arrived_ref = bf16[128,64,128]{2,1,0:T(8,128)(2,1)S(1)} async-done(((bf16[128,64,128]{2,1,0:T(8,128)(2,1)}), bf16[128,64,128]{2,1,0:T(8,128)(2,1)S(1)}, u32[]{:S(2)}, u32[]{:S(2)}) %all-to-all-start.9) | async-done | bytes 2097184 | tf_op jit(solution)/shard_map/all_to_all | solution.py:277
  362.2 5.6 %shard_map.104 = (bf16[32,64,128]{2,1,0:T(8,128)(2,1)}, bf16[128,64,128]{2,1,0:T(8,128)(2,1)}) custom-call(s32[1,128]{1,0:T(1,128)S(1)} %copy-done.36, bf16[128,64,128]{2,1,0:T(8,128)(2,1)S(1)} %all-to-all-done.9.arrived_ref, bf16[128,128,128]{2,1,0:T(8,128)(2,1)} %tiles_ref.17, f32[32,64,128]{2,1,0:T(8,128)} %copy-done.16), custom_call_target="tpu_custom_call" | custom-call | flops 268435456 | bytes 10485760 | tf_op jit(solution)/shard_map/pallas_call | solution.py:25
  367.8 5.9 %all-to-all-start.10 = ((bf16[128,64,128]{2,1,0:T(8,128)(2,1)}), bf16[128,64,128]{2,1,0:T(8,128)(2,1)}, u32[]{:S(2)}, u32[]{:S(2)}) async-start(bf16[128,64,128]{2,1,0:T(8,128)(2,1)} %get-tuple-element.44), calls=%async_computation.10 | async-start | bytes 4194304 | tf_op jit(solution)/shard_map/all_to_all | solution.py:277
  374.1 2.8 copy-done.8
  376.9 3.1 shard_map.105.part_ref
  381.1 22.7 %all-to-all-done.10.arrived_ref = bf16[128,64,128]{2,1,0:T(8,128)(2,1)} async-done(((bf16[128,64,128]{2,1,0:T(8,128)(2,1)}), bf16[128,64,128]{2,1,0:T(8,128)(2,1)}, u32[]{:S(2)}, u32[]{:S(2)}) %all-to-all-start.10) | async-done | bytes 2097184 | tf_op jit(solution)/shard_map/all_to_all | solution.py:277
  403.7 4.0 shard_map.107
  407.8 8.9 %all_to_all.67 = f32[8,40,128]{2,1,0:T(8,128)S(1)} all-to-all(f32[8,40,128]{2,1,0:T(8,128)S(1)} %broadcast_in_dim.10), channel_id=1, replica_groups={{0,1,2,3,4,5,6,7},{8,9,10,11,12,13,14,15},{16,17,18,19,20,21,22,23},{24..., dimensions={0} | all-to-all | bytes 327680 | tf_op jit(solution)/shard_map/all_to_all | solution.py:299
  416.7 12.1 %all_to_all.68 = f32[16,40,128]{2,1,0:T(8,128)S(1)} all-to-all(f32[16,40,128]{2,1,0:T(8,128)S(1)} %broadcast_in_dim.11), channel_id=1, replica_groups={{0,8,16,24,32,40,48,56,64,72,80,88,96,104,112,120},{1,9,17,25,33,41,49,..., dimensions={0} | all-to-all | bytes 655360 | tf_op jit(solution)/shard_map/all_to_all | solution.py:299
  428.8 5.6 %shard_map.108 = (bf16[64,4096]{1,0:T(8,128)(2,1)}, f32[64,64]{1,0:T(8,128)}) custom-call(f32[40,128]{1,0:T(8,128)S(1)} %reduce_sum.39.sums_ref, bf16[32,64,128]{2,1,0:T(8,128)(2,1)} %get-tuple-element.45.refs_0_.cur_ref), custom_call_target="tpu_custom_call" | custom-call | flops 16777216 | bytes 2097152 | tf_op jit(solution)/shard_map/pallas_call | solution.py:25
  (82 shorter events, 37.1 us)
Async XLA Ops:
  0.6 0.7 copy-start.35
  6.7 11.8 %copy-start.37 = (s32[1,96,2]{1,2,0:T(2,128)S(1)}, s32[1,96,2]{1,2,0:T(2,128)}, u32[]{:S(2)}) copy-start(s32[1,96,2]{1,2,0:T(2,128)} %param.12) | copy-start | bytes 2308
  6.7 11.8 %copy-start.9 = (bf16[32,128,128]{2,1,0:T(8,128)(2,1)S(1)}, bf16[32,128,128]{2,1,0:T(8,128)(2,1)}, u32[]{:S(2)}) copy-start(bf16[32,128,128]{2,1,0:T(8,128)(2,1)} %refs_1_.5) | copy-start | bytes 3145732
  6.7 41.6 %all-to-all-start = ((bf16[128,64,128]{2,1,0:T(8,128)(2,1)}), bf16[128,64,128]{2,1,0:T(8,128)(2,1)S(1)}, u32[]{:S(2)}, u32[]{:S(2)}) async-start(bf16[128,64,128]{2,1,0:T(8,128)(2,1)} %get-tuple-element.24), calls=%async_computation | async-start | bytes 4194304 | tf_op jit(solution)/shard_map/all_to_all | solution.py:277
  18.5 2.8 copy-start
  21.3 1.0 copy-start.22
  22.4 25.9 %copy-start.36 = (s32[1,128]{1,0:T(1,128)S(1)}, s32[1,128]{1,0:T(1,128)}, u32[]{:S(2)}) copy-start(s32[1,128]{1,0:T(1,128)} %rows_ref.21) | copy-start | bytes 1540
  25.5 1.0 copy-start.21
  53.9 35.1 %all-to-all-start.1 = ((bf16[128,64,128]{2,1,0:T(8,128)(2,1)}), bf16[128,64,128]{2,1,0:T(8,128)(2,1)S(1)}, u32[]{:S(2)}, u32[]{:S(2)}) async-start(bf16[128,64,128]{2,1,0:T(8,128)(2,1)} %get-tuple-element.26), calls=%async_computation.1 | async-start | bytes 4194304 | tf_op jit(solution)/shard_map/all_to_all | solution.py:277
  58.6 2.8 copy-start.1
  61.4 1.0 copy-start.23
  62.4 1.0 copy-start.30
  66.6 1.0 copy-start.17
  94.6 35.1 %all-to-all-start.2 = ((bf16[128,64,128]{2,1,0:T(8,128)(2,1)}), bf16[128,64,128]{2,1,0:T(8,128)(2,1)S(1)}, u32[]{:S(2)}, u32[]{:S(2)}) async-start(bf16[128,64,128]{2,1,0:T(8,128)(2,1)} %get-tuple-element.28), calls=%async_computation.2 | async-start | bytes 4194304 | tf_op jit(solution)/shard_map/all_to_all | solution.py:277
  99.3 2.8 copy-start.2
  102.1 1.0 copy-start.26
  103.1 1.0 copy-start.31
  107.3 1.0 copy-start.18
  135.3 35.1 %all-to-all-start.3 = ((bf16[128,64,128]{2,1,0:T(8,128)(2,1)}), bf16[128,64,128]{2,1,0:T(8,128)(2,1)S(1)}, u32[]{:S(2)}, u32[]{:S(2)}) async-start(bf16[128,64,128]{2,1,0:T(8,128)(2,1)} %get-tuple-element.30), calls=%async_computation.3 | async-start | bytes 4194304 | tf_op jit(solution)/shard_map/all_to_all | solution.py:277
  140.0 2.8 copy-start.3
  142.8 1.0 copy-start.27
  143.8 1.0 copy-start.33
  148.2 1.0 copy-start.15
  176.0 35.1 %all-to-all-start.4 = ((bf16[128,64,128]{2,1,0:T(8,128)(2,1)}), bf16[128,64,128]{2,1,0:T(8,128)(2,1)S(1)}, u32[]{:S(2)}, u32[]{:S(2)}) async-start(bf16[128,64,128]{2,1,0:T(8,128)(2,1)} %get-tuple-element.32), calls=%async_computation.4 | async-start | bytes 4194304 | tf_op jit(solution)/shard_map/all_to_all | solution.py:277
  180.7 1.0 copy-start.11
  182.1 2.8 copy-start.4
  184.9 1.0 copy-start.12
  189.1 1.0 copy-start.14
  245.4 35.1 %all-to-all-start.7 = ((bf16[128,64,128]{2,1,0:T(8,128)(2,1)}), bf16[128,64,128]{2,1,0:T(8,128)(2,1)S(1)}, u32[]{:S(2)}, u32[]{:S(2)}) async-start(bf16[128,64,128]{2,1,0:T(8,128)(2,1)} %get-tuple-element.36), calls=%async_computation.7 | async-start | bytes 4194304 | tf_op jit(solution)/shard_map/all_to_all | solution.py:277
  250.1 2.8 copy-start.5
  252.9 1.0 copy-start.24
  254.0 1.0 copy-start.32
  258.8 1.0 copy-start.19
  286.2 35.3 %all-to-all-start.8 = ((bf16[128,64,128]{2,1,0:T(8,128)(2,1)}), bf16[128,64,128]{2,1,0:T(8,128)(2,1)S(1)}, u32[]{:S(2)}, u32[]{:S(2)}) async-start(bf16[128,64,128]{2,1,0:T(8,128)(2,1)} %get-tuple-element.40), calls=%async_computation.8 | async-start | bytes 4194304 | tf_op jit(solution)/shard_map/all_to_all | solution.py:277
  291.0 2.8 copy-start.6
  293.8 1.0 copy-start.25
  294.9 1.0 copy-start.28
  299.7 1.0 copy-start.20
  327.1 35.1 %all-to-all-start.9 = ((bf16[128,64,128]{2,1,0:T(8,128)(2,1)}), bf16[128,64,128]{2,1,0:T(8,128)(2,1)S(1)}, u32[]{:S(2)}, u32[]{:S(2)}) async-start(bf16[128,64,128]{2,1,0:T(8,128)(2,1)} %get-tuple-element.42), calls=%async_computation.9 | async-start | bytes 4194304 | tf_op jit(solution)/shard_map/all_to_all | solution.py:277
  331.7 2.8 copy-start.7
  334.5 1.0 copy-start.29
  335.6 1.0 copy-start.34
  340.4 1.0 copy-start.16
  367.8 5.9 %copy-start.10 = (bf16[32,64,128]{2,1,0:T(8,128)(2,1)S(1)}, bf16[32,64,128]{2,1,0:T(8,128)(2,1)}, u32[]{:S(2)}) copy-start(bf16[32,64,128]{2,1,0:T(8,128)(2,1)} %get-tuple-element.45.refs_0_.cur_ref) | copy-start | bytes 1572868
  367.8 35.9 %all-to-all-start.10 = ((bf16[128,64,128]{2,1,0:T(8,128)(2,1)}), bf16[128,64,128]{2,1,0:T(8,128)(2,1)}, u32[]{:S(2)}, u32[]{:S(2)}) async-start(bf16[128,64,128]{2,1,0:T(8,128)(2,1)} %get-tuple-element.44), calls=%async_computation.10 | async-start | bytes 4194304 | tf_op jit(solution)/shard_map/all_to_all | solution.py:277
  374.1 2.8 copy-start.8
  380.1 1.0 copy-start.13

commit v5 on v4

--- a/solution.py
+++ b/solution.py
@@ -78,13 +78,13 @@
 
 
 def start_kernel(rows_ref, vec_ref, tiles_ref, cur_ref, out_ref, tiles, vec, block, slots, loads, sems):
-    first = begin(vec_ref, vec, sems.at[WAVES])
+    first = begin(vec_ref, vec, loads.at[CHUNKS])
     coming = load(tiles_ref, tiles, loads)
     first.wait()
     width = block.shape[2]
     for r in range(block.shape[0]):
         block[r] = vec[:, r * width : (r + 1) * width]
-    going = [begin(block, cur_ref, sems.at[WAVES])]
+    going = [begin(block, cur_ref, loads.at[CHUNKS + 1])]
     going += send(rows_ref, block, tiles, coming, slots, out_ref, sems)
     for copy in going:
         copy.wait()
@@ -128,12 +128,12 @@
 
 
 def halo_kernel(factor, rows_ref, arrived_ref, tiles_ref, part_ref, cur_ref, out_ref, tiles, part, acc, block, slots, loads, sems):
-    also = begin(part_ref, part, sems.at[WAVES])
+    also = begin(part_ref, part, loads.at[CHUNKS])
     coming = load(tiles_ref, tiles, loads)
     receive(rows_ref, arrived_ref, acc)
     also.wait()
     block[...] = (factor * (acc[...] + part[...])).astype(BF16)
-    going = [begin(block, cur_ref, sems.at[WAVES])]
+    going = [begin(block, cur_ref, loads.at[CHUNKS + 1])]
     going += send(rows_ref, block, tiles, coming, slots, out_ref, sems)
     for copy in going:
         copy.wait()
@@ -186,12 +186,10 @@
         going = begin(acc, image_ref, sems.at[2])
     more.wait()
     k = gram_ref.shape[0]
-    value = jnp.zeros((k, k), F32)
+    value = jnp.zeros((3 * k, k), F32)
     for r in range(acc.shape[0]):
-        block = cur[r]
-        for third in thirds(acc[r]):
-            value = value + mm_t(block, third)
-    sums_ref[...] = packed(gram_ref[...], value)
+        value = value + mm_t(jnp.concatenate(thirds(acc[r]), axis=0), cur[r])
+    sums_ref[...] = packed(gram_ref[...], value[:k] + (value[k : 2 * k] + value[2 * k :]))
     if keep:
         going.wait()
 
@@ -217,27 +215,36 @@
     return work[:, n:] / jnp.sqrt(pivots)
 
 
-def apply_square(parts, block):
-    return mm(parts[0], block) + (mm(parts[1], block) + mm(parts[2], block))
+def apply_square(stack, block):
+    k = stack.shape[1]
+    value = mm(stack, block)
+    return value[:k] + (value[k : 2 * k] + value[2 * k :])
+
+
+def apply_wide(stack, block):
+    k = stack.shape[1]
+    high, middle, low = thirds(block)
+    first, second, third = mm(stack, high), mm(stack[: 2 * k], middle), mm(stack[:k], low)
+    return first[:k] + ((first[k : 2 * k] + second[:k]) + (first[2 * k :] + second[k:] + third))
 
 
 def turn_kernel(total, rows_ref, sums_ref, cur_ref, image_ref, tiles_ref, next_ref, y_ref, out_ref, centre_ref, *scratch):
     cur, image, begun, block, tiles, slots, loads, sems = scratch
-    first = begin(cur_ref, cur, sems.at[0])
-    second = begin(image_ref, image, sems.at[1])
+    first = begin(cur_ref, cur, loads.at[CHUNKS])
+    second = begin(image_ref, image, loads.at[CHUNKS + 1])
     coming = load(tiles_ref, tiles, loads)
     gram, product = unpacked(sums_ref[...])
     inverse = inverse_factor(gram / total)
     half = jnp.dot(inverse, product / total, precision=HI, preferred_element_type=F32)
     centre = jnp.sum(half * inverse) / inverse.shape[0] - 1.0
     centre_ref[0, 0] = centre
-    parts = thirds(inverse)
+    stack = jnp.concatenate(thirds(inverse), axis=0)
     first.wait()
     second.wait()
     for r in range(cur.shape[0]):
-        value = apply_square(parts, cur[r]).astype(BF16)
+        value = apply_square(stack, cur[r]).astype(BF16)
         begun[r] = value
-        turned = jnp.dot(inverse, image[r], precision=HI, preferred_element_type=F32)
+        turned = apply_wide(stack, image[r])
         block[r] = (turned - centre * value.astype(F32)).astype(BF16)
     going = [begin(begun, next_ref, sems.at[WAVES]), begin(block, y_ref, sems.at[WAVES + 1])]
     going += send(rows_ref, block, tiles, coming, slots, out_ref, sems)
@@ -250,10 +257,10 @@
     width = cur.shape[2]
     gram, product = unpacked(sums_ref[...])
     inverse = inverse_factor(gram / total)
-    parts = thirds(inverse)
+    stack = jnp.concatenate(thirds(inverse), axis=0)
     coming.wait()
     for r in range(cur.shape[0]):
-        basis_ref[:, r * width : (r + 1) * width] = apply_square(parts, cur[r]).astype(BF16)
+        basis_ref[:, r * width : (r + 1) * width] = apply_square(stack, cur[r]).astype(BF16)
     half = jnp.dot(inverse, product / total, precision=HI, preferred_element_type=F32)
     ritz_ref[...] = mm_t(half, inverse, HI)
 
@@ -271,7 +278,7 @@
     def room(shape, dtype):
         return pltpu.VMEM(shape, dtype)
 
-    loads, sems = pltpu.SemaphoreType.DMA((CHUNKS,)), pltpu.SemaphoreType.DMA((WAVES + 2,))
+    loads, sems = pltpu.SemaphoreType.DMA((CHUNKS + 2,)), pltpu.SemaphoreType.DMA((WAVES + 2,))
 
     def exchange(out):
         return lax.all_to_all(out, "dom", 0, 0, tiled=True)

time: 437 us -> 428 us (0.979)
  waiting for transfers between devices: 192 us -> 158 us
  Pallas kernels: 98.8 us -> 125 us
    all_to_all x9, waiting for transfers between devices: 192 us -> 158 us  [exchange(): return lax.all_to_all(out, 'dom', 0, 0, tiled=True)]
    pallas_call x23, Pallas kernels: 98.8 us -> 125 us  [call(): pl.pallas_call(body, out_shape=[(place[kind] if kind in place else jax.Sh...]
  transfers between devices with their start and end apart: 9 -> 9, of which waited for: 9 -> 9; matrix products, arithmetic and copies ran while one was open for 0% -> 0% of each run, Pallas kernels for 7% -> 15%
where the time goes in v5:
time: 428 us; the launch traced here: 426 us
  waiting for transfers between devices  158 us (37%)
  Pallas kernels  125 us (29%)
  local copies, waits for them, and re-layouts  50.1 us (12%)
  starting transfers between devices  50 us (12%)
  blocking collectives  41.9 us (10%)
    all_to_all x9, waiting for transfers between devices, exchange(): return lax.all_to_all(out, 'dom', 0, 0, tiled=True)  158 us
    pallas_call x23, Pallas kernels, call(): pl.pallas_call(body, out_shape=[(place[kind] if kind in place else jax.Sh...  125 us
    unnamed x76, local copies, waits for them, and re-layouts  50.1 us
    all_to_all x9, starting transfers between devices, exchange(): return lax.all_to_all(out, 'dom', 0, 0, tiled=True)  50 us
    all_to_all x4, blocking collectives, everywhere(): lax.all_to_all(many, 'dom', 0, 0, axis_index_groups=groups, tiled=True)  41.9 us
  transfers between devices with their start and end apart: 9, of which 9 were waited for; matrix products, arithmetic and copies ran while one was open for 0% of the time, Pallas kernels for 15%

profile of v5, /device:TPU:0, one launch (start us, length us, event | category | flops | bytes accessed | tf_op | source)
XLA Modules:
  0.0 426.2 jit_solution(12909255108822801105)
XLA Ops:
  1.3 4.5 %shard_map.86 = (bf16[32,64,128]{2,1,0:T(8,128)(2,1)}, bf16[128,64,128]{2,1,0:T(8,128)(2,1)}) custom-call(s32[1,128]{1,0:T(1,128)S(1)} %copy-done.35, bf16[64,4096]{1,0:T(8,128)(2,1)} %vec_ref.1, bf16[128,128,128]{2,1,0:T(8,128)(2,1)} %tiles_ref.17), custom_call_target="tpu_custom_call" | custom-call | flops 268435456 | bytes 8388608 | tf_op jit(solution)/shard_map/pallas_call | solution.py:25
  5.8 11.2 %all-to-all-start = ((bf16[128,64,128]{2,1,0:T(8,128)(2,1)}), bf16[128,64,128]{2,1,0:T(8,128)(2,1)S(1)}, u32[]{:S(2)}, u32[]{:S(2)}) async-start(bf16[128,64,128]{2,1,0:T(8,128)(2,1)} %get-tuple-element.24), calls=%async_computation | async-start | bytes 4194304 | tf_op jit(solution)/shard_map/all_to_all | solution.py:284
  21.5 6.9 %shard_map.87.part_ref = f32[32,64,128]{2,1,0:T(8,128)S(1)} custom-call(s32[96]{0:T(128)S(1)} %get-tuple-element.47.first_ref, s32[96]{0:T(128)S(1)} %get-tuple-element.46.second_ref, s32[1]{0:T(128)S(6)} %copy.9.count_ref, bf16[32,64,128]{2,1,0:T(8,128)(2,1)S(1)} %copy-done.22, bf16[32,128,128]{2,1,0:T(8,128)(2,1)S(1)} %copy-done.9, ...), custom_call_target="tpu_custom_call" | custom-call | flops 469762048 | bytes 9437184 | tf_op jit(solution)/shard_map/pallas_call | solution.py:25
  29.4 18.0 %all-to-all-done.arrived_ref = bf16[128,64,128]{2,1,0:T(8,128)(2,1)S(1)} async-done(((bf16[128,64,128]{2,1,0:T(8,128)(2,1)}), bf16[128,64,128]{2,1,0:T(8,128)(2,1)S(1)}, u32[]{:S(2)}, u32[]{:S(2)}) %all-to-all-start) | async-done | bytes 2097184 | tf_op jit(solution)/shard_map/all_to_all | solution.py:284
  47.4 4.7 %shard_map.88 = (bf16[32,64,128]{2,1,0:T(8,128)(2,1)}, bf16[128,64,128]{2,1,0:T(8,128)(2,1)}) custom-call(s32[1,128]{1,0:T(1,128)S(1)} %copy-done.36, bf16[128,64,128]{2,1,0:T(8,128)(2,1)S(1)} %all-to-all-done.arrived_ref, bf16[128,128,128]{2,1,0:T(8,128)(2,1)} %tiles_ref.17, f32[32,64,128]{2,1,0:T(8,128)} %copy-done.21), custom_call_target="tpu_custom_call" | custom-call | flops 268435456 | bytes 10485760 | tf_op jit(solution)/shard_map/pallas_call | solution.py:25
  52.1 4.7 %all-to-all-start.1 = ((bf16[128,64,128]{2,1,0:T(8,128)(2,1)}), bf16[128,64,128]{2,1,0:T(8,128)(2,1)S(1)}, u32[]{:S(2)}, u32[]{:S(2)}) async-start(bf16[128,64,128]{2,1,0:T(8,128)(2,1)} %get-tuple-element.26), calls=%async_computation.1 | async-start | bytes 4194304 | tf_op jit(solution)/shard_map/all_to_all | solution.py:284
  61.7 6.9 %shard_map.89.part_ref = f32[32,64,128]{2,1,0:T(8,128)S(1)} custom-call(s32[96]{0:T(128)S(1)} %get-tuple-element.47.first_ref, s32[96]{0:T(128)S(1)} %get-tuple-element.46.second_ref, s32[1]{0:T(128)S(6)} %copy.9.count_ref, f32[1,1]{1,0:T(1,128)} %constant.0.clone.1.refs_0_, bf16[32,64,128]{2,1,0:T(8,128)(2,1)S(1)} %copy-done.30, ...), custom_call_target="tpu_custom_call" | custom-call | flops 469762048 | bytes 9437184 | tf_op jit(solution)/shard_map/pallas_call | solution.py:25
  69.6 17.6 %all-to-all-done.1.arrived_ref = bf16[128,64,128]{2,1,0:T(8,128)(2,1)S(1)} async-done(((bf16[128,64,128]{2,1,0:T(8,128)(2,1)}), bf16[128,64,128]{2,1,0:T(8,128)(2,1)S(1)}, u32[]{:S(2)}, u32[]{:S(2)}) %all-to-all-start.1) | async-done | bytes 2097184 | tf_op jit(solution)/shard_map/all_to_all | solution.py:284
  87.2 4.7 %shard_map.90 = (bf16[32,64,128]{2,1,0:T(8,128)(2,1)}, bf16[128,64,128]{2,1,0:T(8,128)(2,1)}) custom-call(s32[1,128]{1,0:T(1,128)S(1)} %copy-done.36, bf16[128,64,128]{2,1,0:T(8,128)(2,1)S(1)} %all-to-all-done.1.arrived_ref, bf16[128,128,128]{2,1,0:T(8,128)(2,1)} %tiles_ref.17, f32[32,64,128]{2,1,0:T(8,128)} %copy-done.17), custom_call_target="tpu_custom_call" | custom-call | flops 268435456 | bytes 10485760 | tf_op jit(solution)/shard_map/pallas_call | solution.py:25
  91.9 4.7 %all-to-all-start.2 = ((bf16[128,64,128]{2,1,0:T(8,128)(2,1)}), bf16[128,64,128]{2,1,0:T(8,128)(2,1)S(1)}, u32[]{:S(2)}, u32[]{:S(2)}) async-start(bf16[128,64,128]{2,1,0:T(8,128)(2,1)} %get-tuple-element.28), calls=%async_computation.2 | async-start | bytes 4194304 | tf_op jit(solution)/shard_map/all_to_all | solution.py:284
  101.5 6.9 %shard_map.91.part_ref = f32[32,64,128]{2,1,0:T(8,128)S(1)} custom-call(s32[96]{0:T(128)S(1)} %get-tuple-element.47.first_ref, s32[96]{0:T(128)S(1)} %get-tuple-element.46.second_ref, s32[1]{0:T(128)S(6)} %copy.9.count_ref, f32[1,1]{1,0:T(1,128)} %constant.0.clone.1.refs_0_, bf16[32,64,128]{2,1,0:T(8,128)(2,1)S(1)} %copy-done.26, ...), custom_call_target="tpu_custom_call" | custom-call | flops 469762048 | bytes 9437184 | tf_op jit(solution)/shard_map/pallas_call | solution.py:25
  109.4 17.6 %all-to-all-done.2.arrived_ref = bf16[128,64,128]{2,1,0:T(8,128)(2,1)S(1)} async-done(((bf16[128,64,128]{2,1,0:T(8,128)(2,1)}), bf16[128,64,128]{2,1,0:T(8,128)(2,1)S(1)}, u32[]{:S(2)}, u32[]{:S(2)}) %all-to-all-start.2) | async-done | bytes 2097184 | tf_op jit(solution)/shard_map/all_to_all | solution.py:284
  127.0 4.7 %shard_map.92 = (bf16[32,64,128]{2,1,0:T(8,128)(2,1)}, bf16[128,64,128]{2,1,0:T(8,128)(2,1)}) custom-call(s32[1,128]{1,0:T(1,128)S(1)} %copy-done.36, bf16[128,64,128]{2,1,0:T(8,128)(2,1)S(1)} %all-to-all-done.2.arrived_ref, bf16[128,128,128]{2,1,0:T(8,128)(2,1)} %tiles_ref.17, f32[32,64,128]{2,1,0:T(8,128)} %copy-done.18), custom_call_target="tpu_custom_call" | custom-call | flops 268435456 | bytes 10485760 | tf_op jit(solution)/shard_map/pallas_call | solution.py:25
  131.7 4.7 %all-to-all-start.3 = ((bf16[128,64,128]{2,1,0:T(8,128)(2,1)}), bf16[128,64,128]{2,1,0:T(8,128)(2,1)S(1)}, u32[]{:S(2)}, u32[]{:S(2)}) async-start(bf16[128,64,128]{2,1,0:T(8,128)(2,1)} %get-tuple-element.30), calls=%async_computation.3 | async-start | bytes 4194304 | tf_op jit(solution)/shard_map/all_to_all | solution.py:284
  136.4 2.8 copy-done.3
  141.3 7.1 %shard_map.93.part_ref = f32[32,64,128]{2,1,0:T(8,128)S(1)} custom-call(s32[96]{0:T(128)S(1)} %get-tuple-element.47.first_ref, s32[96]{0:T(128)S(1)} %get-tuple-element.46.second_ref, s32[1]{0:T(128)S(6)} %copy.9.count_ref, f32[1,1]{1,0:T(1,128)} %constant.0.clone.1.refs_0_, bf16[32,64,128]{2,1,0:T(8,128)(2,1)S(1)} %copy-done.33, ...), custom_call_target="tpu_custom_call" | custom-call | flops 469762048 | bytes 9437184 | tf_op jit(solution)/shard_map/pallas_call | solution.py:25
  149.4 17.5 %all-to-all-done.3.arrived_ref = bf16[128,64,128]{2,1,0:T(8,128)(2,1)S(1)} async-done(((bf16[128,64,128]{2,1,0:T(8,128)(2,1)}), bf16[128,64,128]{2,1,0:T(8,128)(2,1)S(1)}, u32[]{:S(2)}, u32[]{:S(2)}) %all-to-all-start.3) | async-done | bytes 2097184 | tf_op jit(solution)/shard_map/all_to_all | solution.py:284
  166.9 4.7 %shard_map.94 = (bf16[32,64,128]{2,1,0:T(8,128)(2,1)}, bf16[128,64,128]{2,1,0:T(8,128)(2,1)}) custom-call(s32[1,128]{1,0:T(1,128)S(1)} %copy-done.36, bf16[128,64,128]{2,1,0:T(8,128)(2,1)S(1)} %all-to-all-done.3.arrived_ref, bf16[128,128,128]{2,1,0:T(8,128)(2,1)} %tiles_ref.17, f32[32,64,128]{2,1,0:T(8,128)} %copy-done.15), custom_call_target="tpu_custom_call" | custom-call | flops 268435456 | bytes 10485760 | tf_op jit(solution)/shard_map/pallas_call | solution.py:25
  171.6 4.7 %all-to-all-start.4 = ((bf16[128,64,128]{2,1,0:T(8,128)(2,1)}), bf16[128,64,128]{2,1,0:T(8,128)(2,1)S(1)}, u32[]{:S(2)}, u32[]{:S(2)}) async-start(bf16[128,64,128]{2,1,0:T(8,128)(2,1)} %get-tuple-element.32), calls=%async_computation.4 | async-start | bytes 4194304 | tf_op jit(solution)/shard_map/all_to_all | solution.py:284
  177.7 2.8 copy-done.4
  181.5 6.9 %shard_map.95.part_ref = f32[32,64,128]{2,1,0:T(8,128)S(1)} custom-call(s32[96]{0:T(128)S(1)} %get-tuple-element.47.first_ref, s32[96]{0:T(128)S(1)} %get-tuple-element.46.second_ref, s32[1]{0:T(128)S(6)} %copy.9.count_ref, bf16[32,64,128]{2,1,0:T(8,128)(2,1)S(1)} %copy-done.12, bf16[32,128,128]{2,1,0:T(8,128)(2,1)S(1)} %copy-done.9, ...), custom_call_target="tpu_custom_call" | custom-call | flops 469762048 | bytes 9437184 | tf_op jit(solution)/shard_map/pallas_call | solution.py:25
  189.4 17.3 %all-to-all-done.4.arrived_ref = bf16[128,64,128]{2,1,0:T(8,128)(2,1)S(1)} async-done(((bf16[128,64,128]{2,1,0:T(8,128)(2,1)}), bf16[128,64,128]{2,1,0:T(8,128)(2,1)S(1)}, u32[]{:S(2)}, u32[]{:S(2)}) %all-to-all-start.4) | async-done | bytes 2097184 | tf_op jit(solution)/shard_map/all_to_all | solution.py:284
  206.7 2.9 shard_map.97
  209.6 8.9 %all_to_all.65 = f32[8,40,128]{2,1,0:T(8,128)S(1)} all-to-all(f32[8,40,128]{2,1,0:T(8,128)S(1)} %broadcast_in_dim.8), channel_id=1, replica_groups={{0,1,2,3,4,5,6,7},{8,9,10,11,12,13,14,15},{16,17,18,19,20,21,22,23},{24..., dimensions={0} | all-to-all | bytes 327680 | tf_op jit(solution)/shard_map/all_to_all | solution.py:306
  218.5 12.1 %all_to_all.66 = f32[16,40,128]{2,1,0:T(8,128)S(1)} all-to-all(f32[16,40,128]{2,1,0:T(8,128)S(1)} %broadcast_in_dim.9), channel_id=1, replica_groups={{0,8,16,24,32,40,48,56,64,72,80,88,96,104,112,120},{1,9,17,25,33,41,49,..., dimensions={0} | all-to-all | bytes 655360 | tf_op jit(solution)/shard_map/all_to_all | solution.py:306
  230.6 9.7 %shard_map.98 = (bf16[32,64,128]{2,1,0:T(8,128)(2,1)}, bf16[32,64,128]{2,1,0:T(8,128)(2,1)}, bf16[128,64,128]{2,1,0:T(8,128)(2,1)}, f32[1,1]{1,0:T(1,128)}) custom-call(s32[1,128]{1,0:T(1,128)S(1)} %copy-done.36, f32[40,128]{1,0:T(8,128)S(1)} %reduce_sum.37.sums_ref, bf16[32,64,128]{2,1,0:T(8,128)(2,1)} %get-tuple-element.33.refs_0_.cur_ref, ...), custom_call_target="tpu_custom_call" | custom-call | flops 16777216 | bytes 4194304 | tf_op jit(solution)/shard_map/pallas_call | solution.py:25
  240.3 4.7 %all-to-all-start.7 = ((bf16[128,64,128]{2,1,0:T(8,128)(2,1)}), bf16[128,64,128]{2,1,0:T(8,128)(2,1)S(1)}, u32[]{:S(2)}, u32[]{:S(2)}) async-start(bf16[128,64,128]{2,1,0:T(8,128)(2,1)} %get-tuple-element.36), calls=%async_computation.7 | async-start | bytes 4194304 | tf_op jit(solution)/shard_map/all_to_all | solution.py:284
  245.0 2.8 copy-done.5
  249.9 7.6 %shard_map.99.part_ref = f32[32,64,128]{2,1,0:T(8,128)S(1)} custom-call(s32[96]{0:T(128)S(1)} %get-tuple-element.47.first_ref, s32[96]{0:T(128)S(1)} %get-tuple-element.46.second_ref, s32[1]{0:T(128)S(6)} %copy.9.count_ref, f32[1,1]{1,0:T(1,128)} %get-tuple-element.37.refs_0_, bf16[32,64,128]{2,1,0:T(8,128)(2,1)S(1)} %copy-done.24, ...), custom_call_target="tpu_custom_call" | custom-call | flops 469762048 | bytes 9437184 | tf_op jit(solution)/shard_map/pallas_call | solution.py:25
  258.4 17.0 %all-to-all-done.7.arrived_ref = bf16[128,64,128]{2,1,0:T(8,128)(2,1)S(1)} async-done(((bf16[128,64,128]{2,1,0:T(8,128)(2,1)}), bf16[128,64,128]{2,1,0:T(8,128)(2,1)S(1)}, u32[]{:S(2)}, u32[]{:S(2)}) %all-to-all-start.7) | async-done | bytes 2097184 | tf_op jit(solution)/shard_map/all_to_all | solution.py:284
  275.4 4.7 %shard_map.100 = (bf16[32,64,128]{2,1,0:T(8,128)(2,1)}, bf16[128,64,128]{2,1,0:T(8,128)(2,1)}) custom-call(s32[1,128]{1,0:T(1,128)S(1)} %copy-done.36, bf16[128,64,128]{2,1,0:T(8,128)(2,1)S(1)} %all-to-all-done.7.arrived_ref, bf16[128,128,128]{2,1,0:T(8,128)(2,1)} %tiles_ref.17, f32[32,64,128]{2,1,0:T(8,128)} %copy-done.19), custom_call_target="tpu_custom_call" | custom-call | flops 268435456 | bytes 10485760 | tf_op jit(solution)/shard_map/pallas_call | solution.py:25
  280.1 4.9 %all-to-all-start.8 = ((bf16[128,64,128]{2,1,0:T(8,128)(2,1)}), bf16[128,64,128]{2,1,0:T(8,128)(2,1)S(1)}, u32[]{:S(2)}, u32[]{:S(2)}) async-start(bf16[128,64,128]{2,1,0:T(8,128)(2,1)} %get-tuple-element.40), calls=%async_computation.8 | async-start | bytes 4194304 | tf_op jit(solution)/shard_map/all_to_all | solution.py:284
  285.0 2.8 copy-done.6
  289.9 7.6 %shard_map.101.part_ref = f32[32,64,128]{2,1,0:T(8,128)S(1)} custom-call(s32[96]{0:T(128)S(1)} %get-tuple-element.47.first_ref, s32[96]{0:T(128)S(1)} %get-tuple-element.46.second_ref, s32[1]{0:T(128)S(6)} %copy.9.count_ref, f32[1,1]{1,0:T(1,128)} %get-tuple-element.37.refs_0_, bf16[32,64,128]{2,1,0:T(8,128)(2,1)S(1)} %copy-done.28, ...), custom_call_target="tpu_custom_call" | custom-call | flops 469762048 | bytes 9437184 | tf_op jit(solution)/shard_map/pallas_call | solution.py:25
  298.5 16.8 %all-to-all-done.8.arrived_ref = bf16[128,64,128]{2,1,0:T(8,128)(2,1)S(1)} async-done(((bf16[128,64,128]{2,1,0:T(8,128)(2,1)}), bf16[128,64,128]{2,1,0:T(8,128)(2,1)S(1)}, u32[]{:S(2)}, u32[]{:S(2)}) %all-to-all-start.8) | async-done | bytes 2097184 | tf_op jit(solution)/shard_map/all_to_all | solution.py:284
  315.2 4.7 %shard_map.102 = (bf16[32,64,128]{2,1,0:T(8,128)(2,1)}, bf16[128,64,128]{2,1,0:T(8,128)(2,1)}) custom-call(s32[1,128]{1,0:T(1,128)S(1)} %copy-done.36, bf16[128,64,128]{2,1,0:T(8,128)(2,1)S(1)} %all-to-all-done.8.arrived_ref, bf16[128,128,128]{2,1,0:T(8,128)(2,1)} %tiles_ref.17, f32[32,64,128]{2,1,0:T(8,128)} %copy-done.20), custom_call_target="tpu_custom_call" | custom-call | flops 268435456 | bytes 10485760 | tf_op jit(solution)/shard_map/pallas_call | solution.py:25
  319.9 4.7 %all-to-all-start.9 = ((bf16[128,64,128]{2,1,0:T(8,128)(2,1)}), bf16[128,64,128]{2,1,0:T(8,128)(2,1)S(1)}, u32[]{:S(2)}, u32[]{:S(2)}) async-start(bf16[128,64,128]{2,1,0:T(8,128)(2,1)} %get-tuple-element.42), calls=%async_computation.9 | async-start | bytes 4194304 | tf_op jit(solution)/shard_map/all_to_all | solution.py:284
  329.5 7.6 %shard_map.103.part_ref = f32[32,64,128]{2,1,0:T(8,128)S(1)} custom-call(s32[96]{0:T(128)S(1)} %get-tuple-element.47.first_ref, s32[96]{0:T(128)S(1)} %get-tuple-element.46.second_ref, s32[1]{0:T(128)S(6)} %copy.9.count_ref, f32[1,1]{1,0:T(1,128)} %get-tuple-element.37.refs_0_, bf16[32,64,128]{2,1,0:T(8,128)(2,1)S(1)} %copy-done.34, ...), custom_call_target="tpu_custom_call" | custom-call | flops 469762048 | bytes 9437184 | tf_op jit(solution)/shard_map/pallas_call | solution.py:25
  338.0 17.0 %all-to-all-done.9.arrived_ref = bf16[128,64,128]{2,1,0:T(8,128)(2,1)S(1)} async-done(((bf16[128,64,128]{2,1,0:T(8,128)(2,1)}), bf16[128,64,128]{2,1,0:T(8,128)(2,1)S(1)}, u32[]{:S(2)}, u32[]{:S(2)}) %all-to-all-start.9) | async-done | bytes 2097184 | tf_op jit(solution)/shard_map/all_to_all | solution.py:284
  355.0 4.7 %shard_map.104 = (bf16[32,64,128]{2,1,0:T(8,128)(2,1)}, bf16[128,64,128]{2,1,0:T(8,128)(2,1)}) custom-call(s32[1,128]{1,0:T(1,128)S(1)} %copy-done.36, bf16[128,64,128]{2,1,0:T(8,128)(2,1)S(1)} %all-to-all-done.9.arrived_ref, bf16[128,128,128]{2,1,0:T(8,128)(2,1)} %tiles_ref.17, f32[32,64,128]{2,1,0:T(8,128)} %copy-done.16), custom_call_target="tpu_custom_call" | custom-call | flops 268435456 | bytes 10485760 | tf_op jit(solution)/shard_map/pallas_call | solution.py:25
  359.7 5.9 %all-to-all-start.10 = ((bf16[128,64,128]{2,1,0:T(8,128)(2,1)}), bf16[128,64,128]{2,1,0:T(8,128)(2,1)}, u32[]{:S(2)}, u32[]{:S(2)}) async-start(bf16[128,64,128]{2,1,0:T(8,128)(2,1)} %get-tuple-element.44), calls=%async_computation.10 | async-start | bytes 4194304 | tf_op jit(solution)/shard_map/all_to_all | solution.py:284
  366.1 2.8 copy-done.8
  368.9 6.9 %shard_map.105.part_ref = f32[32,64,128]{2,1,0:T(8,128)S(1)} custom-call(s32[96]{0:T(128)S(1)} %get-tuple-element.47.first_ref, s32[96]{0:T(128)S(1)} %get-tuple-element.46.second_ref, s32[1]{0:T(128)S(6)} %copy.9.count_ref, bf16[32,64,128]{2,1,0:T(8,128)(2,1)S(1)} %copy-done.10, bf16[32,128,128]{2,1,0:T(8,128)(2,1)S(1)} %copy-done.9, ...), custom_call_target="tpu_custom_call" | custom-call | flops 469762048 | bytes 9437184 | tf_op jit(solution)/shard_map/pallas_call | solution.py:25
  376.8 18.9 %all-to-all-done.10.arrived_ref = bf16[128,64,128]{2,1,0:T(8,128)(2,1)} async-done(((bf16[128,64,128]{2,1,0:T(8,128)(2,1)}), bf16[128,64,128]{2,1,0:T(8,128)(2,1)}, u32[]{:S(2)}, u32[]{:S(2)}) %all-to-all-start.10) | async-done | bytes 2097184 | tf_op jit(solution)/shard_map/all_to_all | solution.py:284
  395.7 3.6 shard_map.107
  399.3 8.9 %all_to_all.67 = f32[8,40,128]{2,1,0:T(8,128)S(1)} all-to-all(f32[8,40,128]{2,1,0:T(8,128)S(1)} %broadcast_in_dim.10), channel_id=1, replica_groups={{0,1,2,3,4,5,6,7},{8,9,10,11,12,13,14,15},{16,17,18,19,20,21,22,23},{24..., dimensions={0} | all-to-all | bytes 327680 | tf_op jit(solution)/shard_map/all_to_all | solution.py:306
  408.3 12.1 %all_to_all.68 = f32[16,40,128]{2,1,0:T(8,128)S(1)} all-to-all(f32[16,40,128]{2,1,0:T(8,128)S(1)} %broadcast_in_dim.11), channel_id=1, replica_groups={{0,8,16,24,32,40,48,56,64,72,80,88,96,104,112,120},{1,9,17,25,33,41,49,..., dimensions={0} | all-to-all | bytes 655360 | tf_op jit(solution)/shard_map/all_to_all | solution.py:306
  420.3 5.7 %shard_map.108 = (bf16[64,4096]{1,0:T(8,128)(2,1)}, f32[64,64]{1,0:T(8,128)}) custom-call(f32[40,128]{1,0:T(8,128)S(1)} %reduce_sum.39.sums_ref, bf16[32,64,128]{2,1,0:T(8,128)(2,1)} %get-tuple-element.45.refs_0_.cur_ref), custom_call_target="tpu_custom_call" | custom-call | flops 16777216 | bytes 2097152 | tf_op jit(solution)/shard_map/pallas_call | solution.py:25
  (82 shorter events, 37.1 us)
Async XLA Ops:
  0.6 0.7 copy-start.35
  5.8 11.8 %copy-start.37 = (s32[1,96,2]{1,2,0:T(2,128)S(1)}, s32[1,96,2]{1,2,0:T(2,128)}, u32[]{:S(2)}) copy-start(s32[1,96,2]{1,2,0:T(2,128)} %param.12) | copy-start | bytes 2308
  5.8 11.8 %copy-start.9 = (bf16[32,128,128]{2,1,0:T(8,128)(2,1)S(1)}, bf16[32,128,128]{2,1,0:T(8,128)(2,1)}, u32[]{:S(2)}) copy-start(bf16[32,128,128]{2,1,0:T(8,128)(2,1)} %refs_1_.5) | copy-start | bytes 3145732
  5.8 41.6 %all-to-all-start = ((bf16[128,64,128]{2,1,0:T(8,128)(2,1)}), bf16[128,64,128]{2,1,0:T(8,128)(2,1)S(1)}, u32[]{:S(2)}, u32[]{:S(2)}) async-start(bf16[128,64,128]{2,1,0:T(8,128)(2,1)} %get-tuple-element.24), calls=%async_computation | async-start | bytes 4194304 | tf_op jit(solution)/shard_map/all_to_all | solution.py:284
  17.7 2.8 copy-start
  20.5 1.0 copy-start.22
  21.5 25.9 %copy-start.36 = (s32[1,128]{1,0:T(1,128)S(1)}, s32[1,128]{1,0:T(1,128)}, u32[]{:S(2)}) copy-start(s32[1,128]{1,0:T(1,128)} %rows_ref.21) | copy-start | bytes 1540
  28.5 1.0 copy-start.21
  52.1 35.1 %all-to-all-start.1 = ((bf16[128,64,128]{2,1,0:T(8,128)(2,1)}), bf16[128,64,128]{2,1,0:T(8,128)(2,1)S(1)}, u32[]{:S(2)}, u32[]{:S(2)}) async-start(bf16[128,64,128]{2,1,0:T(8,128)(2,1)} %get-tuple-element.26), calls=%async_computation.1 | async-start | bytes 4194304 | tf_op jit(solution)/shard_map/all_to_all | solution.py:284
  56.8 2.8 copy-start.1
  59.6 1.0 copy-start.23
  60.6 1.0 copy-start.30
  68.6 1.0 copy-start.17
  91.9 35.1 %all-to-all-start.2 = ((bf16[128,64,128]{2,1,0:T(8,128)(2,1)}), bf16[128,64,128]{2,1,0:T(8,128)(2,1)S(1)}, u32[]{:S(2)}, u32[]{:S(2)}) async-start(bf16[128,64,128]{2,1,0:T(8,128)(2,1)} %get-tuple-element.28), calls=%async_computation.2 | async-start | bytes 4194304 | tf_op jit(solution)/shard_map/all_to_all | solution.py:284
  96.6 2.8 copy-start.2
  99.4 1.0 copy-start.26
  100.4 1.0 copy-start.31
  108.4 1.0 copy-start.18
  131.7 35.1 %all-to-all-start.3 = ((bf16[128,64,128]{2,1,0:T(8,128)(2,1)}), bf16[128,64,128]{2,1,0:T(8,128)(2,1)S(1)}, u32[]{:S(2)}, u32[]{:S(2)}) async-start(bf16[128,64,128]{2,1,0:T(8,128)(2,1)} %get-tuple-element.30), calls=%async_computation.3 | async-start | bytes 4194304 | tf_op jit(solution)/shard_map/all_to_all | solution.py:284
  136.4 2.8 copy-start.3
  139.2 1.0 copy-start.27
  140.2 1.0 copy-start.33
  148.4 1.0 copy-start.15
  171.6 35.1 %all-to-all-start.4 = ((bf16[128,64,128]{2,1,0:T(8,128)(2,1)}), bf16[128,64,128]{2,1,0:T(8,128)(2,1)S(1)}, u32[]{:S(2)}, u32[]{:S(2)}) async-start(bf16[128,64,128]{2,1,0:T(8,128)(2,1)} %get-tuple-element.32), calls=%async_computation.4 | async-start | bytes 4194304 | tf_op jit(solution)/shard_map/all_to_all | solution.py:284
  176.2 1.0 copy-start.11
  177.7 2.8 copy-start.4
  180.5 1.0 copy-start.12
  188.4 1.0 copy-start.14
  240.3 35.1 %all-to-all-start.7 = ((bf16[128,64,128]{2,1,0:T(8,128)(2,1)}), bf16[128,64,128]{2,1,0:T(8,128)(2,1)S(1)}, u32[]{:S(2)}, u32[]{:S(2)}) async-start(bf16[128,64,128]{2,1,0:T(8,128)(2,1)} %get-tuple-element.36), calls=%async_computation.7 | async-start | bytes 4194304 | tf_op jit(solution)/shard_map/all_to_all | solution.py:284
  245.0 2.8 copy-start.5
  247.8 1.0 copy-start.24
  248.8 1.0 copy-start.32
  257.5 1.0 copy-start.19
  280.1 35.1 %all-to-all-start.8 = ((bf16[128,64,128]{2,1,0:T(8,128)(2,1)}), bf16[128,64,128]{2,1,0:T(8,128)(2,1)S(1)}, u32[]{:S(2)}, u32[]{:S(2)}) async-start(bf16[128,64,128]{2,1,0:T(8,128)(2,1)} %get-tuple-element.40), calls=%async_computation.8 | async-start | bytes 4194304 | tf_op jit(solution)/shard_map/all_to_all | solution.py:284
  285.0 2.8 copy-start.6
  287.8 1.0 copy-start.25
  288.8 1.0 copy-start.28
  297.5 1.0 copy-start.20
  319.9 35.1 %all-to-all-start.9 = ((bf16[128,64,128]{2,1,0:T(8,128)(2,1)}), bf16[128,64,128]{2,1,0:T(8,128)(2,1)S(1)}, u32[]{:S(2)}, u32[]{:S(2)}) async-start(bf16[128,64,128]{2,1,0:T(8,128)(2,1)} %get-tuple-element.42), calls=%async_computation.9 | async-start | bytes 4194304 | tf_op jit(solution)/shard_map/all_to_all | solution.py:284
  324.6 2.8 copy-start.7
  327.4 1.0 copy-start.29
  328.4 1.0 copy-start.34
  337.1 1.0 copy-start.16
  359.7 5.9 %copy-start.10 = (bf16[32,64,128]{2,1,0:T(8,128)(2,1)S(1)}, bf16[32,64,128]{2,1,0:T(8,128)(2,1)}, u32[]{:S(2)}) copy-start(bf16[32,64,128]{2,1,0:T(8,128)(2,1)} %get-tuple-element.45.refs_0_.cur_ref) | copy-start | bytes 1572868
  359.7 35.9 %all-to-all-start.10 = ((bf16[128,64,128]{2,1,0:T(8,128)(2,1)}), bf16[128,64,128]{2,1,0:T(8,128)(2,1)}, u32[]{:S(2)}, u32[]{:S(2)}) async-start(bf16[128,64,128]{2,1,0:T(8,128)(2,1)} %get-tuple-element.44), calls=%async_computation.10 | async-start | bytes 4194304 | tf_op jit(solution)/shard_map/all_to_all | solution.py:284
  366.1 2.8 copy-start.8
  375.8 1.0 copy-start.13

commit v6 on v5

--- a/solution.py
+++ b/solution.py
@@ -195,22 +195,28 @@
 
 
 def inverse_factor(gram):
-    n = gram.shape[0]
-    row = lax.broadcasted_iota(jnp.int32, (n, n), 0)
-    col = lax.broadcasted_iota(jnp.int32, (n, n), 1)
+    n, some = gram.shape[0], 8
+    row, col = corner(n)
     work = jnp.concatenate([gram, jnp.where(row == col, 1.0, 0.0).astype(F32)], axis=1)
-    at = lax.broadcasted_iota(jnp.int32, work.shape, 0)
+    parts = [work[b : b + some] for b in range(0, n, some)]
+    at = lax.broadcasted_iota(jnp.int32, parts[0].shape, 0)
     for j in range(0, n, 2):
-        first = jnp.broadcast_to(work[:, j : j + 1], work.shape)
-        second = jnp.broadcast_to(work[:, j + 1 : j + 2], work.shape)
-        over = 1.0 / first[j : j + 1]
-        low = first[j + 1 : j + 2] * over
-        upper = second[j : j + 1]
-        under = 1.0 / (second[j + 1 : j + 2] - low * upper)
-        below = work[j + 1 : j + 2] - low * work[j : j + 1]
-        times = first * over
-        again = jnp.where(at > j + 1, (second - times * upper) * under, 0.0)
-        work = work - jnp.where(at > j, times, 0.0) * work[j : j + 1] - again * below
+        own, o = j // some, j % some
+        first = [jnp.broadcast_to(part[:, j : j + 1], part.shape) for part in parts[own:]]
+        second = [jnp.broadcast_to(part[:, j + 1 : j + 2], part.shape) for part in parts[own:]]
+        over = 1.0 / first[0][o : o + 1]
+        low = first[0][o + 1 : o + 2] * over
+        upper = second[0][o : o + 1]
+        under = 1.0 / (second[0][o + 1 : o + 2] - low * upper)
+        above = parts[own][o : o + 1]
+        below = parts[own][o + 1 : o + 2] - low * above
+        for i, part in enumerate(parts[own:]):
+            times = first[i] * over
+            again = (second[i] - times * upper) * under
+            if i == 0:
+                times, again = jnp.where(at > o, times, 0.0), jnp.where(at > o + 1, again, 0.0)
+            parts[own + i] = part - times * above - again * below
+    work = jnp.concatenate(parts, axis=0)
     pivots = jnp.sum(jnp.where(row == col, work[:, :n], 0.0), axis=1, keepdims=True)
     return work[:, n:] / jnp.sqrt(pivots)
 
@@ -228,25 +234,47 @@
     return first[:k] + ((first[k : 2 * k] + second[:k]) + (first[2 * k :] + second[k:] + third))
 
 
-def turn_kernel(total, rows_ref, sums_ref, cur_ref, image_ref, tiles_ref, next_ref, y_ref, out_ref, centre_ref, *scratch):
-    cur, image, begun, block, tiles, slots, loads, sems = scratch
+def shift_kernel(rows_ref, image_ref, cur_ref, tiles_ref, near_ref, z_ref, out_ref, image, cur, block, tiles, slots, loads, sems):
+    del near_ref
     first = begin(cur_ref, cur, loads.at[CHUNKS])
     second = begin(image_ref, image, loads.at[CHUNKS + 1])
     coming = load(tiles_ref, tiles, loads)
+    first.wait()
+    second.wait()
+    block[...] = (image[...] - FIRST_CENTRE * cur[...].astype(F32)).astype(BF16)
+    going = [begin(block, z_ref, loads.at[CHUNKS])]
+    going += send(rows_ref, block, tiles, coming, slots, out_ref, sems)
+    for copy in going:
+        copy.wait()
+
+
+def factor_kernel(total, sums_ref, cur_ref, image_ref, z_ref, part_ref, inverse_ref, y_ref, centre_ref, rest_ref):
     gram, product = unpacked(sums_ref[...])
     inverse = inverse_factor(gram / total)
+    inverse_ref[...] = inverse
     half = jnp.dot(inverse, product / total, precision=HI, preferred_element_type=F32)
     centre = jnp.sum(half * inverse) / inverse.shape[0] - 1.0
     centre_ref[0, 0] = centre
+    change = centre - FIRST_CENTRE
     stack = jnp.concatenate(thirds(inverse), axis=0)
-    first.wait()
-    second.wait()
-    for r in range(cur.shape[0]):
-        value = apply_square(stack, cur[r]).astype(BF16)
-        begun[r] = value
-        turned = apply_wide(stack, image[r])
-        block[r] = (turned - centre * value.astype(F32)).astype(BF16)
-    going = [begin(begun, next_ref, sems.at[WAVES]), begin(block, y_ref, sems.at[WAVES + 1])]
+    for r in range(cur_ref.shape[0]):
+        block = cur_ref[r]
+        begun = apply_square(stack, block).astype(BF16)
+        moved = z_ref[r].astype(F32) - change * block.astype(F32)
+        y_ref[r] = apply_wide(stack, moved).astype(BF16)
+        rest = apply_wide(stack, part_ref[r] - change * image_ref[r] - centre * moved)
+        rest_ref[r] = 2.0 * rest - begun.astype(F32)
+
+
+def turn_kernel(rows_ref, arrived_ref, tiles_ref, part_ref, inverse_ref, cur_ref, out_ref, tiles, part, acc, block, slots, loads, sems):
+    also = begin(part_ref, part, loads.at[CHUNKS])
+    coming = load(tiles_ref, tiles, loads)
+    receive(rows_ref, arrived_ref, acc)
+    stack = jnp.concatenate(thirds(inverse_ref[...]), axis=0)
+    also.wait()
+    for r in range(block.shape[0]):
+        block[r] = (2.0 * apply_wide(stack, acc[r]) + part[r]).astype(BF16)
+    going = [begin(block, cur_ref, loads.at[CHUNKS + 1])]
     going += send(rows_ref, block, tiles, coming, slots, out_ref, sems)
     for copy in going:
         copy.wait()
@@ -298,13 +326,16 @@
             [room(halo_tiles.shape, BF16), room(block, F32), room(block, F32), room(block, BF16), room(spots, BF16), loads, sems],
         )
 
-    def everywhere(x):
+    def everywhere(x, between=None):
         near = [list(range(g, g + NODE)) for g in range(0, peers, NODE)]
         far = [list(range(g, peers, NODE)) for g in range(NODE)]
+        result = None
         for groups in (near, far):
+            if between and groups is far:
+                result = between(x)
             many = jnp.broadcast_to(x[None], (len(groups[0]), *x.shape))
             x = jnp.sum(lax.all_to_all(many, "dom", 0, 0, axis_index_groups=groups, tiled=True), axis=0)
-        return x
+        return x, result
 
     def sums(cur, arrived, part, keep):
         [gram] = call(gram_kernel, [(square, F32, "h")], [(cur, "h")], 2 * k * k * own_rows, 1 << 20)
@@ -312,10 +343,10 @@
         ins = [(halo_rows, "s"), (arrived, "v"), (part, "a"), (cur, "a"), (gram, "h")]
         scratch = [room(block, F32), room(block, F32), room(block, BF16), sems]
         *image, value = call(functools.partial(sums_kernel, keep), outs, ins, unit * peers, 10 << 20, scratch)
-        return *image, everywhere(value)
-
-    def filtered(prev, cur, out, centre):
-        for _ in range(3):
+        return *image, value
+
+    def filtered(prev, cur, out, centre, steps):
+        for _ in range(steps):
             arrived = exchange(out)
             part = own("filter", cur, [(prev, "h")], [(centre, "s")])
             prev, (cur, out) = cur, halo(2.0, arrived, part)
@@ -331,23 +362,43 @@
     )
     arrived = exchange(out)
     cur, out = halo(1.0, arrived, own("start", start))
-    cur, out = filtered(start, cur, out, jnp.full((1, 1), FIRST_CENTRE, F32))
+    cur, out = filtered(start, cur, out, jnp.full((1, 1), FIRST_CENTRE, F32), 3)
 
     arrived = exchange(out)
     image, value = sums(cur, arrived, own("image", cur), 1)
-    begun, cur, out, centre = call(
-        functools.partial(turn_kernel, total),
-        [(block, BF16, "a"), (block, BF16, "a"), (spots, BF16, "a"), ((1, 1), F32, "s")],
-        [(halo_rows, "s"), (value, "h"), (cur, "a"), (image, "a"), (halo_tiles, "a")],
+
+    def shift(near):
+        return call(
+            shift_kernel,
+            [(block, BF16, "a"), (spots, BF16, "a")],
+            [(halo_rows, "s"), (image, "a"), (cur, "a"), (halo_tiles, "a"), (near, "a")],
+            unit * peers,
+            8 << 20,
+            [room(block, F32), room(block, BF16), room(block, BF16), room(halo_tiles.shape, BF16), room(spots, BF16), loads, sems],
+        )
+
+    value, (z, out) = everywhere(value, shift)
+    arrived = exchange(out)
+    inverse, first, centre, rest = call(
+        functools.partial(factor_kernel, total),
+        [(square, F32, "h"), (block, BF16, "h"), ((1, 1), F32, "s"), (block, F32, "h")],
+        [(value, "h"), (cur, "h"), (image, "h"), (z, "h"), (own("image", z), "h")],
         1 << 24,
         4 << 20,
-        [room(block, BF16), room(block, F32), room(block, BF16), room(block, BF16)]
-        + [room(halo_tiles.shape, BF16), room(spots, BF16), loads, sems],
     )
-    cur, out = filtered(begun, cur, out, centre)
+    cur, out = call(
+        turn_kernel,
+        [(block, BF16, "a"), (spots, BF16, "a")],
+        [(halo_rows, "s"), (arrived, "v"), (halo_tiles, "a"), (rest, "a"), (inverse, "h")],
+        unit * peers,
+        10 << 20,
+        [room(halo_tiles.shape, BF16), room(block, F32), room(block, F32), room(block, BF16), room(spots, BF16), loads, sems],
+    )
+    cur, out = filtered(first, cur, out, centre, 2)
 
     arrived = exchange(out)
     [value] = sums(cur, arrived, own("image", cur), 0)
+    value, _ = everywhere(value)
     return call(
         functools.partial(end_kernel, total),
         [((k, own_rows), BF16, "h"), (square, F32, "h")],

time: 428 us -> 425 us (level)
  waiting for transfers between devices: 158 us -> 191 us
  Pallas kernels: 125 us -> 95.2 us
  blocking collectives: 41.9 us -> 29.8 us
  starting transfers between devices: 50 us -> 56.1 us
    pallas_call x23 -> x24, Pallas kernels: 125 us -> 95.2 us  [call(): pl.pallas_call(body, out_shape=[(place[kind] if kind in place else jax.Sh...]
    all_to_all x9, waiting for transfers between devices: 158 us -> 186 us  [exchange(): return lax.all_to_all(out, 'dom', 0, 0, tiled=True)]
    all_to_all x4 -> x3, blocking collectives: 41.9 us -> 29.8 us  [everywhere(): lax.all_to_all(many, 'dom', 0, 0, axis_index_groups=groups, tiled=True)]
    all_to_all x0 -> x1, waiting for transfers between devices: none -> 4.5 us  [everywhere(): lax.all_to_all(many, 'dom', 0, 0, axis_index_groups=groups, tiled=True)]
    unnamed x76 -> x80, local copies, waits for them, and re-layouts: 50.1 us -> 48.1 us
  transfers between devices with their start and end apart: 9 -> 10, of which waited for: 9 -> 10; matrix products, arithmetic and copies ran while one was open for 0% -> 0% of each run, Pallas kernels for 15% -> 10%
where the time goes in v6:
time: 425 us; the launch traced here: 423 us
  waiting for transfers between devices  191 us (45%)
  Pallas kernels  95.2 us (22%)
  starting transfers between devices  56.1 us (13%)
  local copies, waits for them, and re-layouts  48.9 us (12%)
  blocking collectives  29.8 us (7%)
    all_to_all x9, waiting for transfers between devices, exchange(): return lax.all_to_all(out, 'dom', 0, 0, tiled=True)  186 us
    pallas_call x24, Pallas kernels, call(): pl.pallas_call(body, out_shape=[(place[kind] if kind in place else jax.Sh...  95.2 us
    all_to_all x9, starting transfers between devices, exchange(): return lax.all_to_all(out, 'dom', 0, 0, tiled=True)  52.5 us
    unnamed x80, local copies, waits for them, and re-layouts  48.1 us
    all_to_all x3, blocking collectives, everywhere(): lax.all_to_all(many, 'dom', 0, 0, axis_index_groups=groups, tiled=True)  29.8 us
  transfers between devices with their start and end apart: 10, of which 10 were waited for; matrix products, arithmetic and copies ran while one was open for 0% of the time, Pallas kernels for 10%

profile of v6, /device:TPU:0, one launch (start us, length us, event | category | flops | bytes accessed | tf_op | source)
XLA Modules:
  0.0 423.2 jit_solution(14209041312966873512)
XLA Ops:
  1.3 4.5 %shard_map.86 = (bf16[32,64,128]{2,1,0:T(8,128)(2,1)}, bf16[128,64,128]{2,1,0:T(8,128)(2,1)}) custom-call(s32[1,128]{1,0:T(1,128)S(1)} %copy-done.36, bf16[64,4096]{1,0:T(8,128)(2,1)} %vec_ref.1, bf16[128,128,128]{2,1,0:T(8,128)(2,1)} %tiles_ref.17), custom_call_target="tpu_custom_call" | custom-call | flops 268435456 | bytes 8388608 | tf_op jit(solution)/shard_map/pallas_call | solution.py:25
  5.9 11.2 %all-to-all-start = ((bf16[128,64,128]{2,1,0:T(8,128)(2,1)}), bf16[128,64,128]{2,1,0:T(8,128)(2,1)S(1)}, u32[]{:S(2)}, u32[]{:S(2)}) async-start(bf16[128,64,128]{2,1,0:T(8,128)(2,1)} %get-tuple-element.26), calls=%async_computation | async-start | bytes 4194304 | tf_op jit(solution)/shard_map/all_to_all | solution.py:312
  17.7 2.8 copy-done
  21.5 3.2 shard_map.87.part_ref
  25.7 21.8 %all-to-all-done.arrived_ref = bf16[128,64,128]{2,1,0:T(8,128)(2,1)S(1)} async-done(((bf16[128,64,128]{2,1,0:T(8,128)(2,1)}), bf16[128,64,128]{2,1,0:T(8,128)(2,1)S(1)}, u32[]{:S(2)}, u32[]{:S(2)}) %all-to-all-start) | async-done | bytes 2097184 | tf_op jit(solution)/shard_map/all_to_all | solution.py:312
  47.5 4.7 %shard_map.88 = (bf16[32,64,128]{2,1,0:T(8,128)(2,1)}, bf16[128,64,128]{2,1,0:T(8,128)(2,1)}) custom-call(s32[1,128]{1,0:T(1,128)S(1)} %copy-done.37, bf16[128,64,128]{2,1,0:T(8,128)(2,1)S(1)} %all-to-all-done.arrived_ref, bf16[128,128,128]{2,1,0:T(8,128)(2,1)} %tiles_ref.17, f32[32,64,128]{2,1,0:T(8,128)} %copy-done.21), custom_call_target="tpu_custom_call" | custom-call | flops 268435456 | bytes 10485760 | tf_op jit(solution)/shard_map/pallas_call | solution.py:25
  52.2 4.7 %all-to-all-start.1 = ((bf16[128,64,128]{2,1,0:T(8,128)(2,1)}), bf16[128,64,128]{2,1,0:T(8,128)(2,1)S(1)}, u32[]{:S(2)}, u32[]{:S(2)}) async-start(bf16[128,64,128]{2,1,0:T(8,128)(2,1)} %get-tuple-element.28), calls=%async_computation.1 | async-start | bytes 4194304 | tf_op jit(solution)/shard_map/all_to_all | solution.py:312
  61.7 3.2 shard_map.89.part_ref
  65.9 21.4 %all-to-all-done.1.arrived_ref = bf16[128,64,128]{2,1,0:T(8,128)(2,1)S(1)} async-done(((bf16[128,64,128]{2,1,0:T(8,128)(2,1)}), bf16[128,64,128]{2,1,0:T(8,128)(2,1)S(1)}, u32[]{:S(2)}, u32[]{:S(2)}) %all-to-all-start.1) | async-done | bytes 2097184 | tf_op jit(solution)/shard_map/all_to_all | solution.py:312
  87.3 4.7 %shard_map.90 = (bf16[32,64,128]{2,1,0:T(8,128)(2,1)}, bf16[128,64,128]{2,1,0:T(8,128)(2,1)}) custom-call(s32[1,128]{1,0:T(1,128)S(1)} %copy-done.37, bf16[128,64,128]{2,1,0:T(8,128)(2,1)S(1)} %all-to-all-done.1.arrived_ref, bf16[128,128,128]{2,1,0:T(8,128)(2,1)} %tiles_ref.17, f32[32,64,128]{2,1,0:T(8,128)} %copy-done.18), custom_call_target="tpu_custom_call" | custom-call | flops 268435456 | bytes 10485760 | tf_op jit(solution)/shard_map/pallas_call | solution.py:25
  92.0 4.7 %all-to-all-start.2 = ((bf16[128,64,128]{2,1,0:T(8,128)(2,1)}), bf16[128,64,128]{2,1,0:T(8,128)(2,1)S(1)}, u32[]{:S(2)}, u32[]{:S(2)}) async-start(bf16[128,64,128]{2,1,0:T(8,128)(2,1)} %get-tuple-element.30), calls=%async_computation.2 | async-start | bytes 4194304 | tf_op jit(solution)/shard_map/all_to_all | solution.py:312
  101.6 3.2 shard_map.91.part_ref
  105.7 21.4 %all-to-all-done.2.arrived_ref = bf16[128,64,128]{2,1,0:T(8,128)(2,1)S(1)} async-done(((bf16[128,64,128]{2,1,0:T(8,128)(2,1)}), bf16[128,64,128]{2,1,0:T(8,128)(2,1)S(1)}, u32[]{:S(2)}, u32[]{:S(2)}) %all-to-all-start.2) | async-done | bytes 2097184 | tf_op jit(solution)/shard_map/all_to_all | solution.py:312
  127.1 4.7 %shard_map.92 = (bf16[32,64,128]{2,1,0:T(8,128)(2,1)}, bf16[128,64,128]{2,1,0:T(8,128)(2,1)}) custom-call(s32[1,128]{1,0:T(1,128)S(1)} %copy-done.37, bf16[128,64,128]{2,1,0:T(8,128)(2,1)S(1)} %all-to-all-done.2.arrived_ref, bf16[128,128,128]{2,1,0:T(8,128)(2,1)} %tiles_ref.17, f32[32,64,128]{2,1,0:T(8,128)} %copy-done.19), custom_call_target="tpu_custom_call" | custom-call | flops 268435456 | bytes 10485760 | tf_op jit(solution)/shard_map/pallas_call | solution.py:25
  131.8 4.7 %all-to-all-start.3 = ((bf16[128,64,128]{2,1,0:T(8,128)(2,1)}), bf16[128,64,128]{2,1,0:T(8,128)(2,1)S(1)}, u32[]{:S(2)}, u32[]{:S(2)}) async-start(bf16[128,64,128]{2,1,0:T(8,128)(2,1)} %get-tuple-element.32), calls=%async_computation.3 | async-start | bytes 4194304 | tf_op jit(solution)/shard_map/all_to_all | solution.py:312
  141.4 3.4 shard_map.93.part_ref
  145.8 21.2 %all-to-all-done.3.arrived_ref = bf16[128,64,128]{2,1,0:T(8,128)(2,1)S(1)} async-done(((bf16[128,64,128]{2,1,0:T(8,128)(2,1)}), bf16[128,64,128]{2,1,0:T(8,128)(2,1)S(1)}, u32[]{:S(2)}, u32[]{:S(2)}) %all-to-all-start.3) | async-done | bytes 2097184 | tf_op jit(solution)/shard_map/all_to_all | solution.py:312
  166.9 4.7 %shard_map.94 = (bf16[32,64,128]{2,1,0:T(8,128)(2,1)}, bf16[128,64,128]{2,1,0:T(8,128)(2,1)}) custom-call(s32[1,128]{1,0:T(1,128)S(1)} %copy-done.37, bf16[128,64,128]{2,1,0:T(8,128)(2,1)S(1)} %all-to-all-done.3.arrived_ref, bf16[128,128,128]{2,1,0:T(8,128)(2,1)} %tiles_ref.17, f32[32,64,128]{2,1,0:T(8,128)} %copy-done.16), custom_call_target="tpu_custom_call" | custom-call | flops 268435456 | bytes 10485760 | tf_op jit(solution)/shard_map/pallas_call | solution.py:25
  171.7 5.9 %all-to-all-start.4 = ((bf16[128,64,128]{2,1,0:T(8,128)(2,1)}), bf16[128,64,128]{2,1,0:T(8,128)(2,1)}, u32[]{:S(2)}, u32[]{:S(2)}) async-start(bf16[128,64,128]{2,1,0:T(8,128)(2,1)} %get-tuple-element.34), calls=%async_computation.4 | async-start | bytes 4194304 | tf_op jit(solution)/shard_map/all_to_all | solution.py:312
  178.0 2.8 copy-done.4
  180.8 3.1 shard_map.95.part_ref
  185.0 22.7 %all-to-all-done.4.arrived_ref = bf16[128,64,128]{2,1,0:T(8,128)(2,1)} async-done(((bf16[128,64,128]{2,1,0:T(8,128)(2,1)}), bf16[128,64,128]{2,1,0:T(8,128)(2,1)}, u32[]{:S(2)}, u32[]{:S(2)}) %all-to-all-start.4) | async-done | bytes 2097184 | tf_op jit(solution)/shard_map/all_to_all | solution.py:312
  207.6 4.0 shard_map.97
  211.7 8.9 %all_to_all.65 = f32[8,40,128]{2,1,0:T(8,128)S(1)} all-to-all(f32[8,40,128]{2,1,0:T(8,128)S(1)} %broadcast_in_dim.8), channel_id=1, replica_groups={{0,1,2,3,4,5,6,7},{8,9,10,11,12,13,14,15},{16,17,18,19,20,21,22,23},{24..., dimensions={0} | all-to-all | bytes 327680 | tf_op jit(solution)/shard_map/all_to_all | solution.py:337
  221.3 3.5 all-to-all-start.7
  224.9 4.9 %shard_map.98 = (bf16[32,64,128]{2,1,0:T(8,128)(2,1)}, bf16[128,64,128]{2,1,0:T(8,128)(2,1)}) custom-call(s32[1,128]{1,0:T(1,128)S(1)} %copy-done.37, f32[32,64,128]{2,1,0:T(8,128)} %get-tuple-element.36.image_ref, bf16[32,64,128]{2,1,0:T(8,128)(2,1)} %get-tuple-element.35.refs_0_.cur_ref, bf16[128,128,128]{2,1,0:T(8,128)(2,1)} %tiles_ref.17, ...), custom_call_target="tpu_custom_call" | custom-call | flops 268435456 | bytes 8388608 | tf_op jit(solution)/shard_map/pallas_call | solution.py:25
  229.8 4.5 %all-to-all-done.7 = f32[16,40,128]{2,1,0:T(8,128)S(1)} async-done(((f32[16,40,128]{2,1,0:T(8,128)}), f32[16,40,128]{2,1,0:T(8,128)S(1)}, u32[]{:S(2)}, u32[]{:S(2)}) %all-to-all-start.7) | async-done | bytes 327712 | tf_op jit(solution)/shard_map/all_to_all | solution.py:337
  234.3 5.9 %all-to-all-start.6 = ((bf16[128,64,128]{2,1,0:T(8,128)(2,1)}), bf16[128,64,128]{2,1,0:T(8,128)(2,1)}, u32[]{:S(2)}, u32[]{:S(2)}) async-start(bf16[128,64,128]{2,1,0:T(8,128)(2,1)} %get-tuple-element.38), calls=%async_computation.6 | async-start | bytes 4194304 | tf_op jit(solution)/shard_map/all_to_all | solution.py:312
  243.0 3.4 shard_map.99.part_ref
  247.6 6.8 %shard_map.100 = (f32[64,64]{1,0:T(8,128)S(1)}, bf16[32,64,128]{2,1,0:T(8,128)(2,1)S(1)}, f32[1,1]{1,0:T(1,128)}, f32[32,64,128]{2,1,0:T(8,128)S(1)}) custom-call(f32[40,128]{1,0:T(8,128)S(1)} %reduce_sum.37.sums_ref, bf16[32,64,128]{2,1,0:T(8,128)(2,1)S(1)} %copy-done.11, f32[32,64,128]{2,1,0:T(8,128)S(1)} %copy-done.15, ...), custom_call_target="tpu_custom_call" | custom-call | flops 16777216 | bytes 4194304 | tf_op jit(solution)/shard_map/pallas_call | solution.py:25
  256.3 13.9 %all-to-all-done.6.arrived_ref = bf16[128,64,128]{2,1,0:T(8,128)(2,1)} async-done(((bf16[128,64,128]{2,1,0:T(8,128)(2,1)}), bf16[128,64,128]{2,1,0:T(8,128)(2,1)}, u32[]{:S(2)}, u32[]{:S(2)}) %all-to-all-start.6) | async-done | bytes 2097184 | tf_op jit(solution)/shard_map/all_to_all | solution.py:312
  270.2 6.5 %shard_map.101 = (bf16[32,64,128]{2,1,0:T(8,128)(2,1)}, bf16[128,64,128]{2,1,0:T(8,128)(2,1)}) custom-call(s32[1,128]{1,0:T(1,128)S(1)} %copy-done.37, bf16[128,64,128]{2,1,0:T(8,128)(2,1)} %all-to-all-done.6.arrived_ref, bf16[128,128,128]{2,1,0:T(8,128)(2,1)} %tiles_ref.17, f32[32,64,128]{2,1,0:T(8,128)} %copy-done.31, ...), custom_call_target="tpu_custom_call" | custom-call | flops 268435456 | bytes 10485760 | tf_op jit(solution)/shard_map/pallas_call | solution.py:25
  276.7 4.7 %all-to-all-start.8 = ((bf16[128,64,128]{2,1,0:T(8,128)(2,1)}), bf16[128,64,128]{2,1,0:T(8,128)(2,1)S(1)}, u32[]{:S(2)}, u32[]{:S(2)}) async-start(bf16[128,64,128]{2,1,0:T(8,128)(2,1)} %get-tuple-element.42), calls=%async_computation.8 | async-start | bytes 4194304 | tf_op jit(solution)/shard_map/all_to_all | solution.py:312
  286.3 3.8 shard_map.102.part_ref
  291.1 20.7 %all-to-all-done.8.arrived_ref = bf16[128,64,128]{2,1,0:T(8,128)(2,1)S(1)} async-done(((bf16[128,64,128]{2,1,0:T(8,128)(2,1)}), bf16[128,64,128]{2,1,0:T(8,128)(2,1)S(1)}, u32[]{:S(2)}, u32[]{:S(2)}) %all-to-all-start.8) | async-done | bytes 2097184 | tf_op jit(solution)/shard_map/all_to_all | solution.py:312
  311.8 4.7 %shard_map.103 = (bf16[32,64,128]{2,1,0:T(8,128)(2,1)}, bf16[128,64,128]{2,1,0:T(8,128)(2,1)}) custom-call(s32[1,128]{1,0:T(1,128)S(1)} %copy-done.37, bf16[128,64,128]{2,1,0:T(8,128)(2,1)S(1)} %all-to-all-done.8.arrived_ref, bf16[128,128,128]{2,1,0:T(8,128)(2,1)} %tiles_ref.17, f32[32,64,128]{2,1,0:T(8,128)} %copy-done.20), custom_call_target="tpu_custom_call" | custom-call | flops 268435456 | bytes 10485760 | tf_op jit(solution)/shard_map/pallas_call | solution.py:25
  316.6 4.7 %all-to-all-start.9 = ((bf16[128,64,128]{2,1,0:T(8,128)(2,1)}), bf16[128,64,128]{2,1,0:T(8,128)(2,1)S(1)}, u32[]{:S(2)}, u32[]{:S(2)}) async-start(bf16[128,64,128]{2,1,0:T(8,128)(2,1)} %get-tuple-element.46), calls=%async_computation.9 | async-start | bytes 4194304 | tf_op jit(solution)/shard_map/all_to_all | solution.py:312
  326.1 3.8 shard_map.104.part_ref
  330.9 20.8 %all-to-all-done.9.arrived_ref = bf16[128,64,128]{2,1,0:T(8,128)(2,1)S(1)} async-done(((bf16[128,64,128]{2,1,0:T(8,128)(2,1)}), bf16[128,64,128]{2,1,0:T(8,128)(2,1)S(1)}, u32[]{:S(2)}, u32[]{:S(2)}) %all-to-all-start.9) | async-done | bytes 2097184 | tf_op jit(solution)/shard_map/all_to_all | solution.py:312
  351.7 4.7 %shard_map.105 = (bf16[32,64,128]{2,1,0:T(8,128)(2,1)}, bf16[128,64,128]{2,1,0:T(8,128)(2,1)}) custom-call(s32[1,128]{1,0:T(1,128)S(1)} %copy-done.37, bf16[128,64,128]{2,1,0:T(8,128)(2,1)S(1)} %all-to-all-done.9.arrived_ref, bf16[128,128,128]{2,1,0:T(8,128)(2,1)} %tiles_ref.17, f32[32,64,128]{2,1,0:T(8,128)} %copy-done.17), custom_call_target="tpu_custom_call" | custom-call | flops 268435456 | bytes 10485760 | tf_op jit(solution)/shard_map/pallas_call | solution.py:25
  356.4 6.2 %all-to-all-start.10 = ((bf16[128,64,128]{2,1,0:T(8,128)(2,1)}), bf16[128,64,128]{2,1,0:T(8,128)(2,1)}, u32[]{:S(2)}, u32[]{:S(2)}) async-start(bf16[128,64,128]{2,1,0:T(8,128)(2,1)} %get-tuple-element.48), calls=%async_computation.10 | async-start | bytes 4194304 | tf_op jit(solution)/shard_map/all_to_all | solution.py:312
  363.0 2.8 copy-done.8
  365.8 3.1 shard_map.106.part_ref
  370.0 22.6 %all-to-all-done.10.arrived_ref = bf16[128,64,128]{2,1,0:T(8,128)(2,1)} async-done(((bf16[128,64,128]{2,1,0:T(8,128)(2,1)}), bf16[128,64,128]{2,1,0:T(8,128)(2,1)}, u32[]{:S(2)}, u32[]{:S(2)}) %all-to-all-start.10) | async-done | bytes 2097184 | tf_op jit(solution)/shard_map/all_to_all | solution.py:312
  392.6 3.6 shard_map.108
  396.3 8.9 %all_to_all.66 = f32[8,40,128]{2,1,0:T(8,128)S(1)} all-to-all(f32[8,40,128]{2,1,0:T(8,128)S(1)} %broadcast_in_dim.10), channel_id=1, replica_groups={{0,1,2,3,4,5,6,7},{8,9,10,11,12,13,14,15},{16,17,18,19,20,21,22,23},{24..., dimensions={0} | all-to-all | bytes 327680 | tf_op jit(solution)/shard_map/all_to_all | solution.py:337
  405.2 12.1 %all_to_all.67 = f32[16,40,128]{2,1,0:T(8,128)S(1)} all-to-all(f32[16,40,128]{2,1,0:T(8,128)S(1)} %broadcast_in_dim.11), channel_id=1, replica_groups={{0,8,16,24,32,40,48,56,64,72,80,88,96,104,112,120},{1,9,17,25,33,41,49,..., dimensions={0} | all-to-all | bytes 655360 | tf_op jit(solution)/shard_map/all_to_all | solution.py:337
  417.3 5.7 %shard_map.109 = (bf16[64,4096]{1,0:T(8,128)(2,1)}, f32[64,64]{1,0:T(8,128)}) custom-call(f32[40,128]{1,0:T(8,128)S(1)} %reduce_sum.39.sums_ref, bf16[32,64,128]{2,1,0:T(8,128)(2,1)} %get-tuple-element.49.refs_0_.cur_ref), custom_call_target="tpu_custom_call" | custom-call | flops 16777216 | bytes 2097152 | tf_op jit(solution)/shard_map/pallas_call | solution.py:25
  (88 shorter events, 41.5 us)
Async XLA Ops:
  5.8 11.8 %copy-start.39 = (s32[1,96,2]{1,2,0:T(2,128)S(1)}, s32[1,96,2]{1,2,0:T(2,128)}, u32[]{:S(2)}) copy-start(s32[1,96,2]{1,2,0:T(2,128)} %param.12) | copy-start | bytes 2308
  5.9 11.8 %copy-start.9 = (bf16[32,128,128]{2,1,0:T(8,128)(2,1)S(1)}, bf16[32,128,128]{2,1,0:T(8,128)(2,1)}, u32[]{:S(2)}) copy-start(bf16[32,128,128]{2,1,0:T(8,128)(2,1)} %refs_1_.7) | copy-start | bytes 3145732
  5.9 41.6 %all-to-all-start = ((bf16[128,64,128]{2,1,0:T(8,128)(2,1)}), bf16[128,64,128]{2,1,0:T(8,128)(2,1)S(1)}, u32[]{:S(2)}, u32[]{:S(2)}) async-start(bf16[128,64,128]{2,1,0:T(8,128)(2,1)} %get-tuple-element.26), calls=%async_computation | async-start | bytes 4194304 | tf_op jit(solution)/shard_map/all_to_all | solution.py:312
  17.7 2.8 copy-start
  20.5 1.0 copy-start.24
  21.5 25.9 %copy-start.37 = (s32[1,128]{1,0:T(1,128)S(1)}, s32[1,128]{1,0:T(1,128)}, u32[]{:S(2)}) copy-start(s32[1,128]{1,0:T(1,128)} %rows_ref.21) | copy-start | bytes 1540
  24.7 1.0 copy-start.21
  52.2 35.1 %all-to-all-start.1 = ((bf16[128,64,128]{2,1,0:T(8,128)(2,1)}), bf16[128,64,128]{2,1,0:T(8,128)(2,1)S(1)}, u32[]{:S(2)}, u32[]{:S(2)}) async-start(bf16[128,64,128]{2,1,0:T(8,128)(2,1)} %get-tuple-element.28), calls=%async_computation.1 | async-start | bytes 4194304 | tf_op jit(solution)/shard_map/all_to_all | solution.py:312
  56.9 2.8 copy-start.1
  59.6 1.0 copy-start.25
  60.7 1.0 copy-start.28
  64.9 1.0 copy-start.18
  92.0 35.1 %all-to-all-start.2 = ((bf16[128,64,128]{2,1,0:T(8,128)(2,1)}), bf16[128,64,128]{2,1,0:T(8,128)(2,1)S(1)}, u32[]{:S(2)}, u32[]{:S(2)}) async-start(bf16[128,64,128]{2,1,0:T(8,128)(2,1)} %get-tuple-element.30), calls=%async_computation.2 | async-start | bytes 4194304 | tf_op jit(solution)/shard_map/all_to_all | solution.py:312
  96.7 2.8 copy-start.2
  99.5 1.0 copy-start.26
  100.5 1.0 copy-start.29
  104.7 1.0 copy-start.19
  131.8 35.1 %all-to-all-start.3 = ((bf16[128,64,128]{2,1,0:T(8,128)(2,1)}), bf16[128,64,128]{2,1,0:T(8,128)(2,1)S(1)}, u32[]{:S(2)}, u32[]{:S(2)}) async-start(bf16[128,64,128]{2,1,0:T(8,128)(2,1)} %get-tuple-element.32), calls=%async_computation.3 | async-start | bytes 4194304 | tf_op jit(solution)/shard_map/all_to_all | solution.py:312
  136.5 2.8 copy-start.3
  139.3 1.0 copy-start.27
  140.3 1.0 copy-start.34
  144.7 1.0 copy-start.16
  171.7 6.0 %copy-start.10 = (bf16[32,64,128]{2,1,0:T(8,128)(2,1)S(1)}, bf16[32,64,128]{2,1,0:T(8,128)(2,1)}, u32[]{:S(2)}) copy-start(bf16[32,64,128]{2,1,0:T(8,128)(2,1)} %get-tuple-element.35.refs_0_.cur_ref) | copy-start | bytes 1572868
  171.7 36.0 %all-to-all-start.4 = ((bf16[128,64,128]{2,1,0:T(8,128)(2,1)}), bf16[128,64,128]{2,1,0:T(8,128)(2,1)}, u32[]{:S(2)}, u32[]{:S(2)}) async-start(bf16[128,64,128]{2,1,0:T(8,128)(2,1)} %get-tuple-element.34), calls=%async_computation.4 | async-start | bytes 4194304 | tf_op jit(solution)/shard_map/all_to_all | solution.py:312
  178.0 2.8 copy-start.4
  184.0 1.0 copy-start.14
  220.6 4.3 %copy-start.38 = (f32[40,128]{1,0:T(8,128)}, f32[40,128]{1,0:T(8,128)S(1)}, u32[]{:S(2)}) copy-start(f32[40,128]{1,0:T(8,128)S(1)} %reduce_sum.36.near_ref) | copy-start | bytes 61444
  221.3 12.9 %all-to-all-start.7 = ((f32[16,40,128]{2,1,0:T(8,128)}), f32[16,40,128]{2,1,0:T(8,128)S(1)}, u32[]{:S(2)}, u32[]{:S(2)}) async-start(f32[16,40,128]{2,1,0:T(8,128)} %broadcast_in_dim.9), calls=%async_computation.7 | async-start | bytes 655360 | tf_op jit(solution)/shard_map/all_to_all | solution.py:337
  234.3 5.9 %copy-start.30 = (bf16[32,64,128]{2,1,0:T(8,128)(2,1)S(1)}, bf16[32,64,128]{2,1,0:T(8,128)(2,1)}, u32[]{:S(2)}) copy-start(bf16[32,64,128]{2,1,0:T(8,128)(2,1)} %get-tuple-element.39.refs_0_.z_ref) | copy-start | bytes 1572868
  234.3 35.9 %all-to-all-start.6 = ((bf16[128,64,128]{2,1,0:T(8,128)(2,1)}), bf16[128,64,128]{2,1,0:T(8,128)(2,1)}, u32[]{:S(2)}, u32[]{:S(2)}) async-start(bf16[128,64,128]{2,1,0:T(8,128)(2,1)} %get-tuple-element.38), calls=%async_computation.6 | async-start | bytes 4194304 | tf_op jit(solution)/shard_map/all_to_all | solution.py:312
  240.2 2.8 copy-start.5
  243.0 3.4 copy-start.11
  246.4 1.2 copy-start.15
  254.4 1.0 copy-start.31
  276.7 35.1 %all-to-all-start.8 = ((bf16[128,64,128]{2,1,0:T(8,128)(2,1)}), bf16[128,64,128]{2,1,0:T(8,128)(2,1)S(1)}, u32[]{:S(2)}, u32[]{:S(2)}) async-start(bf16[128,64,128]{2,1,0:T(8,128)(2,1)} %get-tuple-element.42), calls=%async_computation.8 | async-start | bytes 4194304 | tf_op jit(solution)/shard_map/all_to_all | solution.py:312
  281.4 2.8 copy-start.6
  284.2 1.0 copy-start.22
  285.2 1.0 copy-start.33
  290.1 1.0 copy-start.20
  316.6 35.1 %all-to-all-start.9 = ((bf16[128,64,128]{2,1,0:T(8,128)(2,1)}), bf16[128,64,128]{2,1,0:T(8,128)(2,1)S(1)}, u32[]{:S(2)}, u32[]{:S(2)}) async-start(bf16[128,64,128]{2,1,0:T(8,128)(2,1)} %get-tuple-element.46), calls=%async_computation.9 | async-start | bytes 4194304 | tf_op jit(solution)/shard_map/all_to_all | solution.py:312
  321.2 2.8 copy-start.7
  324.0 1.0 copy-start.23
  325.1 1.0 copy-start.35
  329.9 1.0 copy-start.17
  356.4 6.2 %copy-start.12 = (bf16[32,64,128]{2,1,0:T(8,128)(2,1)S(1)}, bf16[32,64,128]{2,1,0:T(8,128)(2,1)}, u32[]{:S(2)}) copy-start(bf16[32,64,128]{2,1,0:T(8,128)(2,1)} %get-tuple-element.49.refs_0_.cur_ref) | copy-start | bytes 1572868
  356.4 36.2 %all-to-all-start.10 = ((bf16[128,64,128]{2,1,0:T(8,128)(2,1)}), bf16[128,64,128]{2,1,0:T(8,128)(2,1)}, u32[]{:S(2)}, u32[]{:S(2)}) async-start(bf16[128,64,128]{2,1,0:T(8,128)(2,1)} %get-tuple-element.48), calls=%async_computation.10 | async-start | bytes 4194304 | tf_op jit(solution)/shard_map/all_to_all | solution.py:312
  363.0 2.8 copy-start.8
  368.9 1.0 copy-start.13
  (2 other events, 1.5 us)

commit v7 on v5

--- a/solution.py
+++ b/solution.py
@@ -77,15 +77,17 @@
         acc[rows_ref[0, p]] += arrived_ref[p].astype(F32)
 
 
-def start_kernel(rows_ref, vec_ref, tiles_ref, cur_ref, out_ref, tiles, vec, block, slots, loads, sems):
+def start_kernel(rows_ref, vec_ref, tiles_ref, cur_ref, out_ref, rows, tiles, vec, block, slots, loads, sems):
     first = begin(vec_ref, vec, loads.at[CHUNKS])
+    also = begin(rows_ref, rows, loads.at[CHUNKS + 1])
     coming = load(tiles_ref, tiles, loads)
     first.wait()
     width = block.shape[2]
     for r in range(block.shape[0]):
         block[r] = vec[:, r * width : (r + 1) * width]
+    also.wait()
     going = [begin(block, cur_ref, loads.at[CHUNKS + 1])]
-    going += send(rows_ref, block, tiles, coming, slots, out_ref, sems)
+    going += send(rows, block, tiles, coming, slots, out_ref, sems)
     for copy in going:
         copy.wait()
 
@@ -195,22 +197,35 @@
 
 
 def inverse_factor(gram):
-    n = gram.shape[0]
-    row = lax.broadcasted_iota(jnp.int32, (n, n), 0)
-    col = lax.broadcasted_iota(jnp.int32, (n, n), 1)
+    n, some = gram.shape[0], 8
+    row, col = corner(n)
     work = jnp.concatenate([gram, jnp.where(row == col, 1.0, 0.0).astype(F32)], axis=1)
-    at = lax.broadcasted_iota(jnp.int32, work.shape, 0)
-    for j in range(0, n, 2):
-        first = jnp.broadcast_to(work[:, j : j + 1], work.shape)
-        second = jnp.broadcast_to(work[:, j + 1 : j + 2], work.shape)
-        over = 1.0 / first[j : j + 1]
-        low = first[j + 1 : j + 2] * over
-        upper = second[j : j + 1]
-        under = 1.0 / (second[j + 1 : j + 2] - low * upper)
-        below = work[j + 1 : j + 2] - low * work[j : j + 1]
-        times = first * over
-        again = jnp.where(at > j + 1, (second - times * upper) * under, 0.0)
-        work = work - jnp.where(at > j, times, 0.0) * work[j : j + 1] - again * below
+    parts = [work[b : b + some] for b in range(0, n, some)]
+    at = lax.broadcasted_iota(jnp.int32, parts[0].shape, 0)
+    for own in range(len(parts)):
+        live = parts[own:]
+        columns = [[jnp.broadcast_to(part[:, own * some + g : own * some + g + 1], part.shape) for part in live] for g in range(some)]
+        pivot = [[columns[h][0][g : g + 1] for h in range(some)] for g in range(some)]
+        rows = [live[0][g : g + 1] for g in range(some)]
+        over = []
+        for g in range(some):
+            over.append(1.0 / pivot[g][g])
+            for h in range(g + 1, some):
+                low = pivot[h][g] * over[g]
+                rows[h] = rows[h] - low * rows[g]
+                for x in range(g + 1, some):
+                    pivot[h][x] = pivot[h][x] - low * pivot[g][x]
+        for i, part in enumerate(live):
+            times = []
+            for g in range(some):
+                value = columns[g][i]
+                for h in range(g):
+                    value = value - times[h] * pivot[h][g]
+                times.append(value * over[g])
+            for g in range(some):
+                part = part - (jnp.where(at > g, times[g], 0.0) if i == 0 else times[g]) * rows[g]
+            parts[own + i] = part
+    work = jnp.concatenate(parts, axis=0)
     pivots = jnp.sum(jnp.where(row == col, work[:, :n], 0.0), axis=1, keepdims=True)
     return work[:, n:] / jnp.sqrt(pivots)
 
@@ -252,7 +267,7 @@
         copy.wait()
 
 
-def end_kernel(total, sums_ref, cur_ref, basis_ref, ritz_ref, cur, sems):
+def end_kernel(total, sums_ref, cur_ref, basis_ref, ritz_ref, cur, basis, sems):
     coming = begin(cur_ref, cur, sems.at[0])
     width = cur.shape[2]
     gram, product = unpacked(sums_ref[...])
@@ -260,9 +275,11 @@
     stack = jnp.concatenate(thirds(inverse), axis=0)
     coming.wait()
     for r in range(cur.shape[0]):
-        basis_ref[:, r * width : (r + 1) * width] = apply_square(stack, cur[r]).astype(BF16)
+        basis[:, r * width : (r + 1) * width] = apply_square(stack, cur[r]).astype(BF16)
+    going = begin(basis, basis_ref, sems.at[1])
     half = jnp.dot(inverse, product / total, precision=HI, preferred_element_type=F32)
     ritz_ref[...] = mm_t(half, inverse, HI)
+    going.wait()
 
 
 def local(vectors, diag_tiles, pair_tiles, halo_tiles, halo_rows, pair_index, pair_count):
@@ -324,10 +341,11 @@
     start, out = call(
         start_kernel,
         [(block, BF16, "a"), (spots, BF16, "a")],
-        [(halo_rows, "s"), (vectors, "a"), (halo_tiles, "a")],
+        [(halo_rows, "a"), (vectors, "a"), (halo_tiles, "a")],
         unit * peers,
         8 << 20,
-        [room(halo_tiles.shape, BF16), room(vectors.shape, BF16), room(block, BF16), room(spots, BF16), loads, sems],
+        [pltpu.SMEM(halo_rows.shape, jnp.int32), room(halo_tiles.shape, BF16), room(vectors.shape, BF16)]
+        + [room(block, BF16), room(spots, BF16), loads, sems],
     )
     arrived = exchange(out)
     cur, out = halo(1.0, arrived, own("start", start))
@@ -350,11 +368,11 @@
     [value] = sums(cur, arrived, own("image", cur), 0)
     return call(
         functools.partial(end_kernel, total),
-        [((k, own_rows), BF16, "h"), (square, F32, "h")],
+        [((k, own_rows), BF16, "a"), (square, F32, "h")],
         [(value, "h"), (cur, "a")],
         1 << 24,
         2 << 20,
-        [room(block, BF16), sems],
+        [room(block, BF16), room(vectors.shape, BF16), sems],
     )
 
 

time: 428 us -> 425 us (level)
  Pallas kernels: 125 us -> 98.9 us
  waiting for transfers between devices: 158 us -> 181 us
    pallas_call x23, Pallas kernels: 125 us -> 98.9 us  [call(): pl.pallas_call(body, out_shape=[(place[kind] if kind in place else jax.Sh...]
    all_to_all x9, waiting for transfers between devices: 158 us -> 181 us  [exchange(): return lax.all_to_all(out, 'dom', 0, 0, tiled=True)]
    unnamed x76 -> x74, local copies, waits for them, and re-layouts: 50.1 us -> 49.3 us
  transfers between devices with their start and end apart: 9 -> 9, of which waited for: 9 -> 9; matrix products, arithmetic and copies ran while one was open for 0% -> 0% of each run, Pallas kernels for 15% -> 10%
where the time goes in v7:
time: 425 us; the launch traced here: 423 us
  waiting for transfers between devices  181 us (43%)
  Pallas kernels  98.9 us (23%)
  starting transfers between devices  50 us (12%)
  local copies, waits for them, and re-layouts  49.4 us (12%)
  blocking collectives  41.9 us (10%)
    all_to_all x9, waiting for transfers between devices, exchange(): return lax.all_to_all(out, 'dom', 0, 0, tiled=True)  181 us
    pallas_call x23, Pallas kernels, call(): pl.pallas_call(body, out_shape=[(place[kind] if kind in place else jax.Sh...  98.9 us
    all_to_all x9, starting transfers between devices, exchange(): return lax.all_to_all(out, 'dom', 0, 0, tiled=True)  50 us
    unnamed x74, local copies, waits for them, and re-layouts  49.3 us
    all_to_all x4, blocking collectives, everywhere(): lax.all_to_all(many, 'dom', 0, 0, axis_index_groups=groups, tiled=True)  41.9 us
  transfers between devices with their start and end apart: 9, of which 9 were waited for; matrix products, arithmetic and copies ran while one was open for 0% of the time, Pallas kernels for 10%

profile of v7, /device:TPU:0, one launch (start us, length us, event | category | flops | bytes accessed | tf_op | source)
XLA Modules:
  0.0 422.8 jit_solution(6645870742030655685)
XLA Ops:
  0.6 4.0 shard_map.86
  4.7 11.2 %all-to-all-start = ((bf16[128,64,128]{2,1,0:T(8,128)(2,1)}), bf16[128,64,128]{2,1,0:T(8,128)(2,1)S(1)}, u32[]{:S(2)}, u32[]{:S(2)}) async-start(bf16[128,64,128]{2,1,0:T(8,128)(2,1)} %get-tuple-element.24), calls=%async_computation | async-start | bytes 4194304 | tf_op jit(solution)/shard_map/all_to_all | solution.py:301
  16.5 2.8 copy-done
  20.3 4.4 %shard_map.87.part_ref = f32[32,64,128]{2,1,0:T(8,128)S(1)} custom-call(s32[96]{0:T(128)S(1)} %get-tuple-element.47.first_ref, s32[96]{0:T(128)S(1)} %get-tuple-element.46.second_ref, s32[1]{0:T(128)S(6)} %copy.9.count_ref, bf16[32,64,128]{2,1,0:T(8,128)(2,1)S(1)} %copy-done.22, bf16[32,128,128]{2,1,0:T(8,128)(2,1)S(1)} %copy-done.9, ...), custom_call_target="tpu_custom_call" | custom-call | flops 469762048 | bytes 9437184 | tf_op jit(solution)/shard_map/pallas_call | solution.py:25
  25.7 20.5 %all-to-all-done.arrived_ref = bf16[128,64,128]{2,1,0:T(8,128)(2,1)S(1)} async-done(((bf16[128,64,128]{2,1,0:T(8,128)(2,1)}), bf16[128,64,128]{2,1,0:T(8,128)(2,1)S(1)}, u32[]{:S(2)}, u32[]{:S(2)}) %all-to-all-start) | async-done | bytes 2097184 | tf_op jit(solution)/shard_map/all_to_all | solution.py:301
  46.2 4.7 %shard_map.88 = (bf16[32,64,128]{2,1,0:T(8,128)(2,1)}, bf16[128,64,128]{2,1,0:T(8,128)(2,1)}) custom-call(s32[1,128]{1,0:T(1,128)S(1)} %copy-done.35, bf16[128,64,128]{2,1,0:T(8,128)(2,1)S(1)} %all-to-all-done.arrived_ref, bf16[128,128,128]{2,1,0:T(8,128)(2,1)} %tiles_ref.17, f32[32,64,128]{2,1,0:T(8,128)} %copy-done.21), custom_call_target="tpu_custom_call" | custom-call | flops 268435456 | bytes 10485760 | tf_op jit(solution)/shard_map/pallas_call | solution.py:25
  50.9 4.7 %all-to-all-start.1 = ((bf16[128,64,128]{2,1,0:T(8,128)(2,1)}), bf16[128,64,128]{2,1,0:T(8,128)(2,1)S(1)}, u32[]{:S(2)}, u32[]{:S(2)}) async-start(bf16[128,64,128]{2,1,0:T(8,128)(2,1)} %get-tuple-element.26), calls=%async_computation.1 | async-start | bytes 4194304 | tf_op jit(solution)/shard_map/all_to_all | solution.py:301
  60.5 4.4 %shard_map.89.part_ref = f32[32,64,128]{2,1,0:T(8,128)S(1)} custom-call(s32[96]{0:T(128)S(1)} %get-tuple-element.47.first_ref, s32[96]{0:T(128)S(1)} %get-tuple-element.46.second_ref, s32[1]{0:T(128)S(6)} %copy.9.count_ref, f32[1,1]{1,0:T(1,128)} %constant.0.clone.1.refs_0_, bf16[32,64,128]{2,1,0:T(8,128)(2,1)S(1)} %copy-done.30, ...), custom_call_target="tpu_custom_call" | custom-call | flops 469762048 | bytes 9437184 | tf_op jit(solution)/shard_map/pallas_call | solution.py:25
  65.9 20.2 %all-to-all-done.1.arrived_ref = bf16[128,64,128]{2,1,0:T(8,128)(2,1)S(1)} async-done(((bf16[128,64,128]{2,1,0:T(8,128)(2,1)}), bf16[128,64,128]{2,1,0:T(8,128)(2,1)S(1)}, u32[]{:S(2)}, u32[]{:S(2)}) %all-to-all-start.1) | async-done | bytes 2097184 | tf_op jit(solution)/shard_map/all_to_all | solution.py:301
  86.0 4.7 %shard_map.90 = (bf16[32,64,128]{2,1,0:T(8,128)(2,1)}, bf16[128,64,128]{2,1,0:T(8,128)(2,1)}) custom-call(s32[1,128]{1,0:T(1,128)S(1)} %copy-done.35, bf16[128,64,128]{2,1,0:T(8,128)(2,1)S(1)} %all-to-all-done.1.arrived_ref, bf16[128,128,128]{2,1,0:T(8,128)(2,1)} %tiles_ref.17, f32[32,64,128]{2,1,0:T(8,128)} %copy-done.17), custom_call_target="tpu_custom_call" | custom-call | flops 268435456 | bytes 10485760 | tf_op jit(solution)/shard_map/pallas_call | solution.py:25
  90.7 4.7 %all-to-all-start.2 = ((bf16[128,64,128]{2,1,0:T(8,128)(2,1)}), bf16[128,64,128]{2,1,0:T(8,128)(2,1)S(1)}, u32[]{:S(2)}, u32[]{:S(2)}) async-start(bf16[128,64,128]{2,1,0:T(8,128)(2,1)} %get-tuple-element.28), calls=%async_computation.2 | async-start | bytes 4194304 | tf_op jit(solution)/shard_map/all_to_all | solution.py:301
  95.4 2.8 copy-done.2
  100.3 4.4 %shard_map.91.part_ref = f32[32,64,128]{2,1,0:T(8,128)S(1)} custom-call(s32[96]{0:T(128)S(1)} %get-tuple-element.47.first_ref, s32[96]{0:T(128)S(1)} %get-tuple-element.46.second_ref, s32[1]{0:T(128)S(6)} %copy.9.count_ref, f32[1,1]{1,0:T(1,128)} %constant.0.clone.1.refs_0_, bf16[32,64,128]{2,1,0:T(8,128)(2,1)S(1)} %copy-done.26, ...), custom_call_target="tpu_custom_call" | custom-call | flops 469762048 | bytes 9437184 | tf_op jit(solution)/shard_map/pallas_call | solution.py:25
  105.7 20.2 %all-to-all-done.2.arrived_ref = bf16[128,64,128]{2,1,0:T(8,128)(2,1)S(1)} async-done(((bf16[128,64,128]{2,1,0:T(8,128)(2,1)}), bf16[128,64,128]{2,1,0:T(8,128)(2,1)S(1)}, u32[]{:S(2)}, u32[]{:S(2)}) %all-to-all-start.2) | async-done | bytes 2097184 | tf_op jit(solution)/shard_map/all_to_all | solution.py:301
  125.9 4.7 %shard_map.92 = (bf16[32,64,128]{2,1,0:T(8,128)(2,1)}, bf16[128,64,128]{2,1,0:T(8,128)(2,1)}) custom-call(s32[1,128]{1,0:T(1,128)S(1)} %copy-done.35, bf16[128,64,128]{2,1,0:T(8,128)(2,1)S(1)} %all-to-all-done.2.arrived_ref, bf16[128,128,128]{2,1,0:T(8,128)(2,1)} %tiles_ref.17, f32[32,64,128]{2,1,0:T(8,128)} %copy-done.18), custom_call_target="tpu_custom_call" | custom-call | flops 268435456 | bytes 10485760 | tf_op jit(solution)/shard_map/pallas_call | solution.py:25
  130.6 4.7 %all-to-all-start.3 = ((bf16[128,64,128]{2,1,0:T(8,128)(2,1)}), bf16[128,64,128]{2,1,0:T(8,128)(2,1)S(1)}, u32[]{:S(2)}, u32[]{:S(2)}) async-start(bf16[128,64,128]{2,1,0:T(8,128)(2,1)} %get-tuple-element.30), calls=%async_computation.3 | async-start | bytes 4194304 | tf_op jit(solution)/shard_map/all_to_all | solution.py:301
  140.1 4.6 %shard_map.93.part_ref = f32[32,64,128]{2,1,0:T(8,128)S(1)} custom-call(s32[96]{0:T(128)S(1)} %get-tuple-element.47.first_ref, s32[96]{0:T(128)S(1)} %get-tuple-element.46.second_ref, s32[1]{0:T(128)S(6)} %copy.9.count_ref, f32[1,1]{1,0:T(1,128)} %constant.0.clone.1.refs_0_, bf16[32,64,128]{2,1,0:T(8,128)(2,1)S(1)} %copy-done.33, ...), custom_call_target="tpu_custom_call" | custom-call | flops 469762048 | bytes 9437184 | tf_op jit(solution)/shard_map/pallas_call | solution.py:25
  145.7 20.0 %all-to-all-done.3.arrived_ref = bf16[128,64,128]{2,1,0:T(8,128)(2,1)S(1)} async-done(((bf16[128,64,128]{2,1,0:T(8,128)(2,1)}), bf16[128,64,128]{2,1,0:T(8,128)(2,1)S(1)}, u32[]{:S(2)}, u32[]{:S(2)}) %all-to-all-start.3) | async-done | bytes 2097184 | tf_op jit(solution)/shard_map/all_to_all | solution.py:301
  165.7 4.7 %shard_map.94 = (bf16[32,64,128]{2,1,0:T(8,128)(2,1)}, bf16[128,64,128]{2,1,0:T(8,128)(2,1)}) custom-call(s32[1,128]{1,0:T(1,128)S(1)} %copy-done.35, bf16[128,64,128]{2,1,0:T(8,128)(2,1)S(1)} %all-to-all-done.3.arrived_ref, bf16[128,128,128]{2,1,0:T(8,128)(2,1)} %tiles_ref.17, f32[32,64,128]{2,1,0:T(8,128)} %copy-done.15), custom_call_target="tpu_custom_call" | custom-call | flops 268435456 | bytes 10485760 | tf_op jit(solution)/shard_map/pallas_call | solution.py:25
  170.4 4.7 %all-to-all-start.4 = ((bf16[128,64,128]{2,1,0:T(8,128)(2,1)}), bf16[128,64,128]{2,1,0:T(8,128)(2,1)S(1)}, u32[]{:S(2)}, u32[]{:S(2)}) async-start(bf16[128,64,128]{2,1,0:T(8,128)(2,1)} %get-tuple-element.32), calls=%async_computation.4 | async-start | bytes 4194304 | tf_op jit(solution)/shard_map/all_to_all | solution.py:301
  176.5 2.8 copy-done.4
  180.3 4.4 %shard_map.95.part_ref = f32[32,64,128]{2,1,0:T(8,128)S(1)} custom-call(s32[96]{0:T(128)S(1)} %get-tuple-element.47.first_ref, s32[96]{0:T(128)S(1)} %get-tuple-element.46.second_ref, s32[1]{0:T(128)S(6)} %copy.9.count_ref, bf16[32,64,128]{2,1,0:T(8,128)(2,1)S(1)} %copy-done.12, bf16[32,128,128]{2,1,0:T(8,128)(2,1)S(1)} %copy-done.9, ...), custom_call_target="tpu_custom_call" | custom-call | flops 469762048 | bytes 9437184 | tf_op jit(solution)/shard_map/pallas_call | solution.py:25
  185.7 19.8 %all-to-all-done.4.arrived_ref = bf16[128,64,128]{2,1,0:T(8,128)(2,1)S(1)} async-done(((bf16[128,64,128]{2,1,0:T(8,128)(2,1)}), bf16[128,64,128]{2,1,0:T(8,128)(2,1)S(1)}, u32[]{:S(2)}, u32[]{:S(2)}) %all-to-all-start.4) | async-done | bytes 2097184 | tf_op jit(solution)/shard_map/all_to_all | solution.py:301
  205.5 2.9 shard_map.97
  208.4 8.9 %all_to_all.65 = f32[8,40,128]{2,1,0:T(8,128)S(1)} all-to-all(f32[8,40,128]{2,1,0:T(8,128)S(1)} %broadcast_in_dim.8), channel_id=1, replica_groups={{0,1,2,3,4,5,6,7},{8,9,10,11,12,13,14,15},{16,17,18,19,20,21,22,23},{24..., dimensions={0} | all-to-all | bytes 327680 | tf_op jit(solution)/shard_map/all_to_all | solution.py:323
  217.3 12.1 %all_to_all.66 = f32[16,40,128]{2,1,0:T(8,128)S(1)} all-to-all(f32[16,40,128]{2,1,0:T(8,128)S(1)} %broadcast_in_dim.9), channel_id=1, replica_groups={{0,8,16,24,32,40,48,56,64,72,80,88,96,104,112,120},{1,9,17,25,33,41,49,..., dimensions={0} | all-to-all | bytes 655360 | tf_op jit(solution)/shard_map/all_to_all | solution.py:323
  229.4 8.2 %shard_map.98 = (bf16[32,64,128]{2,1,0:T(8,128)(2,1)}, bf16[32,64,128]{2,1,0:T(8,128)(2,1)}, bf16[128,64,128]{2,1,0:T(8,128)(2,1)}, f32[1,1]{1,0:T(1,128)}) custom-call(s32[1,128]{1,0:T(1,128)S(1)} %copy-done.35, f32[40,128]{1,0:T(8,128)S(1)} %reduce_sum.37.sums_ref, bf16[32,64,128]{2,1,0:T(8,128)(2,1)} %get-tuple-element.33.refs_0_.cur_ref, ...), custom_call_target="tpu_custom_call" | custom-call | flops 16777216 | bytes 4194304 | tf_op jit(solution)/shard_map/pallas_call | solution.py:25
  237.6 4.7 %all-to-all-start.7 = ((bf16[128,64,128]{2,1,0:T(8,128)(2,1)}), bf16[128,64,128]{2,1,0:T(8,128)(2,1)S(1)}, u32[]{:S(2)}, u32[]{:S(2)}) async-start(bf16[128,64,128]{2,1,0:T(8,128)(2,1)} %get-tuple-element.36), calls=%async_computation.7 | async-start | bytes 4194304 | tf_op jit(solution)/shard_map/all_to_all | solution.py:301
  247.1 5.1 %shard_map.99.part_ref = f32[32,64,128]{2,1,0:T(8,128)S(1)} custom-call(s32[96]{0:T(128)S(1)} %get-tuple-element.47.first_ref, s32[96]{0:T(128)S(1)} %get-tuple-element.46.second_ref, s32[1]{0:T(128)S(6)} %copy.9.count_ref, f32[1,1]{1,0:T(1,128)} %get-tuple-element.37.refs_0_, bf16[32,64,128]{2,1,0:T(8,128)(2,1)S(1)} %copy-done.24, ...), custom_call_target="tpu_custom_call" | custom-call | flops 469762048 | bytes 9437184 | tf_op jit(solution)/shard_map/pallas_call | solution.py:25
  253.2 19.5 %all-to-all-done.7.arrived_ref = bf16[128,64,128]{2,1,0:T(8,128)(2,1)S(1)} async-done(((bf16[128,64,128]{2,1,0:T(8,128)(2,1)}), bf16[128,64,128]{2,1,0:T(8,128)(2,1)S(1)}, u32[]{:S(2)}, u32[]{:S(2)}) %all-to-all-start.7) | async-done | bytes 2097184 | tf_op jit(solution)/shard_map/all_to_all | solution.py:301
  272.7 4.7 %shard_map.100 = (bf16[32,64,128]{2,1,0:T(8,128)(2,1)}, bf16[128,64,128]{2,1,0:T(8,128)(2,1)}) custom-call(s32[1,128]{1,0:T(1,128)S(1)} %copy-done.35, bf16[128,64,128]{2,1,0:T(8,128)(2,1)S(1)} %all-to-all-done.7.arrived_ref, bf16[128,128,128]{2,1,0:T(8,128)(2,1)} %tiles_ref.17, f32[32,64,128]{2,1,0:T(8,128)} %copy-done.19), custom_call_target="tpu_custom_call" | custom-call | flops 268435456 | bytes 10485760 | tf_op jit(solution)/shard_map/pallas_call | solution.py:25
  277.4 4.9 %all-to-all-start.8 = ((bf16[128,64,128]{2,1,0:T(8,128)(2,1)}), bf16[128,64,128]{2,1,0:T(8,128)(2,1)S(1)}, u32[]{:S(2)}, u32[]{:S(2)}) async-start(bf16[128,64,128]{2,1,0:T(8,128)(2,1)} %get-tuple-element.40), calls=%async_computation.8 | async-start | bytes 4194304 | tf_op jit(solution)/shard_map/all_to_all | solution.py:301
  287.2 5.1 %shard_map.101.part_ref = f32[32,64,128]{2,1,0:T(8,128)S(1)} custom-call(s32[96]{0:T(128)S(1)} %get-tuple-element.47.first_ref, s32[96]{0:T(128)S(1)} %get-tuple-element.46.second_ref, s32[1]{0:T(128)S(6)} %copy.9.count_ref, f32[1,1]{1,0:T(1,128)} %get-tuple-element.37.refs_0_, bf16[32,64,128]{2,1,0:T(8,128)(2,1)S(1)} %copy-done.28, ...), custom_call_target="tpu_custom_call" | custom-call | flops 469762048 | bytes 9437184 | tf_op jit(solution)/shard_map/pallas_call | solution.py:25
  293.2 19.5 %all-to-all-done.8.arrived_ref = bf16[128,64,128]{2,1,0:T(8,128)(2,1)S(1)} async-done(((bf16[128,64,128]{2,1,0:T(8,128)(2,1)}), bf16[128,64,128]{2,1,0:T(8,128)(2,1)S(1)}, u32[]{:S(2)}, u32[]{:S(2)}) %all-to-all-start.8) | async-done | bytes 2097184 | tf_op jit(solution)/shard_map/all_to_all | solution.py:301
  312.7 4.7 %shard_map.102 = (bf16[32,64,128]{2,1,0:T(8,128)(2,1)}, bf16[128,64,128]{2,1,0:T(8,128)(2,1)}) custom-call(s32[1,128]{1,0:T(1,128)S(1)} %copy-done.35, bf16[128,64,128]{2,1,0:T(8,128)(2,1)S(1)} %all-to-all-done.8.arrived_ref, bf16[128,128,128]{2,1,0:T(8,128)(2,1)} %tiles_ref.17, f32[32,64,128]{2,1,0:T(8,128)} %copy-done.20), custom_call_target="tpu_custom_call" | custom-call | flops 268435456 | bytes 10485760 | tf_op jit(solution)/shard_map/pallas_call | solution.py:25
  317.4 4.7 %all-to-all-start.9 = ((bf16[128,64,128]{2,1,0:T(8,128)(2,1)}), bf16[128,64,128]{2,1,0:T(8,128)(2,1)S(1)}, u32[]{:S(2)}, u32[]{:S(2)}) async-start(bf16[128,64,128]{2,1,0:T(8,128)(2,1)} %get-tuple-element.42), calls=%async_computation.9 | async-start | bytes 4194304 | tf_op jit(solution)/shard_map/all_to_all | solution.py:301
  322.1 2.8 copy-done.7
  327.0 5.1 %shard_map.103.part_ref = f32[32,64,128]{2,1,0:T(8,128)S(1)} custom-call(s32[96]{0:T(128)S(1)} %get-tuple-element.47.first_ref, s32[96]{0:T(128)S(1)} %get-tuple-element.46.second_ref, s32[1]{0:T(128)S(6)} %copy.9.count_ref, f32[1,1]{1,0:T(1,128)} %get-tuple-element.37.refs_0_, bf16[32,64,128]{2,1,0:T(8,128)(2,1)S(1)} %copy-done.34, ...), custom_call_target="tpu_custom_call" | custom-call | flops 469762048 | bytes 9437184 | tf_op jit(solution)/shard_map/pallas_call | solution.py:25
  333.0 19.5 %all-to-all-done.9.arrived_ref = bf16[128,64,128]{2,1,0:T(8,128)(2,1)S(1)} async-done(((bf16[128,64,128]{2,1,0:T(8,128)(2,1)}), bf16[128,64,128]{2,1,0:T(8,128)(2,1)S(1)}, u32[]{:S(2)}, u32[]{:S(2)}) %all-to-all-start.9) | async-done | bytes 2097184 | tf_op jit(solution)/shard_map/all_to_all | solution.py:301
  352.5 4.7 %shard_map.104 = (bf16[32,64,128]{2,1,0:T(8,128)(2,1)}, bf16[128,64,128]{2,1,0:T(8,128)(2,1)}) custom-call(s32[1,128]{1,0:T(1,128)S(1)} %copy-done.35, bf16[128,64,128]{2,1,0:T(8,128)(2,1)S(1)} %all-to-all-done.9.arrived_ref, bf16[128,128,128]{2,1,0:T(8,128)(2,1)} %tiles_ref.17, f32[32,64,128]{2,1,0:T(8,128)} %copy-done.16), custom_call_target="tpu_custom_call" | custom-call | flops 268435456 | bytes 10485760 | tf_op jit(solution)/shard_map/pallas_call | solution.py:25
  357.2 5.9 %all-to-all-start.10 = ((bf16[128,64,128]{2,1,0:T(8,128)(2,1)}), bf16[128,64,128]{2,1,0:T(8,128)(2,1)}, u32[]{:S(2)}, u32[]{:S(2)}) async-start(bf16[128,64,128]{2,1,0:T(8,128)(2,1)} %get-tuple-element.44), calls=%async_computation.10 | async-start | bytes 4194304 | tf_op jit(solution)/shard_map/all_to_all | solution.py:301
  363.6 2.8 copy-done.8
  366.4 4.4 %shard_map.105.part_ref = f32[32,64,128]{2,1,0:T(8,128)S(1)} custom-call(s32[96]{0:T(128)S(1)} %get-tuple-element.47.first_ref, s32[96]{0:T(128)S(1)} %get-tuple-element.46.second_ref, s32[1]{0:T(128)S(6)} %copy.9.count_ref, bf16[32,64,128]{2,1,0:T(8,128)(2,1)S(1)} %copy-done.10, bf16[32,128,128]{2,1,0:T(8,128)(2,1)S(1)} %copy-done.9, ...), custom_call_target="tpu_custom_call" | custom-call | flops 469762048 | bytes 9437184 | tf_op jit(solution)/shard_map/pallas_call | solution.py:25
  371.8 21.4 %all-to-all-done.10.arrived_ref = bf16[128,64,128]{2,1,0:T(8,128)(2,1)} async-done(((bf16[128,64,128]{2,1,0:T(8,128)(2,1)}), bf16[128,64,128]{2,1,0:T(8,128)(2,1)}, u32[]{:S(2)}, u32[]{:S(2)}) %all-to-all-start.10) | async-done | bytes 2097184 | tf_op jit(solution)/shard_map/all_to_all | solution.py:301
  393.2 3.6 shard_map.107
  396.8 8.9 %all_to_all.67 = f32[8,40,128]{2,1,0:T(8,128)S(1)} all-to-all(f32[8,40,128]{2,1,0:T(8,128)S(1)} %broadcast_in_dim.10), channel_id=1, replica_groups={{0,1,2,3,4,5,6,7},{8,9,10,11,12,13,14,15},{16,17,18,19,20,21,22,23},{24..., dimensions={0} | all-to-all | bytes 327680 | tf_op jit(solution)/shard_map/all_to_all | solution.py:323
  405.8 12.1 %all_to_all.68 = f32[16,40,128]{2,1,0:T(8,128)S(1)} all-to-all(f32[16,40,128]{2,1,0:T(8,128)S(1)} %broadcast_in_dim.11), channel_id=1, replica_groups={{0,8,16,24,32,40,48,56,64,72,80,88,96,104,112,120},{1,9,17,25,33,41,49,..., dimensions={0} | all-to-all | bytes 655360 | tf_op jit(solution)/shard_map/all_to_all | solution.py:323
  417.9 4.7 %shard_map.108 = (bf16[64,4096]{1,0:T(8,128)(2,1)}, f32[64,64]{1,0:T(8,128)}) custom-call(f32[40,128]{1,0:T(8,128)S(1)} %reduce_sum.39.sums_ref, bf16[32,64,128]{2,1,0:T(8,128)(2,1)} %get-tuple-element.45.refs_0_.cur_ref), custom_call_target="tpu_custom_call" | custom-call | flops 16777216 | bytes 2097152 | tf_op jit(solution)/shard_map/pallas_call | solution.py:25
  (80 shorter events, 36.4 us)
Async XLA Ops:
  4.6 11.8 %copy-start.36 = (s32[1,96,2]{1,2,0:T(2,128)S(1)}, s32[1,96,2]{1,2,0:T(2,128)}, u32[]{:S(2)}) copy-start(s32[1,96,2]{1,2,0:T(2,128)} %param.12) | copy-start | bytes 2308
  4.6 11.8 %copy-start.9 = (bf16[32,128,128]{2,1,0:T(8,128)(2,1)S(1)}, bf16[32,128,128]{2,1,0:T(8,128)(2,1)}, u32[]{:S(2)}) copy-start(bf16[32,128,128]{2,1,0:T(8,128)(2,1)} %refs_1_.5) | copy-start | bytes 3145732
  4.7 41.6 %all-to-all-start = ((bf16[128,64,128]{2,1,0:T(8,128)(2,1)}), bf16[128,64,128]{2,1,0:T(8,128)(2,1)S(1)}, u32[]{:S(2)}, u32[]{:S(2)}) async-start(bf16[128,64,128]{2,1,0:T(8,128)(2,1)} %get-tuple-element.24), calls=%async_computation | async-start | bytes 4194304 | tf_op jit(solution)/shard_map/all_to_all | solution.py:301
  16.5 2.8 copy-start
  19.3 1.0 copy-start.22
  20.3 25.9 %copy-start.35 = (s32[1,128]{1,0:T(1,128)S(1)}, s32[1,128]{1,0:T(1,128)}, u32[]{:S(2)}) copy-start(s32[1,128]{1,0:T(1,128)} %rows_ref.21) | copy-start | bytes 1540
  24.7 1.0 copy-start.21
  50.9 35.1 %all-to-all-start.1 = ((bf16[128,64,128]{2,1,0:T(8,128)(2,1)}), bf16[128,64,128]{2,1,0:T(8,128)(2,1)S(1)}, u32[]{:S(2)}, u32[]{:S(2)}) async-start(bf16[128,64,128]{2,1,0:T(8,128)(2,1)} %get-tuple-element.26), calls=%async_computation.1 | async-start | bytes 4194304 | tf_op jit(solution)/shard_map/all_to_all | solution.py:301
  55.6 2.8 copy-start.1
  58.4 1.0 copy-start.23
  59.4 1.0 copy-start.30
  64.9 1.0 copy-start.17
  90.7 35.1 %all-to-all-start.2 = ((bf16[128,64,128]{2,1,0:T(8,128)(2,1)}), bf16[128,64,128]{2,1,0:T(8,128)(2,1)S(1)}, u32[]{:S(2)}, u32[]{:S(2)}) async-start(bf16[128,64,128]{2,1,0:T(8,128)(2,1)} %get-tuple-element.28), calls=%async_computation.2 | async-start | bytes 4194304 | tf_op jit(solution)/shard_map/all_to_all | solution.py:301
  95.4 2.8 copy-start.2
  98.2 1.0 copy-start.26
  99.2 1.0 copy-start.31
  104.7 1.0 copy-start.18
  130.6 35.1 %all-to-all-start.3 = ((bf16[128,64,128]{2,1,0:T(8,128)(2,1)}), bf16[128,64,128]{2,1,0:T(8,128)(2,1)S(1)}, u32[]{:S(2)}, u32[]{:S(2)}) async-start(bf16[128,64,128]{2,1,0:T(8,128)(2,1)} %get-tuple-element.30), calls=%async_computation.3 | async-start | bytes 4194304 | tf_op jit(solution)/shard_map/all_to_all | solution.py:301
  135.2 2.8 copy-start.3
  138.0 1.0 copy-start.27
  139.1 1.0 copy-start.33
  144.7 1.0 copy-start.15
  170.4 35.1 %all-to-all-start.4 = ((bf16[128,64,128]{2,1,0:T(8,128)(2,1)}), bf16[128,64,128]{2,1,0:T(8,128)(2,1)S(1)}, u32[]{:S(2)}, u32[]{:S(2)}) async-start(bf16[128,64,128]{2,1,0:T(8,128)(2,1)} %get-tuple-element.32), calls=%async_computation.4 | async-start | bytes 4194304 | tf_op jit(solution)/shard_map/all_to_all | solution.py:301
  175.0 1.0 copy-start.11
  176.5 2.8 copy-start.4
  179.3 1.0 copy-start.12
  184.7 1.0 copy-start.14
  237.6 35.1 %all-to-all-start.7 = ((bf16[128,64,128]{2,1,0:T(8,128)(2,1)}), bf16[128,64,128]{2,1,0:T(8,128)(2,1)S(1)}, u32[]{:S(2)}, u32[]{:S(2)}) async-start(bf16[128,64,128]{2,1,0:T(8,128)(2,1)} %get-tuple-element.36), calls=%async_computation.7 | async-start | bytes 4194304 | tf_op jit(solution)/shard_map/all_to_all | solution.py:301
  242.3 2.8 copy-start.5
  245.0 1.0 copy-start.24
  246.1 1.0 copy-start.32
  252.2 1.0 copy-start.19
  277.4 35.3 %all-to-all-start.8 = ((bf16[128,64,128]{2,1,0:T(8,128)(2,1)}), bf16[128,64,128]{2,1,0:T(8,128)(2,1)S(1)}, u32[]{:S(2)}, u32[]{:S(2)}) async-start(bf16[128,64,128]{2,1,0:T(8,128)(2,1)} %get-tuple-element.40), calls=%async_computation.8 | async-start | bytes 4194304 | tf_op jit(solution)/shard_map/all_to_all | solution.py:301
  282.3 2.8 copy-start.6
  285.1 1.0 copy-start.25
  286.1 1.0 copy-start.28
  292.2 1.0 copy-start.20
  317.4 35.1 %all-to-all-start.9 = ((bf16[128,64,128]{2,1,0:T(8,128)(2,1)}), bf16[128,64,128]{2,1,0:T(8,128)(2,1)S(1)}, u32[]{:S(2)}, u32[]{:S(2)}) async-start(bf16[128,64,128]{2,1,0:T(8,128)(2,1)} %get-tuple-element.42), calls=%async_computation.9 | async-start | bytes 4194304 | tf_op jit(solution)/shard_map/all_to_all | solution.py:301
  322.1 2.8 copy-start.7
  324.9 1.0 copy-start.29
  325.9 1.0 copy-start.34
  332.0 1.0 copy-start.16
  357.2 6.0 %copy-start.10 = (bf16[32,64,128]{2,1,0:T(8,128)(2,1)S(1)}, bf16[32,64,128]{2,1,0:T(8,128)(2,1)}, u32[]{:S(2)}) copy-start(bf16[32,64,128]{2,1,0:T(8,128)(2,1)} %get-tuple-element.45.refs_0_.cur_ref) | copy-start | bytes 1572868
  357.2 35.9 %all-to-all-start.10 = ((bf16[128,64,128]{2,1,0:T(8,128)(2,1)}), bf16[128,64,128]{2,1,0:T(8,128)(2,1)}, u32[]{:S(2)}, u32[]{:S(2)}) async-start(bf16[128,64,128]{2,1,0:T(8,128)(2,1)} %get-tuple-element.44), calls=%async_computation.10 | async-start | bytes 4194304 | tf_op jit(solution)/shard_map/all_to_all | solution.py:301
  363.6 2.8 copy-start.8
  370.8 1.0 copy-start.13

commit v8 on v7

--- a/solution.py
+++ b/solution.py
@@ -365,7 +365,7 @@
     cur, out = filtered(begun, cur, out, centre)
 
     arrived = exchange(out)
-    [value] = sums(cur, arrived, own("image", cur), 0)
+    _, value = sums(cur, arrived, own("image", cur), 1)
     return call(
         functools.partial(end_kernel, total),
         [((k, own_rows), BF16, "a"), (square, F32, "h")],

time: 425 us -> 424 us (level)
  Pallas kernels: 98.9 us -> 87 us
  waiting for transfers between devices: 181 us -> 190 us
    pallas_call x23, Pallas kernels: 98.9 us -> 87 us  [call(): pl.pallas_call(body, out_shape=[(place[kind] if kind in place else jax.Sh...]
    all_to_all x9, waiting for transfers between devices: 181 us -> 190 us  [exchange(): return lax.all_to_all(out, 'dom', 0, 0, tiled=True)]
    unnamed x74 -> x76, local copies, waits for them, and re-layouts: 49.3 us -> 51.6 us
  transfers between devices with their start and end apart: 9 -> 9, of which waited for: 9 -> 9; matrix products, arithmetic and copies ran while one was open for 0% -> 0% of each run, Pallas kernels for 10% -> 7%
where the time goes in v8:
time: 424 us; the launch traced here: 421 us
  waiting for transfers between devices  190 us (45%)
  Pallas kernels  87 us (21%)
  local copies, waits for them, and re-layouts  51.7 us (12%)
  starting transfers between devices  48.7 us (11%)
  blocking collectives  41.9 us (10%)
    all_to_all x9, waiting for transfers between devices, exchange(): return lax.all_to_all(out, 'dom', 0, 0, tiled=True)  190 us
    pallas_call x23, Pallas kernels, call(): pl.pallas_call(body, out_shape=[(place[kind] if kind in place else jax.Sh...  87 us
    unnamed x76, local copies, waits for them, and re-layouts  51.6 us
    all_to_all x9, starting transfers between devices, exchange(): return lax.all_to_all(out, 'dom', 0, 0, tiled=True)  48.7 us
    all_to_all x4, blocking collectives, everywhere(): lax.all_to_all(many, 'dom', 0, 0, axis_index_groups=groups, tiled=True)  41.9 us
  transfers between devices with their start and end apart: 9, of which 9 were waited for; matrix products, arithmetic and copies ran while one was open for 0% of the time, Pallas kernels for 7%

profile of v8, /device:TPU:0, one launch (start us, length us, event | category | flops | bytes accessed | tf_op | source)
XLA Modules:
  0.0 421.3 jit_solution(1015648571815399855)
XLA Ops:
  0.6 4.0 shard_map.86
  4.7 11.2 %all-to-all-start = ((bf16[128,64,128]{2,1,0:T(8,128)(2,1)}), bf16[128,64,128]{2,1,0:T(8,128)(2,1)S(1)}, u32[]{:S(2)}, u32[]{:S(2)}) async-start(bf16[128,64,128]{2,1,0:T(8,128)(2,1)} %get-tuple-element.25), calls=%async_computation | async-start | bytes 4194304 | tf_op jit(solution)/shard_map/all_to_all | solution.py:301
  16.5 2.8 copy-done
  20.3 3.2 shard_map.87.part_ref
  24.5 21.8 %all-to-all-done.arrived_ref = bf16[128,64,128]{2,1,0:T(8,128)(2,1)S(1)} async-done(((bf16[128,64,128]{2,1,0:T(8,128)(2,1)}), bf16[128,64,128]{2,1,0:T(8,128)(2,1)S(1)}, u32[]{:S(2)}, u32[]{:S(2)}) %all-to-all-start) | async-done | bytes 2097184 | tf_op jit(solution)/shard_map/all_to_all | solution.py:301
  46.3 4.7 %shard_map.88 = (bf16[32,64,128]{2,1,0:T(8,128)(2,1)}, bf16[128,64,128]{2,1,0:T(8,128)(2,1)}) custom-call(s32[1,128]{1,0:T(1,128)S(1)} %copy-done.36, bf16[128,64,128]{2,1,0:T(8,128)(2,1)S(1)} %all-to-all-done.arrived_ref, bf16[128,128,128]{2,1,0:T(8,128)(2,1)} %tiles_ref.17, f32[32,64,128]{2,1,0:T(8,128)} %copy-done.22), custom_call_target="tpu_custom_call" | custom-call | flops 268435456 | bytes 10485760 | tf_op jit(solution)/shard_map/pallas_call | solution.py:25
  51.0 4.7 %all-to-all-start.1 = ((bf16[128,64,128]{2,1,0:T(8,128)(2,1)}), bf16[128,64,128]{2,1,0:T(8,128)(2,1)S(1)}, u32[]{:S(2)}, u32[]{:S(2)}) async-start(bf16[128,64,128]{2,1,0:T(8,128)(2,1)} %get-tuple-element.27), calls=%async_computation.1 | async-start | bytes 4194304 | tf_op jit(solution)/shard_map/all_to_all | solution.py:301
  55.7 2.8 copy-done.1
  60.5 3.2 shard_map.89.part_ref
  64.7 21.4 %all-to-all-done.1.arrived_ref = bf16[128,64,128]{2,1,0:T(8,128)(2,1)S(1)} async-done(((bf16[128,64,128]{2,1,0:T(8,128)(2,1)}), bf16[128,64,128]{2,1,0:T(8,128)(2,1)S(1)}, u32[]{:S(2)}, u32[]{:S(2)}) %all-to-all-start.1) | async-done | bytes 2097184 | tf_op jit(solution)/shard_map/all_to_all | solution.py:301
  86.1 4.7 %shard_map.90 = (bf16[32,64,128]{2,1,0:T(8,128)(2,1)}, bf16[128,64,128]{2,1,0:T(8,128)(2,1)}) custom-call(s32[1,128]{1,0:T(1,128)S(1)} %copy-done.36, bf16[128,64,128]{2,1,0:T(8,128)(2,1)S(1)} %all-to-all-done.1.arrived_ref, bf16[128,128,128]{2,1,0:T(8,128)(2,1)} %tiles_ref.17, f32[32,64,128]{2,1,0:T(8,128)} %copy-done.18), custom_call_target="tpu_custom_call" | custom-call | flops 268435456 | bytes 10485760 | tf_op jit(solution)/shard_map/pallas_call | solution.py:25
  90.8 4.7 %all-to-all-start.2 = ((bf16[128,64,128]{2,1,0:T(8,128)(2,1)}), bf16[128,64,128]{2,1,0:T(8,128)(2,1)S(1)}, u32[]{:S(2)}, u32[]{:S(2)}) async-start(bf16[128,64,128]{2,1,0:T(8,128)(2,1)} %get-tuple-element.29), calls=%async_computation.2 | async-start | bytes 4194304 | tf_op jit(solution)/shard_map/all_to_all | solution.py:301
  95.5 2.8 copy-done.2
  100.3 3.2 shard_map.91.part_ref
  104.5 21.4 %all-to-all-done.2.arrived_ref = bf16[128,64,128]{2,1,0:T(8,128)(2,1)S(1)} async-done(((bf16[128,64,128]{2,1,0:T(8,128)(2,1)}), bf16[128,64,128]{2,1,0:T(8,128)(2,1)S(1)}, u32[]{:S(2)}, u32[]{:S(2)}) %all-to-all-start.2) | async-done | bytes 2097184 | tf_op jit(solution)/shard_map/all_to_all | solution.py:301
  125.9 4.7 %shard_map.92 = (bf16[32,64,128]{2,1,0:T(8,128)(2,1)}, bf16[128,64,128]{2,1,0:T(8,128)(2,1)}) custom-call(s32[1,128]{1,0:T(1,128)S(1)} %copy-done.36, bf16[128,64,128]{2,1,0:T(8,128)(2,1)S(1)} %all-to-all-done.2.arrived_ref, bf16[128,128,128]{2,1,0:T(8,128)(2,1)} %tiles_ref.17, f32[32,64,128]{2,1,0:T(8,128)} %copy-done.19), custom_call_target="tpu_custom_call" | custom-call | flops 268435456 | bytes 10485760 | tf_op jit(solution)/shard_map/pallas_call | solution.py:25
  130.6 4.7 %all-to-all-start.3 = ((bf16[128,64,128]{2,1,0:T(8,128)(2,1)}), bf16[128,64,128]{2,1,0:T(8,128)(2,1)S(1)}, u32[]{:S(2)}, u32[]{:S(2)}) async-start(bf16[128,64,128]{2,1,0:T(8,128)(2,1)} %get-tuple-element.31), calls=%async_computation.3 | async-start | bytes 4194304 | tf_op jit(solution)/shard_map/all_to_all | solution.py:301
  140.1 3.4 shard_map.93.part_ref
  144.5 21.2 %all-to-all-done.3.arrived_ref = bf16[128,64,128]{2,1,0:T(8,128)(2,1)S(1)} async-done(((bf16[128,64,128]{2,1,0:T(8,128)(2,1)}), bf16[128,64,128]{2,1,0:T(8,128)(2,1)S(1)}, u32[]{:S(2)}, u32[]{:S(2)}) %all-to-all-start.3) | async-done | bytes 2097184 | tf_op jit(solution)/shard_map/all_to_all | solution.py:301
  165.7 4.7 %shard_map.94 = (bf16[32,64,128]{2,1,0:T(8,128)(2,1)}, bf16[128,64,128]{2,1,0:T(8,128)(2,1)}) custom-call(s32[1,128]{1,0:T(1,128)S(1)} %copy-done.36, bf16[128,64,128]{2,1,0:T(8,128)(2,1)S(1)} %all-to-all-done.3.arrived_ref, bf16[128,128,128]{2,1,0:T(8,128)(2,1)} %tiles_ref.17, f32[32,64,128]{2,1,0:T(8,128)} %copy-done.16), custom_call_target="tpu_custom_call" | custom-call | flops 268435456 | bytes 10485760 | tf_op jit(solution)/shard_map/pallas_call | solution.py:25
  170.4 4.7 %all-to-all-start.4 = ((bf16[128,64,128]{2,1,0:T(8,128)(2,1)}), bf16[128,64,128]{2,1,0:T(8,128)(2,1)S(1)}, u32[]{:S(2)}, u32[]{:S(2)}) async-start(bf16[128,64,128]{2,1,0:T(8,128)(2,1)} %get-tuple-element.33), calls=%async_computation.4 | async-start | bytes 4194304 | tf_op jit(solution)/shard_map/all_to_all | solution.py:301
  176.5 2.8 copy-done.4
  180.4 3.1 shard_map.95.part_ref
  184.5 21.0 %all-to-all-done.4.arrived_ref = bf16[128,64,128]{2,1,0:T(8,128)(2,1)S(1)} async-done(((bf16[128,64,128]{2,1,0:T(8,128)(2,1)}), bf16[128,64,128]{2,1,0:T(8,128)(2,1)S(1)}, u32[]{:S(2)}, u32[]{:S(2)}) %all-to-all-start.4) | async-done | bytes 2097184 | tf_op jit(solution)/shard_map/all_to_all | solution.py:301
  205.5 2.9 shard_map.97
  208.5 8.9 %all_to_all.65 = f32[8,40,128]{2,1,0:T(8,128)S(1)} all-to-all(f32[8,40,128]{2,1,0:T(8,128)S(1)} %broadcast_in_dim.8), channel_id=1, replica_groups={{0,1,2,3,4,5,6,7},{8,9,10,11,12,13,14,15},{16,17,18,19,20,21,22,23},{24..., dimensions={0} | all-to-all | bytes 327680 | tf_op jit(solution)/shard_map/all_to_all | solution.py:323
  217.4 12.1 %all_to_all.66 = f32[16,40,128]{2,1,0:T(8,128)S(1)} all-to-all(f32[16,40,128]{2,1,0:T(8,128)S(1)} %broadcast_in_dim.9), channel_id=1, replica_groups={{0,8,16,24,32,40,48,56,64,72,80,88,96,104,112,120},{1,9,17,25,33,41,49,..., dimensions={0} | all-to-all | bytes 655360 | tf_op jit(solution)/shard_map/all_to_all | solution.py:323
  229.5 8.2 %shard_map.98 = (bf16[32,64,128]{2,1,0:T(8,128)(2,1)}, bf16[32,64,128]{2,1,0:T(8,128)(2,1)}, bf16[128,64,128]{2,1,0:T(8,128)(2,1)}, f32[1,1]{1,0:T(1,128)}) custom-call(s32[1,128]{1,0:T(1,128)S(1)} %copy-done.36, f32[40,128]{1,0:T(8,128)S(1)} %reduce_sum.37.sums_ref, bf16[32,64,128]{2,1,0:T(8,128)(2,1)} %get-tuple-element.34.refs_0_.cur_ref, ...), custom_call_target="tpu_custom_call" | custom-call | flops 16777216 | bytes 4194304 | tf_op jit(solution)/shard_map/pallas_call | solution.py:25
  237.7 4.7 %all-to-all-start.7 = ((bf16[128,64,128]{2,1,0:T(8,128)(2,1)}), bf16[128,64,128]{2,1,0:T(8,128)(2,1)S(1)}, u32[]{:S(2)}, u32[]{:S(2)}) async-start(bf16[128,64,128]{2,1,0:T(8,128)(2,1)} %get-tuple-element.37), calls=%async_computation.7 | async-start | bytes 4194304 | tf_op jit(solution)/shard_map/all_to_all | solution.py:301
  247.2 3.8 shard_map.99.part_ref
  252.0 20.7 %all-to-all-done.7.arrived_ref = bf16[128,64,128]{2,1,0:T(8,128)(2,1)S(1)} async-done(((bf16[128,64,128]{2,1,0:T(8,128)(2,1)}), bf16[128,64,128]{2,1,0:T(8,128)(2,1)S(1)}, u32[]{:S(2)}, u32[]{:S(2)}) %all-to-all-start.7) | async-done | bytes 2097184 | tf_op jit(solution)/shard_map/all_to_all | solution.py:301
  272.8 4.7 %shard_map.100 = (bf16[32,64,128]{2,1,0:T(8,128)(2,1)}, bf16[128,64,128]{2,1,0:T(8,128)(2,1)}) custom-call(s32[1,128]{1,0:T(1,128)S(1)} %copy-done.36, bf16[128,64,128]{2,1,0:T(8,128)(2,1)S(1)} %all-to-all-done.7.arrived_ref, bf16[128,128,128]{2,1,0:T(8,128)(2,1)} %tiles_ref.17, f32[32,64,128]{2,1,0:T(8,128)} %copy-done.20), custom_call_target="tpu_custom_call" | custom-call | flops 268435456 | bytes 10485760 | tf_op jit(solution)/shard_map/pallas_call | solution.py:25
  277.5 4.9 %all-to-all-start.8 = ((bf16[128,64,128]{2,1,0:T(8,128)(2,1)}), bf16[128,64,128]{2,1,0:T(8,128)(2,1)S(1)}, u32[]{:S(2)}, u32[]{:S(2)}) async-start(bf16[128,64,128]{2,1,0:T(8,128)(2,1)} %get-tuple-element.41), calls=%async_computation.8 | async-start | bytes 4194304 | tf_op jit(solution)/shard_map/all_to_all | solution.py:301
  287.3 3.8 shard_map.101.part_ref
  292.1 20.7 %all-to-all-done.8.arrived_ref = bf16[128,64,128]{2,1,0:T(8,128)(2,1)S(1)} async-done(((bf16[128,64,128]{2,1,0:T(8,128)(2,1)}), bf16[128,64,128]{2,1,0:T(8,128)(2,1)S(1)}, u32[]{:S(2)}, u32[]{:S(2)}) %all-to-all-start.8) | async-done | bytes 2097184 | tf_op jit(solution)/shard_map/all_to_all | solution.py:301
  312.8 4.7 %shard_map.102 = (bf16[32,64,128]{2,1,0:T(8,128)(2,1)}, bf16[128,64,128]{2,1,0:T(8,128)(2,1)}) custom-call(s32[1,128]{1,0:T(1,128)S(1)} %copy-done.36, bf16[128,64,128]{2,1,0:T(8,128)(2,1)S(1)} %all-to-all-done.8.arrived_ref, bf16[128,128,128]{2,1,0:T(8,128)(2,1)} %tiles_ref.17, f32[32,64,128]{2,1,0:T(8,128)} %copy-done.21), custom_call_target="tpu_custom_call" | custom-call | flops 268435456 | bytes 10485760 | tf_op jit(solution)/shard_map/pallas_call | solution.py:25
  317.5 4.7 %all-to-all-start.9 = ((bf16[128,64,128]{2,1,0:T(8,128)(2,1)}), bf16[128,64,128]{2,1,0:T(8,128)(2,1)S(1)}, u32[]{:S(2)}, u32[]{:S(2)}) async-start(bf16[128,64,128]{2,1,0:T(8,128)(2,1)} %get-tuple-element.43), calls=%async_computation.9 | async-start | bytes 4194304 | tf_op jit(solution)/shard_map/all_to_all | solution.py:301
  327.1 3.8 shard_map.103.part_ref
  331.9 20.7 %all-to-all-done.9.arrived_ref = bf16[128,64,128]{2,1,0:T(8,128)(2,1)S(1)} async-done(((bf16[128,64,128]{2,1,0:T(8,128)(2,1)}), bf16[128,64,128]{2,1,0:T(8,128)(2,1)S(1)}, u32[]{:S(2)}, u32[]{:S(2)}) %all-to-all-start.9) | async-done | bytes 2097184 | tf_op jit(solution)/shard_map/all_to_all | solution.py:301
  352.6 4.7 %shard_map.104 = (bf16[32,64,128]{2,1,0:T(8,128)(2,1)}, bf16[128,64,128]{2,1,0:T(8,128)(2,1)}) custom-call(s32[1,128]{1,0:T(1,128)S(1)} %copy-done.36, bf16[128,64,128]{2,1,0:T(8,128)(2,1)S(1)} %all-to-all-done.9.arrived_ref, bf16[128,128,128]{2,1,0:T(8,128)(2,1)} %tiles_ref.17, f32[32,64,128]{2,1,0:T(8,128)} %copy-done.17), custom_call_target="tpu_custom_call" | custom-call | flops 268435456 | bytes 10485760 | tf_op jit(solution)/shard_map/pallas_call | solution.py:25
  357.4 4.7 %all-to-all-start.10 = ((bf16[128,64,128]{2,1,0:T(8,128)(2,1)}), bf16[128,64,128]{2,1,0:T(8,128)(2,1)S(1)}, u32[]{:S(2)}, u32[]{:S(2)}) async-start(bf16[128,64,128]{2,1,0:T(8,128)(2,1)} %get-tuple-element.45), calls=%async_computation.10 | async-start | bytes 4194304 | tf_op jit(solution)/shard_map/all_to_all | solution.py:301
  363.5 2.8 copy-done.8
  367.3 3.1 shard_map.105.part_ref
  371.4 21.0 %all-to-all-done.10.arrived_ref = bf16[128,64,128]{2,1,0:T(8,128)(2,1)S(1)} async-done(((bf16[128,64,128]{2,1,0:T(8,128)(2,1)}), bf16[128,64,128]{2,1,0:T(8,128)(2,1)S(1)}, u32[]{:S(2)}, u32[]{:S(2)}) %all-to-all-start.10) | async-done | bytes 2097184 | tf_op jit(solution)/shard_map/all_to_all | solution.py:301
  392.5 2.9 shard_map.107
  395.4 8.9 %all_to_all.67 = f32[8,40,128]{2,1,0:T(8,128)S(1)} all-to-all(f32[8,40,128]{2,1,0:T(8,128)S(1)} %broadcast_in_dim.10), channel_id=1, replica_groups={{0,1,2,3,4,5,6,7},{8,9,10,11,12,13,14,15},{16,17,18,19,20,21,22,23},{24..., dimensions={0} | all-to-all | bytes 327680 | tf_op jit(solution)/shard_map/all_to_all | solution.py:323
  404.3 12.1 %all_to_all.68 = f32[16,40,128]{2,1,0:T(8,128)S(1)} all-to-all(f32[16,40,128]{2,1,0:T(8,128)S(1)} %broadcast_in_dim.11), channel_id=1, replica_groups={{0,8,16,24,32,40,48,56,64,72,80,88,96,104,112,120},{1,9,17,25,33,41,49,..., dimensions={0} | all-to-all | bytes 655360 | tf_op jit(solution)/shard_map/all_to_all | solution.py:323
  416.4 4.7 %shard_map.108 = (bf16[64,4096]{1,0:T(8,128)(2,1)}, f32[64,64]{1,0:T(8,128)}) custom-call(f32[40,128]{1,0:T(8,128)S(1)} %reduce_sum.39.sums_ref, bf16[32,64,128]{2,1,0:T(8,128)(2,1)} %get-tuple-element.46.refs_0_.cur_ref), custom_call_target="tpu_custom_call" | custom-call | flops 16777216 | bytes 2097152 | tf_op jit(solution)/shard_map/pallas_call | solution.py:25
  (82 shorter events, 38.6 us)
Async XLA Ops:
  4.6 11.8 %copy-start.37 = (s32[1,96,2]{1,2,0:T(2,128)S(1)}, s32[1,96,2]{1,2,0:T(2,128)}, u32[]{:S(2)}) copy-start(s32[1,96,2]{1,2,0:T(2,128)} %param.12) | copy-start | bytes 2308
  4.7 11.8 %copy-start.9 = (bf16[32,128,128]{2,1,0:T(8,128)(2,1)S(1)}, bf16[32,128,128]{2,1,0:T(8,128)(2,1)}, u32[]{:S(2)}) copy-start(bf16[32,128,128]{2,1,0:T(8,128)(2,1)} %refs_1_.5) | copy-start | bytes 3145732
  4.7 41.6 %all-to-all-start = ((bf16[128,64,128]{2,1,0:T(8,128)(2,1)}), bf16[128,64,128]{2,1,0:T(8,128)(2,1)S(1)}, u32[]{:S(2)}, u32[]{:S(2)}) async-start(bf16[128,64,128]{2,1,0:T(8,128)(2,1)} %get-tuple-element.25), calls=%async_computation | async-start | bytes 4194304 | tf_op jit(solution)/shard_map/all_to_all | solution.py:301
  16.5 2.8 copy-start
  19.3 1.0 copy-start.23
  20.3 25.9 %copy-start.36 = (s32[1,128]{1,0:T(1,128)S(1)}, s32[1,128]{1,0:T(1,128)}, u32[]{:S(2)}) copy-start(s32[1,128]{1,0:T(1,128)} %rows_ref.21) | copy-start | bytes 1540
  23.5 1.0 copy-start.22
  51.0 35.1 %all-to-all-start.1 = ((bf16[128,64,128]{2,1,0:T(8,128)(2,1)}), bf16[128,64,128]{2,1,0:T(8,128)(2,1)S(1)}, u32[]{:S(2)}, u32[]{:S(2)}) async-start(bf16[128,64,128]{2,1,0:T(8,128)(2,1)} %get-tuple-element.27), calls=%async_computation.1 | async-start | bytes 4194304 | tf_op jit(solution)/shard_map/all_to_all | solution.py:301
  55.6 2.8 copy-start.1
  58.4 1.0 copy-start.24
  59.5 1.0 copy-start.31
  63.7 1.0 copy-start.18
  90.8 35.1 %all-to-all-start.2 = ((bf16[128,64,128]{2,1,0:T(8,128)(2,1)}), bf16[128,64,128]{2,1,0:T(8,128)(2,1)S(1)}, u32[]{:S(2)}, u32[]{:S(2)}) async-start(bf16[128,64,128]{2,1,0:T(8,128)(2,1)} %get-tuple-element.29), calls=%async_computation.2 | async-start | bytes 4194304 | tf_op jit(solution)/shard_map/all_to_all | solution.py:301
  95.5 2.8 copy-start.2
  98.2 1.0 copy-start.27
  99.3 1.0 copy-start.32
  103.5 1.0 copy-start.19
  130.6 35.1 %all-to-all-start.3 = ((bf16[128,64,128]{2,1,0:T(8,128)(2,1)}), bf16[128,64,128]{2,1,0:T(8,128)(2,1)S(1)}, u32[]{:S(2)}, u32[]{:S(2)}) async-start(bf16[128,64,128]{2,1,0:T(8,128)(2,1)} %get-tuple-element.31), calls=%async_computation.3 | async-start | bytes 4194304 | tf_op jit(solution)/shard_map/all_to_all | solution.py:301
  135.3 2.8 copy-start.3
  138.1 1.0 copy-start.28
  139.1 1.0 copy-start.34
  143.5 1.0 copy-start.16
  170.4 35.1 %all-to-all-start.4 = ((bf16[128,64,128]{2,1,0:T(8,128)(2,1)}), bf16[128,64,128]{2,1,0:T(8,128)(2,1)S(1)}, u32[]{:S(2)}, u32[]{:S(2)}) async-start(bf16[128,64,128]{2,1,0:T(8,128)(2,1)} %get-tuple-element.33), calls=%async_computation.4 | async-start | bytes 4194304 | tf_op jit(solution)/shard_map/all_to_all | solution.py:301
  175.1 1.0 copy-start.12
  176.5 2.8 copy-start.4
  179.3 1.0 copy-start.13
  183.5 1.0 copy-start.15
  237.7 35.1 %all-to-all-start.7 = ((bf16[128,64,128]{2,1,0:T(8,128)(2,1)}), bf16[128,64,128]{2,1,0:T(8,128)(2,1)S(1)}, u32[]{:S(2)}, u32[]{:S(2)}) async-start(bf16[128,64,128]{2,1,0:T(8,128)(2,1)} %get-tuple-element.37), calls=%async_computation.7 | async-start | bytes 4194304 | tf_op jit(solution)/shard_map/all_to_all | solution.py:301
  242.3 2.8 copy-start.5
  245.1 1.0 copy-start.25
  246.2 1.0 copy-start.33
  251.0 1.0 copy-start.20
  277.5 35.3 %all-to-all-start.8 = ((bf16[128,64,128]{2,1,0:T(8,128)(2,1)}), bf16[128,64,128]{2,1,0:T(8,128)(2,1)S(1)}, u32[]{:S(2)}, u32[]{:S(2)}) async-start(bf16[128,64,128]{2,1,0:T(8,128)(2,1)} %get-tuple-element.41), calls=%async_computation.8 | async-start | bytes 4194304 | tf_op jit(solution)/shard_map/all_to_all | solution.py:301
  282.4 2.8 copy-start.6
  285.2 1.0 copy-start.26
  286.2 1.0 copy-start.29
  291.1 1.0 copy-start.21
  317.5 35.1 %all-to-all-start.9 = ((bf16[128,64,128]{2,1,0:T(8,128)(2,1)}), bf16[128,64,128]{2,1,0:T(8,128)(2,1)S(1)}, u32[]{:S(2)}, u32[]{:S(2)}) async-start(bf16[128,64,128]{2,1,0:T(8,128)(2,1)} %get-tuple-element.43), calls=%async_computation.9 | async-start | bytes 4194304 | tf_op jit(solution)/shard_map/all_to_all | solution.py:301
  322.2 2.8 copy-start.7
  325.0 1.0 copy-start.30
  326.0 1.0 copy-start.35
  330.9 1.0 copy-start.17
  357.4 35.1 %all-to-all-start.10 = ((bf16[128,64,128]{2,1,0:T(8,128)(2,1)}), bf16[128,64,128]{2,1,0:T(8,128)(2,1)S(1)}, u32[]{:S(2)}, u32[]{:S(2)}) async-start(bf16[128,64,128]{2,1,0:T(8,128)(2,1)} %get-tuple-element.45), calls=%async_computation.10 | async-start | bytes 4194304 | tf_op jit(solution)/shard_map/all_to_all | solution.py:301
  362.0 1.0 copy-start.10
  363.5 2.8 copy-start.8
  366.3 1.0 copy-start.11
  370.5 1.0 copy-start.14
